TPU v7x, 32 devices: a whole 2x2x4 slice. The times are simulated.
32 devices in a mesh: nar: 4 (over x, core), wide: 8 (over z, y).
Axes of the slice: x: 2, y: 2, z: 4, core: 2. Of those that a mesh axis runs over, the one named last changes fastest.
Arguments:
- tokens: bfloat16 [32768, 768], P(('nar', 'wide')), may hold values from -6 to 6
- cotangent: bfloat16 [32768, 768], P(('nar', 'wide')), may hold values from -6 to 6
- image_ids: int32 [32, 1024], P(('nar', 'wide')), may hold values from -1 to 3, as said below
- w_in: bfloat16 [5376, 768], P('wide'), may hold values from -0.21875 to 0.21875
- w_out: bfloat16 [3840, 768], P('wide'), may hold values from -0.8164966 to 0.8164966
- gains: float32 [896], replicated, may hold values from 0.25 to 1.75
- mom_in: float32 [5376, 768], P('wide'), may hold values from -832 to 832
- mom_out: float32 [3840, 768], P('wide'), may hold values from -832 to 832
- gain_m: float32 [896], replicated, may hold values from -112 to 112
- gain_v: float32 [896], replicated, may hold values from 1092 to 6553
Outputs:
- result: bfloat16 [32768, 768], P(('nar', 'wide'))
- grad_tokens: bfloat16 [32768, 768], P(('nar', 'wide'))
- grad_w_in: float32 [5376, 768], P('wide')
- grad_w_out: float32 [3840, 768], P('wide')
- grad_gains: float32 [896], replicated
- mom_in_new: float32 [5376, 768], P('wide')
- mom_out_new: float32 [3840, 768], P('wide')
- gain_m_new: float32 [896], replicated
- gain_v_new: float32 [896], replicated
- w_in_new: float32 [5376, 768], P('wide')
- w_out_new: float32 [3840, 768], P('wide')
- gains_new: float32 [896], replicated
Inputs may be any that keep to these rules, and one draw needn't show every extreme that they name: `image_ids`: each row is one packed sequence: images numbered 0 to 3 in increasing order, each a contiguous run of tokens (earlier ones may be empty, the last is not), followed by padding marked -1.
All inputs are finite; a program needn't handle non-finite values.
Results may differ from a plain program's by a relative error of at most 0.015.
Values may be sent and summed in bfloat16 or wider, within the bound.
No kernel may reach another device: no remote copies, remote signals or barrier semaphores. Data moves between devices by JAX's collectives and lax.ppermute only.
A program may use at most 320 MiB of HBM per device.

v0:
```python
from functools import partial

import jax
import jax.numpy as jnp
from jax import lax
from jax.sharding import PartitionSpec as P

D = 768
HEADS = 12
HEAD = 64
LEN = 1024
SWEEPS = 5
STEP = 10
FIN = 5376
FOUT = 3840


highest = lax.Precision.HIGHEST
ns_linear = 3.4445
ns_cubic = -4.775
ns_quintic = 2.0315
muon_beta = 0.5
muon_rate = 0.8
muon_decay = 0.1
adam_rate = 0.8
adam_first = 0.9
adam_second = 0.95
adam_eps = 1e-08
norm_eps = 1e-06
masked_score = -1e30
head_group = 4


def shortened(shard):
    return jax.tree.map(lambda a: a.astype(jnp.bfloat16) if a.dtype == jnp.float32 else a, shard)


def normalize(values):
    center = values - jnp.mean(values, axis=-1, keepdims=True)
    variance = jnp.mean(center * center, axis=-1, keepdims=True)
    inverse = lax.rsqrt(variance + norm_eps)
    return (center * inverse, inverse)


def norm_backward(grad_scaled, normed, inverse):
    mean_grad = jnp.mean(grad_scaled, axis=-1, keepdims=True)
    mean_cross = jnp.mean(grad_scaled * normed, axis=-1, keepdims=True)
    return inverse * (grad_scaled - mean_grad - normed * mean_cross)


def masked_scores(query_block, key_group, ids_block, ids_seq):
    scores = HEAD ** (-0.5) * jnp.einsum(
        "qhd,khd->hqk", query_block, key_group, preferred_element_type=jnp.float32
    )
    allowed = ids_block[:, None] == ids_seq[None, :]
    return jnp.where(allowed[None], scores, masked_score)


def attend_forward(inputs):
    query_seq, key_seq, value_seq, ids_seq = inputs
    length = query_seq.shape[0]
    block_rows = min(512, length)
    row_parts = []
    total_parts = []
    for row_start in range(0, length, block_rows):
        ids_block = ids_seq[row_start : row_start + block_rows]
        head_parts = []
        head_totals = []
        for head_start in range(0, HEADS, head_group):
            query_block = query_seq[
                row_start : row_start + block_rows, head_start : head_start + head_group
            ]
            key_group = key_seq[:, head_start : head_start + head_group]
            value_group = value_seq[:, head_start : head_start + head_group]
            scores = masked_scores(query_block, key_group, ids_block, ids_seq)
            row_max = jnp.max(scores, axis=-1, keepdims=True)
            exp_terms = jnp.exp(scores - row_max)
            exp_sum = jnp.sum(exp_terms, axis=-1, keepdims=True)
            softmax_w = (exp_terms / exp_sum).astype(jnp.bfloat16)
            head_parts.append(
                jnp.einsum(
                    "hqk,khd->qhd", softmax_w, value_group, preferred_element_type=jnp.float32
                )
            )
            head_totals.append(row_max + jnp.log(exp_sum))
        row_parts.append(jnp.concatenate(head_parts, axis=1))
        total_parts.append(jnp.concatenate(head_totals, axis=0))
    return (jnp.concatenate(row_parts, axis=0), jnp.concatenate(total_parts, axis=1))


def attend_backward(inputs):
    query_seq, key_seq, value_seq, ids_seq, dout_seq, log_total = inputs
    length = query_seq.shape[0]
    block_rows = min(512, length)
    scaling = HEAD ** (-0.5)
    group_total = HEADS // head_group
    dkey_sums = [
        jnp.zeros((length, head_group, HEAD), jnp.float32) for group_index in range(group_total)
    ]
    dvalue_sums = [
        jnp.zeros((length, head_group, HEAD), jnp.float32) for group_index in range(group_total)
    ]
    dquery_rows = []
    for row_start in range(0, length, block_rows):
        ids_block = ids_seq[row_start : row_start + block_rows]
        dquery_heads = []
        for group_index in range(group_total):
            head_start = group_index * head_group
            query_block = query_seq[
                row_start : row_start + block_rows, head_start : head_start + head_group
            ]
            dout_block = dout_seq[
                row_start : row_start + block_rows, head_start : head_start + head_group
            ]
            key_group = key_seq[:, head_start : head_start + head_group]
            value_group = value_seq[:, head_start : head_start + head_group]
            scores = masked_scores(query_block, key_group, ids_block, ids_seq)
            block_total = log_total[
                head_start : head_start + head_group, row_start : row_start + block_rows
            ]
            softmax_w = jnp.exp(scores - block_total)
            dsoftmax = jnp.einsum(
                "qhd,khd->hqk", dout_block, value_group, preferred_element_type=jnp.float32
            )
            inner_sum = jnp.sum(softmax_w * dsoftmax, axis=-1, keepdims=True)
            dscores = (softmax_w * (dsoftmax - inner_sum)).astype(jnp.bfloat16)
            dquery_heads.append(
                scaling
                * jnp.einsum("hqk,khd->qhd", dscores, key_group, preferred_element_type=jnp.float32)
            )
            dkey_sums[group_index] = dkey_sums[group_index] + scaling * jnp.einsum(
                "hqk,qhd->khd", dscores, query_block, preferred_element_type=jnp.float32
            )
            dvalue_sums[group_index] = dvalue_sums[group_index] + jnp.einsum(
                "hqk,qhd->khd",
                softmax_w.astype(jnp.bfloat16),
                dout_block,
                preferred_element_type=jnp.float32,
            )
        dquery_rows.append(jnp.concatenate(dquery_heads, axis=1))
    return (
        jnp.concatenate(dquery_rows, axis=0),
        jnp.concatenate(dkey_sums, axis=1),
        jnp.concatenate(dvalue_sums, axis=1),
    )


def gram_matrix(matrix):
    return lax.dot_general(
        matrix,
        matrix,
        (((0,), (0,)), ((), ())),
        precision=highest,
        preferred_element_type=jnp.float32,
    )


def quintic_step(matrix, gram):
    square = jnp.dot(gram, gram, precision=highest, preferred_element_type=jnp.float32)
    mixing = ns_cubic * gram + ns_quintic * square
    return ns_linear * matrix + jnp.dot(
        matrix, mixing, precision=highest, preferred_element_type=jnp.float32
    )


def on_device(tokens, cotangent, image_ids, w_in, w_out, gains, mom_in, mom_out, gain_m, gain_v):
    x_float = tokens.astype(jnp.float32)
    row_count = tokens.shape[0]
    seq_count = image_ids.shape[0]
    shape_seq = (seq_count, LEN, HEADS, HEAD)
    shape_rows = (row_count, HEADS, HEAD)
    ln_gain = gains[:D]
    q_gain = gains[D : D + HEAD]
    k_gain = gains[D + HEAD :]
    x_hat, x_inverse = normalize(x_float)
    x_low = (x_hat * ln_gain).astype(jnp.bfloat16)
    joined_rows = lax.dot_general(
        x_low,
        lax.all_gather(w_in, "wide", axis=0, tiled=True),
        (((1,), (1,)), ((), ())),
        preferred_element_type=jnp.float32,
    ).astype(jnp.bfloat16)
    q_hat, q_inverse = normalize(joined_rows[:, :D].astype(jnp.float32).reshape(shape_rows))
    k_hat, k_inverse = normalize(joined_rows[:, D : 2 * D].astype(jnp.float32).reshape(shape_rows))
    query_low = (q_hat * q_gain).astype(jnp.bfloat16)
    key_low = (k_hat * k_gain).astype(jnp.bfloat16)
    value_low = joined_rows[:, 2 * D : 3 * D].reshape(shape_rows)
    upward = joined_rows[:, 3 * D :].astype(jnp.float32)
    attended, log_total = lax.map(
        attend_forward,
        (
            query_low.reshape(shape_seq),
            key_low.reshape(shape_seq),
            value_low.reshape(shape_seq),
            image_ids,
        ),
    )
    attended_low = attended.reshape(row_count, D).astype(jnp.bfloat16)
    active, gelu_pull = jax.vjp(partial(jax.nn.gelu, approximate=False), upward)
    hidden = jnp.concatenate([attended_low, active.astype(jnp.bfloat16)], axis=1)
    rows_piece = lax.all_gather(w_out, "wide", axis=0, tiled=True)
    columns = lax.slice_in_dim(hidden, 0, rows_piece.shape[0], axis=1)
    branch = jnp.zeros((row_count, D), jnp.float32) + jnp.dot(
        columns, rows_piece, preferred_element_type=jnp.float32
    )
    result = (x_float + branch).astype(jnp.bfloat16)
    live = (image_ids.reshape(row_count) >= 0)[:, None]
    grad_y = jnp.where(live, cotangent, jnp.zeros_like(cotangent))
    grad_hidden = lax.dot_general(
        grad_y,
        lax.all_gather(w_out, "wide", axis=0, tiled=True),
        (((1,), (1,)), ((), ())),
        preferred_element_type=jnp.float32,
    )
    dattended = grad_hidden[:, :D].astype(jnp.bfloat16).reshape(shape_seq)
    dupward = gelu_pull(grad_hidden[:, D:])[0]
    dquery_n, dkey_n, dvalues = lax.map(
        attend_backward,
        (
            query_low.reshape(shape_seq),
            key_low.reshape(shape_seq),
            value_low.reshape(shape_seq),
            image_ids,
            dattended,
            log_total,
        ),
    )
    dquery_n = dquery_n.reshape(shape_rows)
    dkey_n = dkey_n.reshape(shape_rows)
    q_gain_grad = jnp.sum(dquery_n * q_hat, axis=(0, 1))
    k_gain_grad = jnp.sum(dkey_n * k_hat, axis=(0, 1))
    dqueries = norm_backward(dquery_n * q_gain, q_hat, q_inverse)
    dkeys = norm_backward(dkey_n * k_gain, k_hat, k_inverse)
    grad_joined = jnp.concatenate(
        [
            dqueries.reshape(row_count, D).astype(jnp.bfloat16),
            dkeys.reshape(row_count, D).astype(jnp.bfloat16),
            dvalues.reshape(row_count, D).astype(jnp.bfloat16),
            dupward.astype(jnp.bfloat16),
        ],
        axis=1,
    )
    rows_piece = lax.all_gather(w_in, "wide", axis=0, tiled=True)
    grad_slice = lax.slice_in_dim(grad_joined, 0, rows_piece.shape[0], axis=1)
    grad_normed = jnp.zeros((row_count, D), jnp.float32) + jnp.dot(
        grad_slice, rows_piece, preferred_element_type=jnp.float32
    )
    ln_grad = jnp.sum(grad_normed * x_hat, axis=0)
    grad_tokens = (
        grad_y.astype(jnp.float32) + norm_backward(grad_normed * ln_gain, x_hat, x_inverse)
    ).astype(jnp.bfloat16)
    rows_in = w_in.shape[0]
    rows_out = w_out.shape[0]
    hidden_slice = lax.slice_in_dim(hidden, 0, rows_out * lax.axis_size("wide"), axis=1)
    grad_out_part = lax.psum_scatter(
        lax.dot_general(
            hidden_slice, grad_y, (((0,), (0,)), ((), ())), preferred_element_type=jnp.float32
        ).astype(jnp.bfloat16),
        "wide",
        scatter_dimension=0,
        tiled=True,
    )
    grad_slice = lax.slice_in_dim(grad_joined, 0, rows_in * lax.axis_size("wide"), axis=1)
    grad_in_part = lax.psum_scatter(
        lax.dot_general(
            grad_slice, x_low, (((0,), (0,)), ((), ())), preferred_element_type=jnp.float32
        ).astype(jnp.bfloat16),
        "wide",
        scatter_dimension=0,
        tiled=True,
    )
    grad_w_in, grad_w_out = (
        lax.psum(grad_in_part, "nar").astype(jnp.float32),
        lax.psum(grad_out_part, "nar").astype(jnp.float32),
    )
    mom_in_new = muon_beta * mom_in + grad_w_in
    mom_out_new = muon_beta * mom_out + grad_w_out
    gain_terms = jnp.concatenate([ln_grad, q_gain_grad, k_gain_grad])
    nar_count = lax.axis_size("nar")
    nar_place = lax.axis_index("nar")
    share_in = rows_in // nar_count
    share_out = rows_out // nar_count
    block_in = lax.dynamic_slice_in_dim(mom_in_new, nar_place * share_in, share_in, 0)
    block_out = lax.dynamic_slice_in_dim(mom_out_new, nar_place * share_out, share_out, 0)
    square_in, square_out, grad_gains = lax.psum(
        (jnp.sum(block_in * block_in), jnp.sum(block_out * block_out), gain_terms), ("nar", "wide")
    )
    ortho_in = block_in / (jnp.sqrt(square_in) + 1e-07)
    ortho_out = block_out / (jnp.sqrt(square_out) + 1e-07)
    for ns_sweep in range(SWEEPS):
        gram_in, gram_out = lax.psum(
            (gram_matrix(ortho_in), gram_matrix(ortho_out)), ("nar", "wide")
        )
        ortho_in = quintic_step(ortho_in, gram_in)
        ortho_out = quintic_step(ortho_out, gram_out)
    ortho_in, ortho_out = (
        lax.all_gather(shortened(ortho_in), "nar", axis=0, tiled=True).astype(ortho_in.dtype),
        lax.all_gather(shortened(ortho_out), "nar", axis=0, tiled=True).astype(ortho_out.dtype),
    )
    w_in_new = (
        w_in.astype(jnp.float32) * (1 - muon_rate * muon_decay)
        - muon_rate * (FIN / D) ** 0.5 * ortho_in
    )
    w_out_new = (
        w_out.astype(jnp.float32) * (1 - muon_rate * muon_decay)
        - muon_rate * (FOUT / D) ** 0.5 * ortho_out
    )
    gain_m_new = adam_first * gain_m + (1 - adam_first) * grad_gains
    gain_v_new = adam_second * gain_v + (1 - adam_second) * grad_gains * grad_gains
    gains_new = gains - adam_rate * (gain_m_new / (1 - adam_first**STEP)) / (
        jnp.sqrt(gain_v_new / (1 - adam_second**STEP)) + adam_eps
    )
    return (
        result,
        grad_tokens,
        grad_w_in,
        grad_w_out,
        grad_gains,
        mom_in_new,
        mom_out_new,
        gain_m_new,
        gain_v_new,
        w_in_new,
        w_out_new,
        gains_new,
    )


def solution(mesh):
    return jax.shard_map(
        on_device,
        mesh=mesh,
        in_specs=(
            P(("nar", "wide"), None),
            P(("nar", "wide"), None),
            P(("nar", "wide"), None),
            P("wide", None),
            P("wide", None),
            P(),
            P("wide", None),
            P("wide", None),
            P(),
            P(),
        ),
        out_specs=(
            P(("nar", "wide"), None),
            P(("nar", "wide"), None),
            P("wide", None),
            P("wide", None),
            P(),
            P("wide", None),
            P("wide", None),
            P(),
            P(),
            P("wide", None),
            P("wide", None),
            P(),
        ),
        check_vma=False,
    )
```

profile of v0, /device:TPU:0, one launch (start us, length us, event | category | flops | bytes accessed | tf_op | source)
XLA Modules:
  0.0 1688.5 jit_solution(5112789608846598570)
XLA Ops:
  14.9 92.3 %all-gather.5.cloned.1.call-done = bf16[3840,768]{1,0:T(8,128)(2,1)} async-done(((bf16[480,768]{1,0:T(8,128)(2,1)}), bf16[3840,768]{1,0:T(8,128)(2,1)}) %all-gather.5.cloned.1.call-update) | async-done | bytes 5898256 | tf_op jit(solution)/shard_map/all_gather | solution.py:201
  107.2 9.0 fusion.314
  116.2 5.5 copy-done.31
  123.8 107.0 %all-gather.3.cloned.1.call-done = bf16[5376,768]{1,0:T(8,128)(2,1)} async-done(((bf16[672,768]{1,0:T(8,128)(2,1)}), bf16[5376,768]{1,0:T(8,128)(2,1)}) %all-gather.3.cloned.1.call-update) | async-done | bytes 8257552 | tf_op jit(solution)/shard_map/all_gather | solution.py:179
  230.8 14.8 convolution_convert_fusion
  245.6 32.3 %fusion.8 = (bf16[1024,3072]{1,0:T(8,128)(2,1)}, f32[1024,3072]{1,0:T(8,128)}) fusion(f32[1024,3840]{1,0:T(8,128)} %copy-done.31, bf16[1024,5376]{1,0:T(8,128)(2,1)} %convolution_convert_fusion), kind=kLoop, calls=%fused_computation.11 | loop fusion | flops 229638144 | bytes 37748736 | tf_op jit(solution)/shard_map/convert_element_type | solution.py:239
  277.9 5.8 slice_convert_fusion.2
  295.1 5.0 fusion.321
  300.1 4.9 fusion.322
  305.1 5.0 fusion.323
  310.0 4.9 fusion.324
  314.9 5.0 fusion.325
  319.9 5.2 fusion.326
  325.8 4.9 fusion.42
  330.7 5.9 fusion.236
  381.9 11.3 fusion.2
  396.3 7.2 multiply_reduce_fusion.3
  403.6 5.0 fusion.166
  408.6 5.0 fusion.163
  417.1 6.9 multiply_convert_fusion
  427.6 5.1 multiply_convert_fusion.1
  443.1 11.5 convolution_convert_fusion.2
  454.6 7.5 multiply_convert_fusion.3
  465.6 6.2 multiply_reduce_fusion.4
  533.0 13.9 multiply_reduce_fusion.7
  546.9 17.2 %convolution_convert_fusion.1 = bf16[5376,768]{1,0:T(8,128)(2,1)} fusion(bf16[1024,3072]{1,0:T(8,128)(2,1)} %get-tuple-element.94, bf16[1024,768]{1,0:T(8,128)(2,1)} %copy.88, bf16[1024,768]{1,0:T(8,128)(2,1)S(1)} %get-tuple-element.96, bf16[1024,768]{1,0:T(8,128)(2,1)} %get-tuple-element.97, bf16[1024,768]{1,0:T(8,128)(2,1)S(1)} %copy-done.30, ...), kind=kOutput, calls=%fused_computation.42 | convolution fusion | flops 8507817984 | bytes 20851712 | tf_op jit(solution)/shard_map/dot_general | solution.py:265
  564.7 150.2 %reduce-scatter.3.cloned.1.call-done = bf16[672,768]{1,0:T(8,128)(2,1)} async-done(((bf16[5376,768]{1,0:T(8,128)(2,1)}), bf16[672,768]{1,0:T(8,128)(2,1)}) %reduce-scatter.3.cloned.1.call-update) | async-done | bytes 1032208 | tf_op jit(solution)/shard_map/reduce_scatter | solution.py:264
  715.0 15.2 fusion.86
  730.5 32.0 %all-reduce.24.cloned.1.call-done = (bf16[672,768]{1,0:T(8,128)(2,1)}, bf16[480,768]{1,0:T(8,128)(2,1)}) async-done(((bf16[672,768]{1,0:T(8,128)(2,1)}, bf16[480,768]{1,0:T(8,128)(2,1)}), (bf16[672,768]{1,0:T(8,128)(2,1)}, bf16[480,768]{1,0:T(8,128)(2,1)})) %all-reduce.24.cloned.1.call-update) | async-done | bytes 1769488 | tf_op jit(solution)/shard_map/psum | solution.py:273
  769.3 39.6 %all-reduce = (f32[896]{0:T(1024)S(1)}, f32[]{:T(128)}, f32[]{:T(128)}) all-reduce(f32[896]{0:T(1024)S(1)} %pad_maximum_fusion.13, f32[]{:T(128)} %multiply_reduce_fusion.14, f32[]{:T(128)} %multiply_reduce_fusion.15), channel_id=1, replica_groups=mesh['nar'=4,'wide'=8] {'nar','wide'}, use_global_device_ids=true, to_apply=%region_39.40 | all-reduce | flops 898 | bytes 7184 | tf_op jit(solution)/shard_map/psum | solution.py:285
  819.0 145.4 %all-reduce.22.cloned.1.call-done = (f32[768,768]{1,0:T(8,128)}, f32[768,768]{1,0:T(8,128)}) async-done(((f32[768,768]{1,0:T(8,128)}, f32[768,768]{1,0:T(8,128)}), (f32[768,768]{1,0:T(8,128)}, f32[768,768]{1,0:T(8,128)})) %all-reduce.22.cloned.1.call-update) | async-done | bytes 4718608 | tf_op jit(solution)/shard_map/psum | solution.py:291
  964.5 8.5 fusion.327
  978.5 6.1 fusion.336
  990.0 143.7 %all-reduce.20.cloned.1.call-done = (f32[768,768]{1,0:T(8,128)}, f32[768,768]{1,0:T(8,128)}) async-done(((f32[768,768]{1,0:T(8,128)}, f32[768,768]{1,0:T(8,128)}), (f32[768,768]{1,0:T(8,128)}, f32[768,768]{1,0:T(8,128)})) %all-reduce.20.cloned.1.call-update) | async-done | bytes 4718608 | tf_op jit(solution)/shard_map/psum | solution.py:291
  1133.7 8.5 fusion.329
  1147.7 6.4 fusion.338
  1159.4 143.8 %all-reduce.18.cloned.1.call-done = (f32[768,768]{1,0:T(8,128)}, f32[768,768]{1,0:T(8,128)}) async-done(((f32[768,768]{1,0:T(8,128)}, f32[768,768]{1,0:T(8,128)}), (f32[768,768]{1,0:T(8,128)}, f32[768,768]{1,0:T(8,128)})) %all-reduce.18.cloned.1.call-update) | async-done | bytes 4718608 | tf_op jit(solution)/shard_map/psum | solution.py:291
  1303.2 8.5 fusion.331
  1317.2 6.2 fusion.340
  1328.7 143.7 %all-reduce.16.cloned.1.call-done = (f32[768,768]{1,0:T(8,128)}, f32[768,768]{1,0:T(8,128)}) async-done(((f32[768,768]{1,0:T(8,128)}, f32[768,768]{1,0:T(8,128)}), (f32[768,768]{1,0:T(8,128)}, f32[768,768]{1,0:T(8,128)})) %all-reduce.16.cloned.1.call-update) | async-done | bytes 4718608 | tf_op jit(solution)/shard_map/psum | solution.py:291
  1472.4 8.5 fusion.333
  1486.3 6.4 fusion.342
  1502.1 11.2 fusion.88
  1513.9 128.0 %all-reduce.14.cloned.1.call-done = (f32[768,768]{1,0:T(8,128)}, f32[768,768]{1,0:T(8,128)}) async-done(((f32[768,768]{1,0:T(8,128)}, f32[768,768]{1,0:T(8,128)}), (f32[768,768]{1,0:T(8,128)}, f32[768,768]{1,0:T(8,128)})) %all-reduce.14.cloned.1.call-update) | async-done | bytes 4718608 | tf_op jit(solution)/shard_map/psum | solution.py:291
  1641.9 8.5 fusion.335
  1652.3 10.0 all_gather.16
  1664.0 6.0 fusion.344
  1671.7 8.5 all_gather.17
  (387 shorter events, 222.0 us)
Async XLA Ops:
  7.2 100.0 %copy-start.60 = (bf16[1024,768]{1,0:T(8,128)(2,1)S(1)}, bf16[1024,768]{1,0:T(8,128)(2,1)}, u32[]{:S(2)}) copy-start(bf16[1024,768]{1,0:T(8,128)(2,1)} %param.11) | copy-start | bytes 4718596
  7.2 100.0 %all-gather.5.cloned.1.call-start = ((), (), s32[]{:S(2)}) async-start(), calls=%async_computation.3 | async-start | bytes 6635520 | tf_op jit(solution)/shard_map/all_gather | solution.py:201
  7.9 222.9 %all-gather.3.cloned.1.call-start = ((), (), s32[]{:S(2)}) async-start(), calls=%async_computation.2 | async-start | bytes 9289728 | tf_op jit(solution)/shard_map/all_gather | solution.py:179
  8.7 556.0 %reduce-scatter.5.cloned.1.call-start = ((), (), s32[]{:S(2)}) async-start(), calls=%async_computation.5 | async-start | bytes 6635520 | tf_op jit(solution)/shard_map/reduce_scatter | solution.py:255
  9.6 282.1 %copy-start.78 = (f32[64]{0:T(128)}, f32[64]{0:T(128)S(1)}, u32[]{:S(2)}) copy-start(f32[64]{0:T(128)S(1)} %get-tuple-element.107) | copy-start | bytes 772
  9.6 282.1 %copy-start.80 = (f32[64]{0:T(128)}, f32[64]{0:T(128)S(1)}, u32[]{:S(2)}) copy-start(f32[64]{0:T(128)S(1)} %get-tuple-element.106) | copy-start | bytes 772
  12.6 103.6 %copy-start.85 = (pred[1024]{0:T(1024)(128)(4,1)}, pred[1024]{0:T(1024)(128)(4,1)S(1)}, u32[]{:S(2)}) copy-start(pred[1024]{0:T(1024)(128)(4,1)S(1)} %broadcast_compare_fusion.2) | copy-start | bytes 3076
  12.7 218.2 %copy-start.69 = (f32[1024]{0:T(1024)}, f32[1024]{0:T(1024)S(1)}, u32[]{:S(2)}) copy-start(f32[1024]{0:T(1024)S(1)} %broadcast_multiply_fusion.8) | copy-start | bytes 12292
  13.3 217.5 %copy-start.76 = (f32[1024]{0:T(1024)}, f32[1024]{0:T(1024)S(1)}, u32[]{:S(2)}) copy-start(f32[1024]{0:T(1024)S(1)} %add_rsqrt_fusion.2) | copy-start | bytes 12292
  121.7 109.1 %copy-start.72 = (f32[896]{0:T(1024)S(1)}, f32[896]{0:T(1024)}, u32[]{:S(2)}) copy-start(f32[896]{0:T(1024)} %param.15) | copy-start | bytes 10756
  295.1 24.8 %copy-start.32 = (bf16[1024,12,64]{0,2,1:T(8,128)(2,1)}, bf16[1024,12,64]{0,2,1:T(8,128)(2,1)S(1)}, u32[]{:S(2)}) copy-start(bf16[1024,12,64]{0,2,1:T(8,128)(2,1)S(1)} %get-tuple-element.134) | copy-start | bytes 4718596
  295.1 24.8 %copy-start.54 = (bf16[1024,12,64]{0,2,1:T(8,128)(2,1)}, bf16[1024,12,64]{0,2,1:T(8,128)(2,1)S(1)}, u32[]{:S(2)}) copy-start(bf16[1024,12,64]{0,2,1:T(8,128)(2,1)S(1)} %get-tuple-element.133) | copy-start | bytes 4718596
  325.8 26.8 %copy-start.27 = (bf16[1024,768]{0,1:T(8,128)(2,1)}, bf16[1024,768]{0,1:T(8,128)(2,1)S(1)}, u32[]{:S(2)}) copy-start(bf16[1024,768]{0,1:T(8,128)(2,1)S(1)} %copy.70) | copy-start | bytes 4718596
  403.6 10.1 slice-start.2
  417.1 9.1 slice-start.18
  417.1 10.5 slice-start.19
  426.2 14.5 copy-start.44
  426.2 11.3 slice-start.14
  426.2 11.3 slice-start.22
  427.6 9.9 slice-start.15
  427.6 9.9 slice-start.23
  454.6 260.3 %reduce-scatter.3.cloned.1.call-start = ((), (), s32[]{:S(2)}) async-start(), calls=%async_computation.4 | async-start | bytes 9289728 | tf_op jit(solution)/shard_map/reduce_scatter | solution.py:264
  454.6 9.6 copy-start.57
  465.6 17.6 %copy-start.47 = (f32[512,4,64]{0,2,1:T(8,128)}, f32[512,4,64]{0,2,1:T(8,128)S(1)}, u32[]{:S(2)}) copy-start(f32[512,4,64]{0,2,1:T(8,128)S(1)} %fusion.156) | copy-start | bytes 1572868
  465.6 10.9 slice-start.4
  532.9 14.0 copy-start.30
  532.9 14.0 copy-start.70
  532.9 14.0 copy-start.73
  533.0 14.0 copy-start.77
  564.2 198.3 %all-reduce.24.cloned.1.call-start = ((), (), s32[]{:S(2)}) async-start(), calls=%async_computation.11 | async-start | bytes 3538944 | tf_op jit(solution)/shard_map/psum | solution.py:273
  714.9 249.5 %all-reduce.22.cloned.1.call-start = ((), (), s32[]{:S(2)}) async-start(), calls=%async_computation.10 | async-start | bytes 9437184 | tf_op jit(solution)/shard_map/psum | solution.py:291
  767.6 51.0 %copy-start.37 = (f32[480,768]{1,0:T(8,128)}, f32[480,768]{1,0:T(8,128)S(1)}, u32[]{:S(2)}) copy-start(f32[480,768]{1,0:T(8,128)S(1)} %get-tuple-element.90) | copy-start | bytes 4423684
  808.8 704.4 %copy-start.84 = (f32[896]{0:T(1024)}, f32[896]{0:T(1024)S(1)}, u32[]{:S(2)}) copy-start(f32[896]{0:T(1024)S(1)} %get-tuple-element.72) | copy-start | bytes 10756
  818.6 315.1 %all-reduce.20.cloned.1.call-start = ((), (), s32[]{:S(2)}) async-start(), calls=%async_computation.9 | async-start | bytes 9437184 | tf_op jit(solution)/shard_map/psum | solution.py:291
  964.5 8.5 copy-start.23
  964.5 8.5 copy-start.35
  989.9 313.2 %all-reduce.18.cloned.1.call-start = ((), (), s32[]{:S(2)}) async-start(), calls=%async_computation.8 | async-start | bytes 9437184 | tf_op jit(solution)/shard_map/psum | solution.py:291
  1133.7 8.5 copy-start.24
  1159.3 313.0 %all-reduce.16.cloned.1.call-start = ((), (), s32[]{:S(2)}) async-start(), calls=%async_computation.7 | async-start | bytes 9437184 | tf_op jit(solution)/shard_map/psum | solution.py:291
  1303.1 8.5 copy-start.25
  1328.6 313.2 %all-reduce.14.cloned.1.call-start = ((), (), s32[]{:S(2)}) async-start(), calls=%async_computation.6 | async-start | bytes 9437184 | tf_op jit(solution)/shard_map/psum | solution.py:291
  1472.4 8.5 copy-start.22
  1502.1 11.2 copy-start.82
  1502.1 11.2 copy-start.83
  1641.9 8.5 copy-start.17
  1650.4 11.9 copy-start.42
  1652.3 11.7 copy-start.16
  1670.0 10.1 copy-start.43
  (74 other events, 272.6 us)
Sparse Core Ops, SparseCore 0:
  10.2 96.9 all-gather.4
  109.4 121.3 all-gather.2
  454.7 109.9 reduce-scatter.4
  568.3 146.5 reduce-scatter.2
  717.3 45.2 all-reduce.23
  818.7 145.7 all-reduce.21
  990.1 143.5 all-reduce.19
  1159.4 143.6 all-reduce.17
  1328.7 143.5 all-reduce.15
  1498.1 143.7 all-reduce.13
where the time goes:
time: 1690 us
  waiting for transfers between devices  1090 us (64%)
  matrix products  328 us (19%)
  other arithmetic  129 us (8%)
  local copies, waits for them, and re-layouts  67.1 us (4%)
  blocking collectives  58 us (3%)
  between operations  17.4 us (1%)
    psum x5, waiting for transfers between devices, on_device(): lax.psum((gram_matrix(ortho_in), gram_matrix(ortho_out)), ('nar', 'wide'))  705 us
    reduce_scatter x1, waiting for transfers between devices, on_device(): lax.psum_scatter(lax.dot_general(grad_slice, x_low, (((0,), (0,)), ((), (...  150 us
    all_gather x1, waiting for transfers between devices, on_device(): lax.all_gather(w_in, 'wide', axis=0, tiled=True)  107 us
    all_gather x1, waiting for transfers between devices, on_device(): rows_piece = lax.all_gather(w_out, 'wide', axis=0, tiled=True)  92.3 us
    dot_general x10, matrix products, quintic_step(): jnp.dot(gram, gram, precision=highest, preferred_element_type=jnp.float32)  73.6 us
    psum x1, blocking collectives, on_device(): lax.psum((jnp.sum(block_in * block_in), jnp.sum(block_out * block_out), g...  39.6 us
    dot_general x10, matrix products, gram_matrix(): lax.dot_general(matrix, matrix, (((0,), (0,)), ((), ())), precision=highe...  36.6 us
  transfers between devices with their start and end apart: 10, of which 10 were waited for; matrix products, arithmetic and copies ran while one was open for 9% of the time, Pallas kernels for 0%

commit v1 on v0

v1 whole, which is shorter than its diff:
```python
from functools import partial

import jax
import jax.numpy as jnp
from jax import lax
from jax.experimental import pallas as pl
from jax.experimental.pallas import tpu as pltpu
from jax.sharding import PartitionSpec as P

D = 768
HEADS = 12
HEAD = 64
LEN = 1024
STEP = 10
FIN = 5376
FOUT = 3840
QKV = 3 * D

f32 = jnp.float32
bf16 = jnp.bfloat16
ns_linear = 3.4445
ns_cubic = -4.775
ns_quintic = 2.0315
muon_beta = 0.5
muon_rate = 0.8
muon_decay = 0.1
adam_rate = 0.8
adam_first = 0.9
adam_second = 0.95
adam_eps = 1e-08
norm_eps = 1e-06
penalty = 16384.0
vmem_bytes = 60 * 1024 * 1024
tile_rows = 256
pair = 2 * HEAD


def normalize(values):
    center = values - jnp.mean(values, axis=-1, keepdims=True)
    variance = jnp.mean(center * center, axis=-1, keepdims=True)
    inverse = lax.rsqrt(variance + norm_eps)
    return (center * inverse, inverse)


def norm_backward(grad_scaled, normed, inverse, axis=-1):
    mean_grad = jnp.mean(grad_scaled, axis=axis, keepdims=True)
    mean_cross = jnp.mean(grad_scaled * normed, axis=axis, keepdims=True)
    return inverse * (grad_scaled - mean_grad - normed * mean_cross)


def nn(a, b):
    return jnp.dot(a, b, preferred_element_type=f32)


def contract(a, b, dim_a, dim_b):
    return lax.dot_general(a, b, (((dim_a,), (dim_b,)), ((), ())), preferred_element_type=f32)


def normalize_columns(columns):
    center = columns - jnp.mean(columns, axis=0, keepdims=True)
    variance = jnp.mean(center * center, axis=0, keepdims=True)
    inverse = lax.rsqrt(variance + norm_eps)
    return (center * inverse, inverse)


def attention_kernel(
    q_ref, k_ref, v_ref, do_ref, onek_ref, penq_ref, gq_ref, gk_ref,
    att_ref, dq_ref, dk_ref, dv_ref, ggq_ref, ggk_ref,
    kaug, qaug_t, vaug_t, vaug, qnat, klow_t, exps, out_t, doaug_t, donat,
):
    length = q_ref.shape[0]
    step = pl.program_id(0)
    q_t = q_ref[...].T
    k_t = k_ref[...].T
    v_t = v_ref[...].T
    do_t = do_ref[...].T
    q_gain = gq_ref[...]
    k_gain = gk_ref[...]
    att_parts, dq_parts, dk_parts, dv_parts = [], [], [], []
    q_gain_grad = jnp.zeros((HEAD, 1), f32)
    k_gain_grad = jnp.zeros((HEAD, 1), f32)
    for h in range(2):
        rows = slice(HEAD * h, HEAD * (h + 1))
        q_hat, q_inverse = normalize_columns(q_t[rows].astype(f32))
        k_hat, k_inverse = normalize_columns(k_t[rows].astype(f32))
        q_low = (q_hat * q_gain).astype(bf16)
        k_low = (k_hat * k_gain).astype(bf16)
        klow_t[...] = k_low
        kaug[:, :HEAD] = k_low.T
        kaug[:, HEAD:] = onek_ref[...]
        qaug_t[:HEAD, :] = (q_low.astype(f32) * HEAD ** (-0.5)).astype(bf16)
        qaug_t[HEAD:, :] = penq_ref[...]
        qnat[...] = q_low.T
        v_head = v_t[rows]
        vaug_t[:HEAD, :] = v_head
        vaug_t[HEAD:, :] = jnp.ones((16, length), bf16)
        vaug[:, :HEAD] = v_head.T
        vaug[:, HEAD:] = jnp.ones((length, 16), bf16)
        terms = jnp.exp(nn(kaug[...], qaug_t[...])).astype(bf16)
        exps[...] = terms
        out_t[...] = nn(vaug_t[...], terms)
        summed = out_t[...]
        inverse_sum = 1.0 / summed[HEAD : HEAD + 1]
        attended = summed[:HEAD] * inverse_sum
        att_parts.append(attended)
        do_head = do_t[rows].astype(f32)
        inner = -jnp.sum(do_head * attended, axis=0, keepdims=True) * inverse_sum
        do_low = (do_head * inverse_sum).astype(bf16)
        inner_high = inner.astype(bf16).astype(f32)
        extra = lax.broadcasted_iota(jnp.int32, (16, length), 0)
        extra = jnp.where(extra == 0, inner_high, jnp.where(extra == 1, inner - inner_high, 0.0))
        doaug_t[:HEAD, :] = do_low
        doaug_t[HEAD:, :] = extra.astype(bf16)
        donat[...] = do_low.T
        terms = exps[...]
        dscores = (terms.astype(f32) * nn(vaug[...], doaug_t[...])).astype(bf16)
        dvalue = nn(terms, donat[...])
        dkey = nn(dscores, qnat[...]).T * HEAD ** (-0.5)
        dquery = nn(klow_t[...], dscores) * HEAD ** (-0.5)
        q_gain_grad += jnp.sum(dquery * q_hat, axis=1, keepdims=True)
        k_gain_grad += jnp.sum(dkey * k_hat, axis=1, keepdims=True)
        dq_parts.append(norm_backward(dquery * q_gain, q_hat, q_inverse, 0))
        dk_parts.append(norm_backward(dkey * k_gain, k_hat, k_inverse, 0))
        dv_parts.append(dvalue.T)
    att_ref[...] = jnp.concatenate(att_parts, 0).T.astype(bf16)
    dq_ref[...] = jnp.concatenate(dq_parts, 0).T.astype(bf16)
    dk_ref[...] = jnp.concatenate(dk_parts, 0).T.astype(bf16)
    dv_ref[...] = jnp.concatenate(dv_parts, 0).T.astype(bf16)

    @pl.when(step == 0)
    def _():
        ggq_ref[...] = jnp.zeros_like(ggq_ref)
        ggk_ref[...] = jnp.zeros_like(ggk_ref)

    ggq_ref[...] += jnp.broadcast_to(q_gain_grad, ggq_ref.shape)
    ggk_ref[...] += jnp.broadcast_to(k_gain_grad, ggk_ref.shape)


def attention(joined, dattended, ids, q_gain, k_gain):
    length = joined.shape[0]
    pairs = D // pair
    image = jnp.where(ids < 0, 4, ids)
    number = jnp.arange(16)
    onek = (image[:, None] == number[None, :]).astype(bf16)
    penq = jnp.where(image[None, :] == number[:, None], 0.0, -penalty).astype(bf16)

    def block(part):
        return pl.BlockSpec((length, pair), lambda p: (0, part * pairs + p))

    def whole(shape):
        return pl.BlockSpec(shape, lambda p: (0, 0))

    out = jax.ShapeDtypeStruct((length, D), bf16)
    gain = jax.ShapeDtypeStruct((HEAD, 128), f32)
    outs = pl.pallas_call(
        attention_kernel,
        grid=(pairs,),
        in_specs=[
            block(0), block(1), block(2), block(0),
            whole((length, 16)), whole((16, length)), whole((HEAD, 1)), whole((HEAD, 1)),
        ],
        out_specs=[block(0)] * 4 + [whole((HEAD, 128))] * 2,
        out_shape=[out] * 4 + [gain] * 2,
        scratch_shapes=[
            pltpu.VMEM((length, HEAD + 16), bf16),
            pltpu.VMEM((HEAD + 16, length), bf16),
            pltpu.VMEM((HEAD + 16, length), bf16),
            pltpu.VMEM((length, HEAD + 16), bf16),
            pltpu.VMEM((length, HEAD), bf16),
            pltpu.VMEM((HEAD, length), bf16),
            pltpu.VMEM((length, length), bf16),
            pltpu.VMEM((HEAD + 16, length), f32),
            pltpu.VMEM((HEAD + 16, length), bf16),
            pltpu.VMEM((length, HEAD), bf16),
        ],
        compiler_params=pltpu.CompilerParams(vmem_limit_bytes=vmem_bytes),
        cost_estimate=pl.CostEstimate(
            flops=HEADS * 12 * length * length * 256,
            bytes_accessed=16 * length * D,
            transcendentals=HEADS * length * length,
        ),
        name="attention",
    )(joined, joined, joined, dattended, onek, penq, q_gain.reshape(HEAD, 1), k_gain.reshape(HEAD, 1))
    return (*outs[:4], outs[4][:, 0], outs[5][:, 0])


def gelu_pair(u):
    z = jnp.abs(u) * 0.7071067811865476
    t = 1.0 / (1.0 + 0.3275911 * z)
    e = jnp.exp(-z * z)
    poly = t * (0.127414796 + t * (-0.142248368 + t * (0.7107068705 + t * (-0.7265760135 + t * 0.5307027145))))
    half = poly * e
    phi = jnp.where(u >= 0, 1.0 - half, half)
    return (u * phi, phi + u * (0.3989422804014327 * e))


def mlp_kernel(x_ref, gy_ref, wu_ref, wd_ref, res_ref, gn_ref, gwu_ref, gwd_ref):
    @pl.when(pl.program_id(0) == 0)
    def _():
        res_ref[...] = jnp.zeros_like(res_ref)
        gn_ref[...] = jnp.zeros_like(gn_ref)

    x, grad_y, wu, wd = x_ref[...], gy_ref[...], wu_ref[...], wd_ref[...]
    upward = contract(x, wu, 1, 1).astype(bf16).astype(f32)
    grad_hidden = contract(grad_y, wd, 1, 1)
    active, slope = gelu_pair(upward)
    active = active.astype(bf16)
    dupward = (grad_hidden * slope).astype(bf16)
    res_ref[...] += contract(active, wd, 1, 0)
    gn_ref[...] += contract(dupward, wu, 1, 0)
    gwu_ref[...] = contract(dupward, x, 0, 0).astype(bf16)
    gwd_ref[...] = contract(active, grad_y, 0, 0).astype(bf16)


def mlp(x_low, grad_y, w_up, w_down):
    length = x_low.shape[0]
    hidden = w_up.shape[0]
    tile = 512 if hidden % 512 == 0 else hidden
    whole = pl.BlockSpec((length, D), lambda t: (0, 0))
    part = pl.BlockSpec((tile, D), lambda t: (t, 0))
    total = jax.ShapeDtypeStruct((length, D), f32)
    grad = jax.ShapeDtypeStruct((hidden, D), bf16)
    return pl.pallas_call(
        mlp_kernel,
        grid=(hidden // tile,),
        in_specs=[whole, whole, part, part],
        out_specs=[whole, whole, part, part],
        out_shape=[total, total, grad, grad],
        compiler_params=pltpu.CompilerParams(vmem_limit_bytes=vmem_bytes),
        cost_estimate=pl.CostEstimate(
            flops=18 * length * D * hidden,
            bytes_accessed=12 * length * D + 8 * hidden * D,
            transcendentals=length * hidden,
        ),
        name="mlp",
    )(x_low, grad_y, w_up, w_down)


def split(values):
    high = values.astype(bf16)
    return (high, (values - high.astype(f32)).astype(bf16))


def newton_kernel(g_ref, m_ref, w_ref, o_ref, gh, gl, sh, sl, ph, pw, g32, x32, *, rate, decay):
    count = D // tile_rows

    def span(i):
        return slice(i * tile_rows, (i + 1) * tile_rows)

    def store(high_ref, low_ref, i, j, value):
        high_ref[span(i), span(j)], low_ref[span(i), span(j)] = split(value)
        if i != j:
            high_ref[span(j), span(i)], low_ref[span(j), span(i)] = split(value.T)

    def symmetric(ah, al, bh, bl, post):
        for i in range(count):
            for j in range(i, count):
                rows, columns = span(i), span(j)
                post(
                    i,
                    j,
                    nn(ah[rows, :], bh[:, columns])
                    + (nn(ah[rows, :], bl[:, columns]) + nn(al[rows, :], bh[:, columns])),
                )

    def diagonal(size):
        shape = (size, size)
        return lax.broadcasted_iota(jnp.int32, shape, 0) == lax.broadcasted_iota(jnp.int32, shape, 1)

    gram = g_ref[...]
    trace = jnp.sum(jnp.where(diagonal(D), gram, 0.0), axis=0, keepdims=True)
    trace = jnp.sum(trace, axis=1, keepdims=True)
    inverse = 1.0 / (jnp.sqrt(trace) + 1e-07)
    gram = gram * (inverse * inverse)
    g32[...] = gram
    gh[...], gl[...] = split(gram)
    x32[...] = m_ref[...] * inverse

    def sweep(last):
        def keep_factor(i, j, value):
            value = ns_cubic * g32[span(i), span(j)] + ns_quintic * value
            if i == j:
                value = value + jnp.where(diagonal(tile_rows), ns_linear, 0.0)
            store(ph, pw, i, j, value)

        def keep_gram(i, j, value):
            g32[span(i), span(j)] = value
            store(gh, gl, i, j, value)

        symmetric(gh, gl, gh, gl, keep_factor)
        xh, xl = split(x32[...])
        x32[...] = nn(xh, ph[...]) + (nn(xh, pw[...]) + nn(xl, ph[...]))
        if not last:
            symmetric(gh, gl, ph, pw, partial(store, sh, sl))
            symmetric(sh, sl, ph, pw, keep_gram)

    @pl.loop(0, 4)
    def _(k):
        sweep(False)

    sweep(True)
    o_ref[...] = w_ref[...].astype(f32) * decay - rate * x32[...]


def newton(gram, momentum, weights, rate):
    rows = momentum.shape[0]
    whole = pl.BlockSpec(memory_space=pltpu.VMEM)
    return pl.pallas_call(
        partial(newton_kernel, rate=rate, decay=1 - muon_rate * muon_decay),
        in_specs=[whole] * 3,
        out_specs=whole,
        out_shape=jax.ShapeDtypeStruct((rows, D), f32),
        scratch_shapes=[pltpu.VMEM((D, D), bf16)] * 6 + [pltpu.VMEM((D, D), f32), pltpu.VMEM((rows, D), f32)],
        compiler_params=pltpu.CompilerParams(vmem_limit_bytes=vmem_bytes),
        cost_estimate=pl.CostEstimate(
            flops=6 * D * D * (9 * D + 5 * rows), bytes_accessed=4 * D * D + 10 * rows * D, transcendentals=0
        ),
        name="newton",
    )(gram, momentum, weights)


def gram_matrix(rows):
    return lax.dot_general(
        rows, rows, (((0,), (0,)), ((), ())), precision=lax.Precision.HIGH, preferred_element_type=f32
    )


def swap(values, axis, bit):
    size = lax.axis_size(axis)
    return lax.ppermute(values, axis, [(i, i ^ bit) for i in range(size)])


def bits(size):
    return [1 << b for b in range(size.bit_length() - 1)]


def sum_over(values, halving, full):
    sides = []
    for axis, bit in halving:
        upper = (lax.axis_index(axis) & bit) != 0
        size = values.shape[0] // 2
        low, high = values[:size], values[size:]
        kept, sent = jnp.where(upper, high, low), jnp.where(upper, low, high)
        values = kept + swap(sent, axis, bit)
        sides.append(upper)
    for axis, bit in full:
        values = values + swap(values, axis, bit)
    for (axis, bit), upper in zip(reversed(halving), reversed(sides), strict=True):
        other = swap(values, axis, bit)
        values = jnp.where(
            upper, jnp.concatenate([other, values], 0), jnp.concatenate([values, other], 0)
        )
    return values


def fold(gram):
    half = D // 2
    i = lax.broadcasted_iota(jnp.int32, (half, half), 0)
    j = lax.broadcasted_iota(jnp.int32, (half, half), 1)
    corner = jnp.where(i <= j, gram[:half, :half], gram[half:, half:])
    diagonal = jnp.sum(jnp.where(i == j, gram[half:, half:], 0.0), axis=0)
    return (jnp.concatenate([corner, gram[:half, half:]], axis=1), diagonal)


def unfold(folded, diagonal):
    half = D // 2
    i = lax.broadcasted_iota(jnp.int32, (half, half), 0)
    j = lax.broadcasted_iota(jnp.int32, (half, half), 1)
    corner, side = folded[:, :half], folded[:, half:]
    first = jnp.where(i <= j, corner, corner.T)
    last = jnp.where(i > j, corner, jnp.where(i == j, diagonal[None, :], corner.T))
    return jnp.concatenate(
        [jnp.concatenate([first, side], axis=1), jnp.concatenate([side.T, last], axis=1)], axis=0
    )


def on_device(tokens, cotangent, image_ids, w_in, w_out, gains, mom_in, mom_out, gain_m, gain_v):
    row_count = tokens.shape[0]
    rows_in = w_in.shape[0]
    rows_out = w_out.shape[0]
    nar_count = lax.axis_size("nar")
    wide_count = lax.axis_size("wide")
    nar_place = lax.axis_index("nar")
    share_in = rows_in // nar_count
    share_out = rows_out // nar_count
    everyone = ("wide", "nar")

    def share(rows, size):
        return lax.dynamic_slice_in_dim(rows, nar_place * size, size, 0)

    w_in_all = lax.all_gather(share(w_in, share_in), everyone, axis=0, tiled=True)
    w_out_all = lax.all_gather(share(w_out, share_out), everyone, axis=0, tiled=True)

    x_float = tokens.astype(f32)
    ln_gain = gains[:D]
    x_hat, x_inverse = normalize(x_float)
    x_low = (x_hat * ln_gain).astype(bf16)
    live = (image_ids.reshape(row_count) >= 0)[:, None]
    grad_y = jnp.where(live, cotangent, jnp.zeros_like(cotangent))

    w_qkv, w_up = w_in_all[:QKV], w_in_all[QKV:]
    w_att, w_down = w_out_all[:D], w_out_all[D:]
    joined = contract(x_low, w_qkv, 1, 1).astype(bf16)
    dattended = contract(grad_y, w_att, 1, 1).astype(bf16)
    attended, dqueries, dkeys, dvalues, q_gain_grad, k_gain_grad = attention(
        joined, dattended, image_ids.reshape(row_count), gains[D : D + HEAD], gains[D + HEAD :]
    )
    mlp_result, mlp_normed, grad_up, grad_down = mlp(x_low, grad_y, w_up, w_down)

    result = (x_float + (mlp_result + nn(attended, w_att))).astype(bf16)
    grad_qkv = jnp.concatenate([dqueries, dkeys, dvalues], axis=1)
    grad_normed = mlp_normed + nn(grad_qkv, w_qkv)
    ln_grad = jnp.sum(grad_normed * x_hat, axis=0)
    grad_tokens = (
        grad_y.astype(f32) + norm_backward(grad_normed * ln_gain, x_hat, x_inverse)
    ).astype(bf16)

    grad_out_local = jnp.concatenate([contract(attended, grad_y, 0, 0).astype(bf16), grad_down], axis=0)
    grad_in_local = jnp.concatenate([contract(grad_qkv, x_low, 0, 0).astype(bf16), grad_up], axis=0)
    part_out = lax.psum_scatter(grad_out_local, everyone, scatter_dimension=0, tiled=True)
    part_in = lax.psum_scatter(grad_in_local, everyone, scatter_dimension=0, tiled=True)
    grad_w_out = lax.all_gather(part_out, "nar", axis=0, tiled=True).astype(f32)
    grad_w_in = lax.all_gather(part_in, "nar", axis=0, tiled=True).astype(f32)
    mom_in_new = muon_beta * mom_in + grad_w_in
    mom_out_new = muon_beta * mom_out + grad_w_out

    folded_in, diagonal_in = fold(
        gram_matrix(muon_beta * share(mom_in, share_in) + part_in.astype(f32))
    )
    folded_out, diagonal_out = fold(
        gram_matrix(muon_beta * share(mom_out, share_out) + part_out.astype(f32))
    )
    wide_bits = bits(wide_count)
    halving = [("nar", 1), ("wide", wide_bits[0]), ("nar", 2)]
    full = [("wide", bit) for bit in wide_bits[1:]]
    gain_terms = jnp.concatenate([ln_grad, q_gain_grad, k_gain_grad])
    extra = jnp.concatenate([gain_terms, diagonal_in, diagonal_out])
    extra = jnp.pad(extra, (0, 64 * D - extra.shape[0])).reshape(64, D)
    summed = sum_over(jnp.concatenate([folded_in, folded_out, extra], axis=0), halving, full)
    half = D // 2
    extra = summed[2 * half :].reshape(64 * D)
    count = gain_terms.shape[0]
    grad_gains = extra[:count]
    gram_in = unfold(summed[:half], extra[count : count + half])
    gram_out = unfold(summed[half : 2 * half], extra[count + half : count + 2 * half])

    w_in_new = newton(gram_in, mom_in_new, w_in, muon_rate * (FIN / D) ** 0.5)
    w_out_new = newton(gram_out, mom_out_new, w_out, muon_rate * (FOUT / D) ** 0.5)
    gain_m_new = adam_first * gain_m + (1 - adam_first) * grad_gains
    gain_v_new = adam_second * gain_v + (1 - adam_second) * grad_gains * grad_gains
    gains_new = gains - adam_rate * (gain_m_new / (1 - adam_first**STEP)) / (
        jnp.sqrt(gain_v_new / (1 - adam_second**STEP)) + adam_eps
    )
    return (
        result,
        grad_tokens,
        grad_w_in,
        grad_w_out,
        grad_gains,
        mom_in_new,
        mom_out_new,
        gain_m_new,
        gain_v_new,
        w_in_new,
        w_out_new,
        gains_new,
    )


def solution(mesh):
    rows = P(("nar", "wide"), None)
    wide = P("wide", None)
    return jax.shard_map(
        on_device,
        mesh=mesh,
        in_specs=(rows, rows, rows, wide, wide, P(), wide, wide, P(), P()),
        out_specs=(rows, rows, wide, wide, P(), wide, wide, P(), P(), wide, wide, P()),
        check_vma=False,
    )
```

time: 1690 us -> 764 us (0.45)
  waiting for transfers between devices: 1090 us -> 410 us
  matrix products: 328 us -> 41.2 us
  Pallas kernels: 0 us -> 167 us
  other arithmetic: 129 us -> 51.5 us
  blocking collectives: 58 us -> 18.6 us
  local copies, waits for them, and re-layouts: 67.1 us -> 47.6 us
    psum x6 -> x0, waiting for transfers between devices: 737 us -> none  [the longest x5 705 us: on_device(): lax.psum((gram_matrix(ortho_in), gram_matrix(ortho_out)), ('nar', 'wide'))]
    dot_general x72 -> x8, matrix products: 328 us -> 41.2 us  [the longest x4 21.2 us: contract(): lax.dot_general(a, b, (((dim_a,), (dim_b,)), ((), ())), preferred_element...]
    pallas_call x0 -> x4, Pallas kernels: none -> 167 us  [the longest x2 81.5 us: newton(): pl.pallas_call(partial(newton_kernel, rate=rate, decay=1 - muon_rate * mu...]
    convert_element_type x11 -> x4, other arithmetic: 79.4 us -> 6.29 us  [the longest x1 4.24 us: on_device(): grad_tokens = (grad_y.astype(f32) + norm_backward(grad_normed * ln_gain,...]
    all_gather x2, waiting for transfers between devices: 199 us -> 133 us  [the longest x1 70.4 us: on_device(): lax.all_gather(share(w_in, share_in), everyone, axis=0, tiled=True)]
    reduce_scatter x2, waiting for transfers between devices: 151 us -> 214 us  [the longest x1 132 us: on_device(): lax.psum_scatter(grad_in_local, everyone, scatter_dimension=0, tiled=True)]
    ppermute x0 -> x8, waiting for transfers between devices: none -> 62.7 us  [swap(): return lax.ppermute(values, axis, [(i, i ^ bit) for i in range(size)])]
    psum x1 -> x0, blocking collectives: 39.6 us -> none  [on_device(): lax.psum((jnp.sum(block_in * block_in), jnp.sum(block_out * block_out), g...]
  transfers between devices with their start and end apart: 10 -> 12, of which waited for: 10 -> 11; matrix products, arithmetic and copies ran while one was open for 9% -> 8% of each run, Pallas kernels for 0% -> 0%
where the time goes in v1:
time: 764 us; the launch traced here: 760 us
  waiting for transfers between devices  410 us (54%)
  Pallas kernels  167 us (22%)
  other arithmetic  51.5 us (7%)
  local copies, waits for them, and re-layouts  47.6 us (6%)
  matrix products  41.2 us (5%)
  blocking collectives  18.6 us (2%)
  between operations  14.5 us (2%)
  starting transfers between devices  9.45 us (1%)
    reduce_scatter x1, waiting for transfers between devices, on_device(): lax.psum_scatter(grad_in_local, everyone, scatter_dimension=0, tiled=True)  132 us
    reduce_scatter x1, waiting for transfers between devices, on_device(): lax.psum_scatter(grad_out_local, everyone, scatter_dimension=0, tiled=True)  82.6 us
    pallas_call x2, Pallas kernels, newton(): pl.pallas_call(partial(newton_kernel, rate=rate, decay=1 - muon_rate * mu...  81.5 us
    all_gather x1, waiting for transfers between devices, on_device(): lax.all_gather(share(w_in, share_in), everyone, axis=0, tiled=True)  70.4 us
    all_gather x1, waiting for transfers between devices, on_device(): lax.all_gather(share(w_out, share_out), everyone, axis=0, tiled=True)  62.9 us
    ppermute x8, waiting for transfers between devices, swap(): return lax.ppermute(values, axis, [(i, i ^ bit) for i in range(size)])  62.7 us
    pallas_call x1, Pallas kernels, attention(): pl.pallas_call(attention_kernel, grid=(pairs,), in_specs=[block(0), block...  44.5 us
    pallas_call x1, Pallas kernels, mlp(): pl.pallas_call(mlp_kernel, grid=(hidden // tile,), in_specs=[whole, whole...  40.9 us
  transfers between devices with their start and end apart: 12, of which 11 were waited for; matrix products, arithmetic and copies ran while one was open for 8% of the time, Pallas kernels for 0%

profile of v1, /device:TPU:0, one launch (start us, length us, event | category | flops | bytes accessed | tf_op | source)
XLA Modules:
  0.0 760.2 jit_solution(12327564459641182940)
XLA Ops:
  7.3 1.7 constant_dynamic-slice_fusion
  9.0 1.8 constant_dynamic-slice_fusion.1
  13.1 1.7 convert_reduce_fusion
  19.0 62.9 %all-gather.5.cloned.1.call-done = bf16[3840,768]{1,0:T(8,128)(2,1)} async-done(((bf16[120,768]{1,0:T(8,128)(2,1)}), bf16[3840,768]{1,0:T(8,128)(2,1)}) %all-gather.5.cloned.1.call-update) | async-done | bytes 5898256 | tf_op jit(solution)/shard_map/all_gather | solution.py:392
  81.9 5.0 slice.127.wd_ref
  86.9 3.8 convolution_convert_fusion.2.do_ref
  90.7 70.4 %all-gather.3.cloned.1.call-done = bf16[5376,768]{1,0:T(8,128)(2,1)} async-done(((bf16[168,768]{1,0:T(8,128)(2,1)}), bf16[5376,768]{1,0:T(8,128)(2,1)}) %all-gather.3.cloned.1.call-update) | async-done | bytes 8257552 | tf_op jit(solution)/shard_map/all_gather | solution.py:391
  161.1 7.7 %convolution_convert_fusion.q_ref.k_ref.v_ref = bf16[1024,2304]{1,0:T(8,128)(2,1)} fusion(bf16[1024,768]{1,0:T(8,128)(2,1)S(1)} %fusion.6.x_ref, bf16[5376,768]{1,0:T(8,128)(2,1)} %all-gather.3.cloned.1.call-done), kind=kOutput, calls=%fused_computation.2 | convolution fusion | flops 3626237952 | bytes 9830400 | tf_op jit(solution)/shard_map/dot_general | solution.py:56
  168.8 44.5 %attention.1 = (bf16[1024,768]{1,0:T(8,128)(2,1)}, bf16[1024,768]{1,0:T(8,128)(2,1)}, bf16[1024,768]{1,0:T(8,128)(2,1)}, bf16[1024,768]{1,0:T(8,128)(2,1)}, f32[64,128]{1,0:T(8,128)}, /*index=5*/f32[64,128]{1,0:T(8,128)}) custom-call(bf16[1024,2304]{1,0:T(8,128)(2,1)} %convolution_convert_fusion.q_ref.k_ref.v_ref, ...), custom_call_target="tpu_custom_call" | custom-call | flops 38654705664 | bytes 12582912 | tf_op jit(solution)/shard_map/attention/pallas_call | solution.py:155
  213.4 3.9 convolution_convert_fusion.3
  217.2 4.9 slice.126.wu_ref
  222.1 40.9 %mlp.1 = (f32[1024,768]{1,0:T(8,128)}, f32[1024,768]{1,0:T(8,128)}, bf16[3072,768]{1,0:T(8,128)(2,1)}, bf16[3072,768]{1,0:T(8,128)(2,1)}) custom-call(bf16[1024,768]{1,0:T(8,128)(2,1)} %copy-done.10, bf16[1024,768]{1,0:T(8,128)(2,1)} %broadcast_select_fusion.gy_ref, bf16[3072,768]{1,0:T(8,128)(2,1)} %slice.126.wu_ref, bf16[3072,768]{1,0:T(8,128)(2,1)} %slice.127.wd_ref), custom_call_target="tpu_custom_call" | custom-call | flops 43486543872 | bytes 28311552 | tf_op jit(solution)/shard_map/mlp/pallas_call | solution.py:223
  263.0 5.3 pad_maximum_fusion.1
  268.4 1.6 constant_dynamic-update-slice_fusion.2
  271.9 5.8 convolution_convert_fusion.1
  277.8 7.4 pad_maximum_fusion
  286.1 11.1 %fusion.12 = (f32[768]{0:T(1024)S(1)}, f32[1024]{0:T(1024)}, f32[1024]{0:T(1024)}, f32[1024,768]{1,0:T(8,128)}) fusion(bf16[1024,768]{1,0:T(8,128)(2,1)S(1)} %copy-done, f32[1024]{0:T(1024)S(1)} %add_rsqrt_fusion, f32[1024]{0:T(1024)S(1)} %broadcast_multiply_fusion.2, f32[768]{0:T(1024)S(1)} %bitcast.30, f32[1024,768]{1,0:T(8,128)} %get-tuple-element.24, ...), kind=kOutput, calls=%fused_computation.19 | convolution fusion | flops 3631740160 | bytes 16144384 | tf_op jit(solution)/shard_map/dot_general | solution.py:52
  297.2 82.6 %reduce-scatter.5.cloned.1.call-done = bf16[120,768]{1,0:T(8,128)(2,1)} async-done(((bf16[3840,768]{1,0:T(8,128)(2,1)}), bf16[120,768]{1,0:T(8,128)(2,1)}) %reduce-scatter.5.cloned.1.call-update) | async-done | bytes 184336 | tf_op jit(solution)/shard_map/reduce_scatter | solution.py:420
  379.8 2.4 fusion.33
  383.3 131.7 %reduce-scatter.3.cloned.1.call-done = bf16[168,768]{1,0:T(8,128)(2,1)} async-done(((bf16[5376,768]{1,0:T(8,128)(2,1)}), bf16[168,768]{1,0:T(8,128)(2,1)}) %reduce-scatter.3.cloned.1.call-update) | async-done | bytes 258064 | tf_op jit(solution)/shard_map/reduce_scatter | solution.py:421
  514.9 2.7 fusion.28
  519.0 2.4 fusion.22
  522.9 3.2 collective-permute-done
  527.7 2.8 select_add_fusion
  531.7 2.2 copy.75
  535.4 15.3 %collective-permute-done.1 = f32[208,768]{1,0:T(8,128)} collective-permute-done((f32[208,768]{1,0:T(8,128)}, f32[208,768]{1,0:T(8,128)}, u32[]{:S(2)}, u32[]{:S(2)}) %collective-permute-start.1) | collective-permute-done | bytes 639008 | tf_op jit(solution)/shard_map/ppermute | solution.py:330
  550.7 2.2 copy.76
  556.0 8.9 %collective-permute-done.2 = f32[104,768]{0,1:T(8,128)S(1)} collective-permute-done((f32[104,768]{0,1:T(8,128)S(1)}, f32[104,768]{0,1:T(8,128)S(1)}, u32[]{:S(2)}, u32[]{:S(2)}) %collective-permute-start.2) | collective-permute-done | bytes 319520 | tf_op jit(solution)/shard_map/ppermute | solution.py:330
  566.6 7.9 %collective-permute-done.3 = f32[104,768]{0,1:T(8,128)S(1)} collective-permute-done((f32[104,768]{0,1:T(8,128)S(1)}, f32[104,768]{0,1:T(8,128)S(1)}, u32[]{:S(2)}, u32[]{:S(2)}) %collective-permute-start.3) | collective-permute-done | bytes 319520 | tf_op jit(solution)/shard_map/ppermute | solution.py:330
  574.6 1.8 collective-permute-start.4
  577.7 14.8 %collective-permute-done.4 = f32[104,768]{0,1:T(8,128)S(1)} collective-permute-done((f32[104,768]{0,1:T(8,128)S(1)}, f32[104,768]{0,1:T(8,128)S(1)}, u32[]{:S(2)}, u32[]{:S(2)}) %collective-permute-start.4) | collective-permute-done | bytes 319520 | tf_op jit(solution)/shard_map/ppermute | solution.py:330
  595.0 7.6 %collective-permute-done.5 = f32[104,768]{0,1:T(8,128)S(1)} collective-permute-done((f32[104,768]{0,1:T(8,128)S(1)}, f32[104,768]{0,1:T(8,128)S(1)}, u32[]{:S(2)}, u32[]{:S(2)}) %collective-permute-start.5) | collective-permute-done | bytes 319520 | tf_op jit(solution)/shard_map/ppermute | solution.py:330
  604.9 4.2 fusion.11
  609.1 3.9 fusion.14
  613.0 4.9 collective-permute-done.6
  621.5 8.6 %all_gather.15 = bf16[480,768]{1,0:T(8,128)(2,1)S(1)} all-gather(bf16[120,768]{1,0:T(8,128)(2,1)S(1)} %copy-done.18), channel_id=1, replica_groups=mesh['nar'=4,'wide'=8] {'nar'}, dimensions={0}, use_global_device_ids=true | all-gather | bytes 921600 | tf_op jit(solution)/shard_map/all_gather | solution.py:422
  630.1 1.9 multiply_add_fusion.1
  632.0 10.0 %all_gather.14 = bf16[672,768]{1,0:T(8,128)(2,1)S(1)} all-gather(bf16[168,768]{1,0:T(8,128)(2,1)S(1)} %copy-done.17), channel_id=1, replica_groups=mesh['nar'=4,'wide'=8] {'nar'}, dimensions={0}, use_global_device_ids=true | all-gather | bytes 1290240 | tf_op jit(solution)/shard_map/all_gather | solution.py:423
  642.0 2.3 multiply_add_fusion
  644.3 1.8 copy.81
  646.1 3.4 pad_maximum_fusion.3
  649.5 3.4 copy.83
  653.0 2.1 copy.84
  655.1 2.0 broadcast_select_fusion.1
  659.7 3.1 bitcast_select_fusion.1
  666.8 2.0 copy.88.g_ref
  670.3 42.7 %newton.2 = f32[672,768]{1,0:T(8,128)} custom-call(f32[768,768]{1,0:T(8,128)} %copy.88.g_ref, f32[672,768]{1,0:T(8,128)} %get-tuple-element.41.m_ref, bf16[672,768]{1,0:T(8,128)(2,1)} %w_ref.2), custom_call_target="tpu_custom_call" | custom-call | flops 36352032768 | bytes 7520256 | tf_op jit(solution)/shard_map/newton/pallas_call | solution.py:308
  714.6 38.7 %newton.3 = f32[480,768]{1,0:T(8,128)} custom-call(f32[768,768]{1,0:T(8,128)} %maximum_maximum_fusion.1.g_ref, f32[480,768]{1,0:T(8,128)} %get-tuple-element.39.m_ref, bf16[480,768]{1,0:T(8,128)(2,1)} %w_ref.3), custom_call_target="tpu_custom_call" | custom-call | flops 32954646528 | bytes 6045696 | tf_op jit(solution)/shard_map/newton/pallas_call | solution.py:308
  (130 shorter events, 41.6 us)
Async XLA Ops:
  7.2 7.7 %copy-start = (bf16[1024,768]{1,0:T(8,128)(2,1)S(1)}, bf16[1024,768]{1,0:T(8,128)(2,1)}, u32[]{:S(2)}) copy-start(bf16[1024,768]{1,0:T(8,128)(2,1)} %param.10) | copy-start | bytes 4718596
  7.2 7.6 %copy-start.21 = (s32[1,1024]{1,0:T(1,128)S(1)}, s32[1,1024]{1,0:T(1,128)}, u32[]{:S(2)}) copy-start(s32[1,1024]{1,0:T(1,128)} %param.12) | copy-start | bytes 12292
  7.2 74.7 %all-gather.5.cloned.1.call-start = ((), (), s32[]{:S(2)}) async-start(), calls=%async_computation.3 | async-start | bytes 6082560 | tf_op jit(solution)/shard_map/all_gather | solution.py:392
  9.0 8.1 %copy-start.2 = (bf16[1024,768]{1,0:T(8,128)(2,1)S(1)}, bf16[1024,768]{1,0:T(8,128)(2,1)}, u32[]{:S(2)}) copy-start(bf16[1024,768]{1,0:T(8,128)(2,1)} %param.11) | copy-start | bytes 4718596
  9.0 152.1 %all-gather.3.cloned.1.call-start = ((), (), s32[]{:S(2)}) async-start(), calls=%async_computation.2 | async-start | bytes 8515584 | tf_op jit(solution)/shard_map/all_gather | solution.py:391
  10.8 368.9 %reduce-scatter.5.cloned.1.call-start = ((), (), s32[]{:S(2)}) async-start(), calls=%async_computation.5 | async-start | bytes 6082560 | tf_op jit(solution)/shard_map/reduce_scatter | solution.py:420
  14.9 3.5 copy-start.20
  18.9 142.2 %copy-start.10 = (bf16[1024,768]{1,0:T(8,128)(2,1)}, bf16[1024,768]{1,0:T(8,128)(2,1)S(1)}, u32[]{:S(2)}) copy-start(bf16[1024,768]{1,0:T(8,128)(2,1)S(1)} %fusion.6.x_ref) | copy-start | bytes 4718596
  81.9 5.0 copy-start.14
  168.8 44.6 %copy-start.15 = (bf16[1024,768]{1,0:T(8,128)(2,1)S(1)}, bf16[1024,768]{1,0:T(8,128)(2,1)}, u32[]{:S(2)}) copy-start(bf16[1024,768]{1,0:T(8,128)(2,1)} %broadcast_select_fusion.gy_ref) | copy-start | bytes 4718596
  222.1 40.9 %copy-start.16 = (bf16[768,768]{1,0:T(8,128)(2,1)S(1)}, bf16[768,768]{1,0:T(8,128)(2,1)}, u32[]{:S(2)}) copy-start(bf16[768,768]{1,0:T(8,128)(2,1)} %convolution_convert_fusion.3) | copy-start | bytes 3538948
  268.3 1.9 copy-start.13
  268.3 246.6 %reduce-scatter.3.cloned.1.call-start = ((), (), s32[]{:S(2)}) async-start(), calls=%async_computation.4 | async-start | bytes 8515584 | tf_op jit(solution)/shard_map/reduce_scatter | solution.py:421
  270.0 1.5 copy-start.12
  270.3 1.6 copy-start.11
  271.9 5.8 copy-start.19
  285.2 0.8 copy-start.22
  285.2 0.8 copy-start.23
  522.9 3.2 collective-permute-start
  533.9 16.7 %collective-permute-start.1 = (f32[208,768]{1,0:T(8,128)}, f32[208,768]{1,0:T(8,128)}, u32[]{:S(2)}, u32[]{:S(2)}) collective-permute-start(f32[208,768]{1,0:T(8,128)} %copy.75), channel_id=1, source_target_pairs={{0,1},{1,0},{2,3},{3,2},{4,5},{5,4},{6,7},{7,6},{8,9},{9,8},{10,11... | collective-permute-start | bytes 1916936 | tf_op jit(solution)/shard_map/ppermute | solution.py:330
  554.5 40.5 %copy-start.24 = (f32[1024]{0:T(1024)S(1)}, f32[1024]{0:T(1024)}, u32[]{:S(2)}) copy-start(f32[1024]{0:T(1024)} %get-tuple-element.33) | copy-start | bytes 12292
  554.5 40.5 %copy-start.25 = (f32[1024]{0:T(1024)S(1)}, f32[1024]{0:T(1024)}, u32[]{:S(2)}) copy-start(f32[1024]{0:T(1024)} %get-tuple-element.34) | copy-start | bytes 12292
  554.5 10.4 %collective-permute-start.2 = (f32[104,768]{0,1:T(8,128)S(1)}, f32[104,768]{0,1:T(8,128)S(1)}, u32[]{:S(2)}, u32[]{:S(2)}) collective-permute-start(f32[104,768]{0,1:T(8,128)S(1)} %slice_select_fusion.3), channel_id=1, source_target_pairs={{0,16},{8,24},{16,0},{24,8},{1,17},{9,25},{17,1},{25,9},{2,18},{10... | collective-permute-start | bytes 958472 | tf_op jit(solution)/shard_map/ppermute | solution.py:330
  565.1 9.5 %collective-permute-start.3 = (f32[104,768]{0,1:T(8,128)S(1)}, f32[104,768]{0,1:T(8,128)S(1)}, u32[]{:S(2)}, u32[]{:S(2)}) collective-permute-start(f32[104,768]{0,1:T(8,128)S(1)} %select_add_fusion.2), channel_id=1, source_target_pairs={{0,2},{1,3},{2,0},{3,1},{4,6},{5,7},{6,4},{7,5},{8,10},{9,11},{10,... | collective-permute-start | bytes 958472 | tf_op jit(solution)/shard_map/ppermute | solution.py:330
  574.6 17.9 %collective-permute-start.4 = (f32[104,768]{0,1:T(8,128)S(1)}, f32[104,768]{0,1:T(8,128)S(1)}, u32[]{:S(2)}, u32[]{:S(2)}) collective-permute-start(f32[104,768]{0,1:T(8,128)S(1)} %add.89), channel_id=1, source_target_pairs={{0,4},{1,5},{2,6},{3,7},{4,0},{5,1},{6,2},{7,3},{8,12},{9,13},{10,... | collective-permute-start | bytes 958472 | tf_op jit(solution)/shard_map/ppermute | solution.py:330
  592.5 10.1 %collective-permute-start.5 = (f32[104,768]{0,1:T(8,128)S(1)}, f32[104,768]{0,1:T(8,128)S(1)}, u32[]{:S(2)}, u32[]{:S(2)}) collective-permute-start(f32[104,768]{0,1:T(8,128)S(1)} %add.90), channel_id=1, source_target_pairs={{0,16},{8,24},{16,0},{24,8},{1,17},{9,25},{17,1},{25,9},{2,18},{10... | collective-permute-start | bytes 958472 | tf_op jit(solution)/shard_map/ppermute | solution.py:330
  603.4 14.6 %collective-permute-start.6 = (f32[208,768]{1,0:T(8,128)S(1)}, f32[208,768]{1,0:T(8,128)}, u32[]{:S(2)}, u32[]{:S(2)}) collective-permute-start(f32[208,768]{1,0:T(8,128)S(1)} %copy.77), channel_id=1, source_target_pairs={{0,1},{1,0},{2,3},{3,2},{4,5},{5,4},{6,7},{7,6},{8,9},{9,8},{10,11... | collective-permute-start | bytes 1916936 | tf_op jit(solution)/shard_map/ppermute | solution.py:330
  604.9 4.2 copy-start.28
  604.9 4.2 copy-start.29
  619.3 2.2 copy-start.18
  620.0 10.1 %copy-start.9 = (f32[480,768]{1,0:T(8,128)S(1)}, f32[480,768]{1,0:T(8,128)}, u32[]{:S(2)}) copy-start(f32[480,768]{1,0:T(8,128)} %param.17) | copy-start | bytes 4423684
  621.5 22.8 %collective-permute-start.7 = (f32[416,768]{1,0:T(8,128)}, f32[416,768]{1,0:T(8,128)}, u32[]{:S(2)}, u32[]{:S(2)}) collective-permute-start(f32[416,768]{1,0:T(8,128)} %copy.80), channel_id=1, source_target_pairs={{0,8},{8,0},{16,24},{24,16},{1,9},{9,1},{17,25},{25,17},{2,10},{10... | collective-permute-start | bytes 3833864 | tf_op jit(solution)/shard_map/ppermute | solution.py:330
  630.1 1.9 copy-start.17
  630.1 11.9 %copy-start.3 = (f32[672,768]{1,0:T(8,128)S(1)}, f32[672,768]{1,0:T(8,128)}, u32[]{:S(2)}) copy-start(f32[672,768]{1,0:T(8,128)} %param.16) | copy-start | bytes 6193156
  649.5 3.5 copy-start.1
  665.2 1.3 copy-start.7
  666.7 2.0 copy-start.8
  666.7 2.2 copy-start.26
  666.8 2.2 copy-start.27
  670.3 42.7 %copy-start.4 = (f32[384,384]{1,0:T(8,128)S(1)}, f32[384,384]{1,0:T(8,128)}, u32[]{:S(2)}) copy-start(f32[384,384]{1,0:T(8,128)} %get-tuple-element.43) | copy-start | bytes 1769476
  670.3 42.7 %copy-start.5 = (f32[384,384]{1,0:T(8,128)S(1)}, f32[384,384]{1,0:T(8,128)}, u32[]{:S(2)}) copy-start(f32[384,384]{1,0:T(8,128)} %get-tuple-element.44) | copy-start | bytes 1769476
  670.3 42.7 %copy-start.6 = (f32[384,384]{1,0:T(8,128)S(1)}, f32[384,384]{1,0:T(8,128)}, u32[]{:S(2)}) copy-start(f32[384,384]{1,0:T(8,128)} %get-tuple-element.51) | copy-start | bytes 1769476
Sparse Core Ops, SparseCore 0:
  11.5 70.3 all-gather.4
  85.4 75.6 all-gather.2
  268.4 111.2 reduce-scatter.4
  385.5 129.3 reduce-scatter.2

commit v2 on v1

v2 whole, which is shorter than its diff:
```python
from functools import partial

import jax
import jax.numpy as jnp
from jax import lax
from jax.experimental import pallas as pl
from jax.experimental.pallas import tpu as pltpu
from jax.sharding import PartitionSpec as P

D = 768
HEADS = 12
HEAD = 64
LEN = 1024
STEP = 10
FIN = 5376
FOUT = 3840
QKV = 3 * D

f32 = jnp.float32
bf16 = jnp.bfloat16
ns_linear = 3.4445
ns_cubic = -4.775
ns_quintic = 2.0315
muon_beta = 0.5
muon_rate = 0.8
muon_decay = 0.1
adam_rate = 0.8
adam_first = 0.9
adam_second = 0.95
adam_eps = 1e-08
norm_eps = 1e-06
penalty = 16384.0
vmem_bytes = 60 * 1024 * 1024
tile_rows = 256
extra_rows = 64
pair = 2 * HEAD


def normalize(values):
    center = values - jnp.mean(values, axis=-1, keepdims=True)
    variance = jnp.mean(center * center, axis=-1, keepdims=True)
    inverse = lax.rsqrt(variance + norm_eps)
    return (center * inverse, inverse)


def norm_backward(grad_scaled, normed, inverse, axis=-1):
    mean_grad = jnp.mean(grad_scaled, axis=axis, keepdims=True)
    mean_cross = jnp.mean(grad_scaled * normed, axis=axis, keepdims=True)
    return inverse * (grad_scaled - mean_grad - normed * mean_cross)


def nn(a, b):
    return jnp.dot(a, b, preferred_element_type=f32)


def contract(a, b, dim_a, dim_b):
    return lax.dot_general(a, b, (((dim_a,), (dim_b,)), ((), ())), preferred_element_type=f32)


def normalize_columns(columns):
    center = columns - jnp.mean(columns, axis=0, keepdims=True)
    variance = jnp.mean(center * center, axis=0, keepdims=True)
    inverse = lax.rsqrt(variance + norm_eps)
    return (center * inverse, inverse)


core_spec = pl.BlockSpec(memory_space=pltpu.SMEM)


def halves(values, core_ref, keep_ref, send_ref):
    half = D // 2
    left, right = values[:, :half], values[:, half:]
    first = core_ref[0] == 0
    keep_ref[...] = jnp.where(first, left, right).reshape(keep_ref.shape)
    send_ref[...] = jnp.where(first, right, left).reshape(send_ref.shape)


def forward_kernel(
    q_ref, k_ref, v_ref, onek_ref, penq_ref, gq_ref, gk_ref, gy_ref, core_ref,
    att_ref, terms_ref, exact_ref, sum_ref, keep_ref, send_ref, kaug, qaug_t, vaug_t,
):
    length = q_ref.shape[0]
    q_t = q_ref[...].T
    k_t = k_ref[...].T
    v_t = v_ref[...].T
    parts = []
    for h in range(2):
        rows = slice(HEAD * h, HEAD * (h + 1))
        q_hat, _ = normalize_columns(q_t[rows].astype(f32))
        k_hat, _ = normalize_columns(k_t[rows].astype(f32))
        q_low = (q_hat * gq_ref[...]).astype(bf16)
        k_low = (k_hat * gk_ref[...]).astype(bf16)
        kaug[h, :, :HEAD] = k_low.T
        kaug[h, :, HEAD:] = onek_ref[...]
        qaug_t[h, :HEAD, :] = (q_low.astype(f32) * HEAD ** (-0.5)).astype(bf16)
        qaug_t[h, HEAD:, :] = penq_ref[...]
        vaug_t[h, :HEAD, :] = v_t[rows]
        vaug_t[h, HEAD:, :] = jnp.ones((16, length), bf16)
        terms_ref[h] = jnp.exp(nn(kaug[h], qaug_t[h])).astype(bf16)
        summed = nn(vaug_t[h], terms_ref[h])
        inverse_sum = 1.0 / summed[HEAD : HEAD + 1]
        sum_ref[0, h : h + 1, :] = inverse_sum
        attended = summed[:HEAD] * inverse_sum
        exact_ref[rows, :] = attended
        parts.append(attended)
    attended = jnp.concatenate(parts, 0).astype(bf16)
    halves(nn(attended, gy_ref[...]).astype(bf16), core_ref, keep_ref, send_ref)
    att_ref[...] = attended.T


def attention_forward(joined, ids, q_gain, k_gain, grad_y, core):
    length = joined.shape[0]
    pairs = D // pair
    image = jnp.where(ids < 0, 4, ids)
    number = jnp.arange(16)
    onek = (image[:, None] == number[None, :]).astype(bf16)
    penq = jnp.where(image[None, :] == number[:, None], 0.0, -penalty).astype(bf16)

    def block(part):
        return pl.BlockSpec((length, pair), lambda p: (0, part * pairs + p))

    def whole(shape):
        return pl.BlockSpec(shape, lambda p: (0, 0))

    return pl.pallas_call(
        forward_kernel,
        grid=(pairs,),
        in_specs=[
            block(0), block(1), block(2),
            whole((length, 16)), whole((16, length)), whole((HEAD, 1)), whole((HEAD, 1)),
            whole((length, D)), core_spec,
        ],
        out_specs=[
            block(0),
            pl.BlockSpec((2, length, length), lambda p: (p, 0, 0)),
            pl.BlockSpec((pair, length), lambda p: (p, 0)),
            pl.BlockSpec((1, 8, length), lambda p: (p, 0, 0)),
            *[pl.BlockSpec((pair, D // 2), lambda p: (p, 0))] * 2,
        ],
        out_shape=[
            jax.ShapeDtypeStruct((length, D), bf16),
            jax.ShapeDtypeStruct((HEADS, length, length), bf16),
            jax.ShapeDtypeStruct((D, length), f32),
            jax.ShapeDtypeStruct((pairs, 8, length), f32),
            *[jax.ShapeDtypeStruct((D, D // 2), bf16)] * 2,
        ],
        scratch_shapes=[
            pltpu.VMEM((2, length, HEAD + 16), bf16),
            pltpu.VMEM((2, HEAD + 16, length), bf16),
            pltpu.VMEM((2, HEAD + 16, length), bf16),
        ],
        compiler_params=pltpu.CompilerParams(vmem_limit_bytes=vmem_bytes),
        cost_estimate=pl.CostEstimate(
            flops=HEADS * 4 * length * length * 256,
            bytes_accessed=16 * length * D + 2 * HEADS * length * length,
            transcendentals=HEADS * length * length,
        ),
        name="attention_forward",
    )(
        joined, joined, joined, onek, penq, q_gain.reshape(HEAD, 1), k_gain.reshape(HEAD, 1), grad_y, core
    )


def backward_kernel(
    q_ref, k_ref, v_ref, do_ref, terms_ref, exact_ref, sum_ref, gq_ref, gk_ref, x_ref, core_ref,
    dq_ref, dk_ref, dv_ref, keep_ref, send_ref, ggq_ref, ggk_ref,
    vaug, qnat, klow_t, doaug_t, donat,
):
    length = q_ref.shape[0]
    step = pl.program_id(0)
    q_t = q_ref[...].T
    k_t = k_ref[...].T
    v_t = v_ref[...].T
    do_t = do_ref[...].T
    q_gain = gq_ref[...]
    k_gain = gk_ref[...]
    dq_parts, dk_parts, dv_parts = [], [], []
    q_gain_grad = jnp.zeros((HEAD, 1), f32)
    k_gain_grad = jnp.zeros((HEAD, 1), f32)
    for h in range(2):
        rows = slice(HEAD * h, HEAD * (h + 1))
        q_hat, q_inverse = normalize_columns(q_t[rows].astype(f32))
        k_hat, k_inverse = normalize_columns(k_t[rows].astype(f32))
        klow_t[h] = (k_hat * k_gain).astype(bf16)
        qnat[h] = (q_hat * q_gain).astype(bf16).T
        vaug[h, :, :HEAD] = v_t[rows].T
        vaug[h, :, HEAD:] = jnp.ones((length, 16), bf16)
        inverse_sum = sum_ref[0, h : h + 1, :]
        do_head = do_t[rows].astype(f32)
        inner = -jnp.sum(do_head * exact_ref[rows, :], axis=0, keepdims=True) * inverse_sum
        do_low = (do_head * inverse_sum).astype(bf16)
        inner_high = inner.astype(bf16).astype(f32)
        extra = lax.broadcasted_iota(jnp.int32, (16, length), 0)
        extra = jnp.where(extra == 0, inner_high, jnp.where(extra == 1, inner - inner_high, 0.0))
        doaug_t[h, :HEAD, :] = do_low
        doaug_t[h, HEAD:, :] = extra.astype(bf16)
        donat[h] = do_low.T
        terms = terms_ref[h]
        dscores = (terms.astype(f32) * nn(vaug[h], doaug_t[h])).astype(bf16)
        dvalue = nn(terms, donat[h])
        dkey = nn(dscores, qnat[h]).T * HEAD ** (-0.5)
        dquery = nn(klow_t[h], dscores) * HEAD ** (-0.5)
        q_gain_grad += jnp.sum(dquery * q_hat, axis=1, keepdims=True)
        k_gain_grad += jnp.sum(dkey * k_hat, axis=1, keepdims=True)
        dq_parts.append(norm_backward(dquery * q_gain, q_hat, q_inverse, 0))
        dk_parts.append(norm_backward(dkey * k_gain, k_hat, k_inverse, 0))
        dv_parts.append(dvalue.T)
    grads = jnp.concatenate(dq_parts + dk_parts + dv_parts, 0).astype(bf16)
    halves(nn(grads, x_ref[...]).astype(bf16), core_ref, keep_ref, send_ref)
    dq_ref[...] = grads[:pair].T
    dk_ref[...] = grads[pair : 2 * pair].T
    dv_ref[...] = grads[2 * pair :].T

    @pl.when(step == 0)
    def _():
        ggq_ref[...] = jnp.zeros_like(ggq_ref)
        ggk_ref[...] = jnp.zeros_like(ggk_ref)

    ggq_ref[...] += jnp.broadcast_to(q_gain_grad, ggq_ref.shape)
    ggk_ref[...] += jnp.broadcast_to(k_gain_grad, ggk_ref.shape)


def attention_backward(joined, dattended, terms, exact, inverse_sum, q_gain, k_gain, x_low, core, first, count):
    length = joined.shape[0]
    pairs = D // pair

    def block(part, offset=first):
        return pl.BlockSpec((length, pair), lambda p: (0, part * pairs + offset + p))

    def whole(shape):
        return pl.BlockSpec(shape, lambda p: (0, 0))

    out = jax.ShapeDtypeStruct((length, count * pair), bf16)
    gain = jax.ShapeDtypeStruct((HEAD, 128), f32)
    outs = pl.pallas_call(
        backward_kernel,
        grid=(count,),
        in_specs=[
            block(0), block(1), block(2), block(0),
            pl.BlockSpec((2, length, length), lambda p: (first + p, 0, 0)),
            pl.BlockSpec((pair, length), lambda p: (first + p, 0)),
            pl.BlockSpec((1, 8, length), lambda p: (first + p, 0, 0)),
            whole((HEAD, 1)), whole((HEAD, 1)), whole((length, D)), core_spec,
        ],
        out_specs=[block(0, 0)] * 3
        + [pl.BlockSpec((3, pair, D // 2), lambda p: (0, p, 0))] * 2
        + [whole((HEAD, 128))] * 2,
        out_shape=[out] * 3 + [jax.ShapeDtypeStruct((3, count * pair, D // 2), bf16)] * 2 + [gain] * 2,
        scratch_shapes=[
            pltpu.VMEM((2, length, HEAD + 16), bf16),
            pltpu.VMEM((2, length, HEAD), bf16),
            pltpu.VMEM((2, HEAD, length), bf16),
            pltpu.VMEM((2, HEAD + 16, length), bf16),
            pltpu.VMEM((2, length, HEAD), bf16),
        ],
        compiler_params=pltpu.CompilerParams(vmem_limit_bytes=vmem_bytes),
        cost_estimate=pl.CostEstimate(
            flops=2 * count * 8 * length * length * 256,
            bytes_accessed=24 * length * count * pair + 4 * count * length * length,
            transcendentals=0,
        ),
        name="attention_backward",
    )(
        joined, joined, joined, dattended, terms, exact, inverse_sum,
        q_gain.reshape(HEAD, 1), k_gain.reshape(HEAD, 1), x_low, core,
    )
    return (outs[:3], outs[3], outs[4], outs[5][:, 0], outs[6][:, 0])


def gelu_pair(u):
    z = jnp.abs(u) * 0.7071067811865476
    t = 1.0 / (1.0 + 0.3275911 * z)
    e = jnp.exp(-z * z)
    poly = t * (0.127414796 + t * (-0.142248368 + t * (0.7107068705 + t * (-0.7265760135 + t * 0.5307027145))))
    half = poly * e
    phi = jnp.where(u >= 0, 1.0 - half, half)
    return (u * phi, phi + u * (0.3989422804014327 * e))


def mlp_kernel(
    x_ref, gy_ref, wu_ref, wd_ref, core_ref, res_ref, gn_ref, keep_up, send_up, keep_down, send_down
):
    @pl.when(pl.program_id(0) == 0)
    def _():
        res_ref[...] = jnp.zeros_like(res_ref)
        gn_ref[...] = jnp.zeros_like(gn_ref)

    x, grad_y, wu, wd = x_ref[...], gy_ref[...], wu_ref[...], wd_ref[...]
    upward = contract(x, wu, 1, 1).astype(bf16).astype(f32)
    grad_hidden = contract(grad_y, wd, 1, 1)
    active, slope = gelu_pair(upward)
    active = active.astype(bf16)
    dupward = (grad_hidden * slope).astype(bf16)
    res_ref[...] += contract(active, wd, 1, 0)
    gn_ref[...] += contract(dupward, wu, 1, 0)
    halves(contract(dupward, x, 0, 0).astype(bf16), core_ref, keep_up, send_up)
    halves(contract(active, grad_y, 0, 0).astype(bf16), core_ref, keep_down, send_down)


def mlp(x_low, grad_y, w_in_all, w_out_all, core):
    length = x_low.shape[0]
    hidden = w_in_all.shape[0] - QKV
    tile = D
    whole = pl.BlockSpec((length, D), lambda t: (0, 0))
    total = jax.ShapeDtypeStruct((length, D), f32)
    grad = jax.ShapeDtypeStruct((hidden, D // 2), bf16)
    return pl.pallas_call(
        mlp_kernel,
        grid=(hidden // tile,),
        in_specs=[
            whole,
            whole,
            pl.BlockSpec((tile, D), lambda t: (t + QKV // tile, 0)),
            pl.BlockSpec((tile, D), lambda t: (t + D // tile, 0)),
            core_spec,
        ],
        out_specs=[whole, whole] + [pl.BlockSpec((tile, D // 2), lambda t: (t, 0))] * 4,
        out_shape=[total, total] + [grad] * 4,
        compiler_params=pltpu.CompilerParams(vmem_limit_bytes=vmem_bytes),
        cost_estimate=pl.CostEstimate(
            flops=18 * length * D * hidden,
            bytes_accessed=12 * length * D + 8 * hidden * D,
            transcendentals=length * hidden,
        ),
        name="mlp",
    )(x_low, grad_y, w_in_all, w_out_all, core)


def split(values):
    high = values.astype(bf16)
    return (high, (values - high.astype(f32)).astype(bf16))


def newton_kernel(g_ref, x_ref, *refs, sweeps, opening, closing, rate):
    if closing:
        w_ref, o_ref, gh, gl, sh, sl, ph, pw, g32, x32 = refs
    else:
        g32, x32, gh, gl, sh, sl, ph, pw = refs
    count = D // tile_rows

    def span(i):
        return slice(i * tile_rows, (i + 1) * tile_rows)

    def store(high_ref, low_ref, i, j, value):
        high_ref[span(i), span(j)], low_ref[span(i), span(j)] = split(value)
        if i != j:
            high_ref[span(j), span(i)], low_ref[span(j), span(i)] = split(value.T)

    def symmetric(ah, al, bh, bl, post):
        for i in range(count):
            for j in range(i, count):
                rows, columns = span(i), span(j)
                post(
                    i,
                    j,
                    nn(ah[rows, :], bh[:, columns])
                    + (nn(ah[rows, :], bl[:, columns]) + nn(al[rows, :], bh[:, columns])),
                )

    def sweep(last):
        def keep_factor(i, j, value):
            value = ns_cubic * g32[span(i), span(j)] + ns_quintic * value
            if i == j:
                shape = (tile_rows, tile_rows)
                diagonal = lax.broadcasted_iota(jnp.int32, shape, 0) == lax.broadcasted_iota(jnp.int32, shape, 1)
                value = value + jnp.where(diagonal, ns_linear, 0.0)
            store(ph, pw, i, j, value)

        def keep_gram(i, j, value):
            g32[span(i), span(j)] = value
            if i != j:
                g32[span(j), span(i)] = value.T
            store(gh, gl, i, j, value)

        symmetric(gh, gl, gh, gl, keep_factor)
        xh, xl = split(x32[...])
        x32[...] = nn(xh, ph[...]) + (nn(xh, pw[...]) + nn(xl, ph[...]))
        if not last:
            symmetric(gh, gl, ph, pw, partial(store, sh, sl))
            symmetric(sh, sl, ph, pw, keep_gram)

    if opening:
        half = D // 2
        corner, side = g_ref[:half, :half], g_ref[:half, half:]
        i = lax.broadcasted_iota(jnp.int32, (half, half), 0)
        j = lax.broadcasted_iota(jnp.int32, (half, half), 1)
        corner_t = corner.T
        first = jnp.where(i <= j, corner, corner_t)
        last = jnp.where(i > j, corner, jnp.where(i == j, g_ref[half : half + 1, :half], corner_t))
        trace = jnp.sum(jnp.where(i == j, first + last, 0.0), axis=0, keepdims=True)
        trace = jnp.sum(trace, axis=1, keepdims=True)
        inverse = 1.0 / (jnp.sqrt(trace) + 1e-07)
        square = inverse * inverse
        g32[:half, :half] = first * square
        g32[half:, half:] = last * square
        g32[:half, half:] = side * square
        g32[half:, :half] = side.T * square
        x32[...] = x_ref[...] * inverse
    else:
        g32[...] = g_ref[...]
        x32[...] = x_ref[...]
    gh[...], gl[...] = split(g32[...])
    plain = sweeps - 1 if closing else sweeps
    if plain > 1:
        pl.loop(0, plain)(lambda k: sweep(False))
    elif plain == 1:
        sweep(False)
    if closing:
        sweep(True)
        o_ref[...] = w_ref[...].astype(f32) * (1 - muon_rate * muon_decay) - rate * x32[...]


def newton(gram, momentum, sweeps, opening=False, weights=None, rate=None):
    rows = momentum.shape[0]
    whole = pl.BlockSpec(memory_space=pltpu.VMEM)
    state = [pltpu.VMEM((D, D), f32), pltpu.VMEM((rows, D), f32)]
    parts = [pltpu.VMEM((D, D), bf16)] * 6
    closing = weights is not None
    moved = jax.ShapeDtypeStruct((rows, D), f32)
    return pl.pallas_call(
        partial(newton_kernel, sweeps=sweeps, opening=opening, closing=closing, rate=rate),
        in_specs=[whole] * (3 if closing else 2),
        out_specs=whole if closing else [whole] * 2,
        out_shape=moved if closing else [jax.ShapeDtypeStruct((D, D), f32), moved],
        scratch_shapes=parts + state if closing else parts,
        compiler_params=pltpu.CompilerParams(vmem_limit_bytes=vmem_bytes),
        cost_estimate=pl.CostEstimate(
            flops=6 * D * D * (2 * D + rows) * sweeps, bytes_accessed=8 * D * D + 10 * rows * D, transcendentals=0
        ),
        name="newton",
    )(gram, momentum, *([weights] if closing else []))


def gram_kernel(m_ref, extra_ref, core_ref, o_ref):
    half = D // 2
    left, right = slice(0, half), slice(half, D)

    def product(a, b):
        ah, al = split(m_ref[:, a])
        bh, bl = split(m_ref[:, b])
        return contract(ah, bh, 0, 0) + (contract(ah, bl, 0, 0) + contract(al, bh, 0, 0))

    o_ref[half:, :] = extra_ref[...]

    @pl.when(core_ref[0] == 0)
    def _():
        i = lax.broadcasted_iota(jnp.int32, (half, half), 0)
        j = lax.broadcasted_iota(jnp.int32, (half, half), 1)
        last = product(right, right)
        o_ref[:half, :] = jnp.where(i <= j, product(left, left), last)
        o_ref[half : half + 1, :] = jnp.sum(jnp.where(i == j, last, 0.0), axis=0, keepdims=True)

    @pl.when(core_ref[0] != 0)
    def _():
        o_ref[:half, :] = product(left, right)


def folded_gram(rows, extra, core):
    rows = jnp.pad(rows, ((0, -rows.shape[0] % 16), (0, 0)))
    whole = pl.BlockSpec(memory_space=pltpu.VMEM)
    return pl.pallas_call(
        gram_kernel,
        in_specs=[whole, whole, core_spec],
        out_specs=whole,
        out_shape=jax.ShapeDtypeStruct((D // 2 + extra_rows, D // 2), f32),
        compiler_params=pltpu.CompilerParams(vmem_limit_bytes=vmem_bytes),
        cost_estimate=pl.CostEstimate(
            flops=4 * rows.shape[0] * D * D, bytes_accessed=8 * rows.shape[0] * D, transcendentals=0
        ),
        name="gram",
    )(rows, extra, core)


def swap(values, axis, bit):
    size = lax.axis_size(axis)
    return lax.ppermute(values, axis, [(i, i ^ bit) for i in range(size)])


def bits(size):
    return [1 << b for b in range(size.bit_length() - 1)]


def take(values, index, axis):
    return lax.dynamic_index_in_dim(values, index, axis, keepdims=False)


def after(value, *others):
    return lax.optimization_barrier((value, *others))[0]


def exchange(values, axis, bit, fill=()):
    return after(swap(values, axis, bit), *fill)


def sum_over(values, halving, full, fills=()):
    fills = list(fills)

    def step(sent, axis, bit):
        fill = fills.pop(0)(sent) if fills else ()
        return exchange(sent, axis, bit, fill)

    sides = []
    for axis, bit in halving:
        side = (lax.axis_index(axis) // bit) % 2
        pieces = values.reshape(2, values.shape[0] // 2, values.shape[1])
        values = take(pieces, side, 0) + step(take(pieces, 1 - side, 0), axis, bit)
        sides.append(side)
    for axis, bit in full:
        values = values + step(values, axis, bit)
    for (axis, bit), side in zip(reversed(halving), reversed(sides), strict=True):
        values = join(values, step(values, axis, bit), side, 0).reshape(-1, values.shape[1])
    return join(values, step(values, "nar", 1), lax.axis_index("nar") % 2, 1).reshape(values.shape[0], -1)


def halve(values, axis, name, bit, fill):
    side = (lax.axis_index(name) // bit) % 2
    other = exchange(take(values, 1 - side, axis), name, bit, fill)
    return (take(values, side, axis).astype(f32) + other.astype(f32)).astype(bf16)


def scatter_stages(values):
    wide = lax.axis_size("wide")
    far = wide // 2
    rows, columns = values.shape[0] // (2 * wide), values.shape[1]
    cut = rows // 32 * 16
    place = lax.axis_index("wide") // 2
    values = values.reshape(far, 2, 2, rows, columns)

    def one(*fill):
        return (
            halve(values[:, :, :, :cut], 1, "wide", 1, fill),
            halve(values[:, :, :, cut:], 2, "nar", 2, fill),
        )

    def two(held, *fill):
        return jnp.concatenate(
            [halve(held[0], 1, "nar", 2, fill), halve(held[1], 1, "wide", 1, fill)], axis=1
        )

    def rest(held, *fill):
        total = take(held, place, 0).astype(f32)
        for shift in range(1, far):
            pairs = [(i, (i // 2 + shift) % far * 2 + i % 2) for i in range(wide)]
            sent = take(held, (place + shift) % far, 0)
            total = total + after(lax.ppermute(sent, "wide", pairs), *fill).astype(f32)
        return total.astype(bf16)

    return one, two, rest


def both_cores(values):
    other = swap(values, "nar", 1)
    return join(values, other, lax.axis_index("nar") % 2, 1).reshape(values.shape[0], D)


def both_chips(values):
    return join(values, swap(values, "nar", 2), lax.axis_index("nar") // 2, 0).reshape(-1, D)


def join(values, other, side, axis):
    ordered = [jnp.where(side == 0, values, other), jnp.where(side == 0, other, values)]
    return jnp.stack(ordered, axis)


def gather(values):
    wide = lax.axis_size("wide")
    rows = values.shape[0]
    far = wide // 2
    place, side = lax.axis_index("wide") // 2, lax.axis_index("wide") % 2
    chip, core = lax.axis_index("nar") // 2, lax.axis_index("nar") % 2
    held = lax.dynamic_update_index_in_dim(jnp.zeros((far, rows, D), values.dtype), values, place, 0)
    for shift in range(1, far):
        pairs = [(i, (i // 2 + shift) % far * 2 + i % 2) for i in range(wide)]
        held = lax.dynamic_update_index_in_dim(
            held, lax.ppermute(values, "wide", pairs), (place - shift) % far, 0
        )
    cut = rows // 32 * 16
    first, second = held[:, :cut], held[:, cut:]
    first = join(first, swap(first, "wide", 1), side, 1)
    second = join(second, swap(second, "nar", 2), chip, 1)
    first = join(first, swap(first, "nar", 2), chip, 2)
    second = join(second, swap(second, "wide", 1), side, 1)
    held = jnp.concatenate([first, second], axis=3)
    return join(held, swap(held, "nar", 1), core, 3).reshape(-1, D)


def on_device(tokens, cotangent, image_ids, w_in, w_out, gains, mom_in, mom_out, gain_m, gain_v):
    row_count = tokens.shape[0]
    rows_in = w_in.shape[0]
    rows_out = w_out.shape[0]
    nar_count = lax.axis_size("nar")
    wide_count = lax.axis_size("wide")
    nar_place = lax.axis_index("nar")
    share_in = rows_in // nar_count
    share_out = rows_out // nar_count
    everyone = ("wide", "nar")

    def share(rows, size):
        return lax.dynamic_slice_in_dim(rows, nar_place * size, size, 0)

    w_in_all = lax.all_gather(share(w_in, share_in), everyone, axis=0, tiled=True)
    w_out_all = gather(share(w_out, share_out))

    x_float = tokens.astype(f32)
    ln_gain = gains[:D]
    x_hat, x_inverse = normalize(x_float)
    x_low = (x_hat * ln_gain).astype(bf16)
    live = (image_ids.reshape(row_count) >= 0)[:, None]
    grad_y = jnp.where(live, cotangent, jnp.zeros_like(cotangent))

    core = (nar_place % 2).reshape(1)
    chip = nar_place // 2
    w_qkv = w_in_all[:QKV]
    w_att = w_out_all[:D]
    joined = contract(x_low, w_qkv, 1, 1).astype(bf16)
    dattended = contract(grad_y, w_att, 1, 1).astype(bf16)
    q_gain, k_gain = gains[D : D + HEAD], gains[D + HEAD :]
    attended, terms, exact, inverse_sum, keep_att, send_att = attention_forward(
        joined, image_ids.reshape(row_count), q_gain, k_gain, grad_y, core
    )
    mlp_result, mlp_normed, keep_up, send_up, keep_down, send_down = mlp(
        after(x_low, keep_att), grad_y, w_in_all, w_out_all, core
    )

    def backward(begin, count, *earlier):
        return attention_backward(
            joined, dattended, terms, exact, inverse_sum, q_gain, k_gain, after(x_low, *earlier), core, begin, count
        )

    def cores(keep, send, *fill):
        other = exchange(send, "nar", 1, fill)
        return (keep.astype(f32) + other.astype(f32)).astype(bf16).reshape(-1, D // 2)

    pairs = D // pair
    first = rows_in * 4 // 7
    second = rows_in - first
    parted = wide_count == 8 and first == D // 2 and rows_in == 672
    start = 96 * jnp.minimum(lax.axis_index("wide"), 3)
    row = lax.broadcasted_iota(jnp.int32, (rows_in, 1), 0)
    hidden = keep_up.shape[0]
    if parted:
        grads_a, keep_a, send_a, q_grad_a, k_grad_a = backward(0, pairs // 2, keep_up)
        up = cores(keep_up, send_up, keep_a)
        out = jnp.concatenate([cores(keep_att, send_att, keep_a), cores(keep_down, send_down, keep_a)], axis=0)
        out_one, out_two, out_rest = scatter_stages(out)
        grads_b, keep_b, send_b, q_grad_b, k_grad_b = backward(pairs // 2, pairs // 2, keep_a, out)
        held_a = cores(keep_a, send_a, keep_b)
        held_a = [held_a, up[:first]] + [up[rows_in * i : rows_in * i + first] for i in range(1, 5)]
        a_one, a_two, a_rest = scatter_stages(jnp.concatenate(held_a, axis=0))
        held_out = out_one(keep_b)
        held_b = cores(keep_b, send_b)
        held_b = [held_b] + [up[rows_in * i + first : rows_in * (i + 1)] for i in range(4)]
        b_one, b_two, b_rest = scatter_stages(jnp.concatenate(held_b, axis=0))
        held_out = out_two(held_out)
        held_a = a_one()
        part_out = out_rest(held_out)
        part_a = a_rest(a_two(held_a))
        part_b = b_rest(b_two(b_one()))
        q_gain_grad, k_gain_grad = q_grad_a + q_grad_b, k_grad_a + k_grad_b
        grad_qkv = [a for pieces in zip(grads_a, grads_b, strict=True) for a in pieces]
        part_in = jnp.concatenate([part_a, part_b], axis=0)

        def halved(rows):
            inside = lax.dynamic_slice_in_dim(rows, start, first, 0)
            others = jnp.where(row[:second] < start, rows[:second], rows[first:])
            return jnp.concatenate(
                [
                    lax.dynamic_slice_in_dim(inside, chip * (first // 2), first // 2, 0),
                    lax.dynamic_slice_in_dim(others, chip * (second // 2), second // 2, 0),
                ],
                axis=0,
            )

        def rejoined(rows):
            a, b = both_chips(rows[: first // 2]), both_chips(rows[first // 2 :])
            a = lax.dynamic_update_slice_in_dim(jnp.zeros((rows_in, D), a.dtype), a, start, 0)
            empty = jnp.zeros((first, D), b.dtype)
            below = jnp.concatenate([b, empty], axis=0)
            above = jnp.concatenate([empty, b], axis=0)
            inside = (row >= start) & (row < start + first)
            return jnp.where(inside, a, jnp.where(row < start, below, above))

    else:
        grad_qkv, keep_a, send_a, q_gain_grad, k_gain_grad = backward(0, pairs, keep_up)
        out = jnp.concatenate([cores(keep_att, send_att), cores(keep_down, send_down)], axis=0)
        out_one, out_two, out_rest = scatter_stages(out)
        part_out = out_rest(out_two(out_one()))
        both = jnp.concatenate([cores(keep_a, send_a), cores(keep_up, send_up)], axis=0)
        in_one, in_two, in_rest = scatter_stages(both)
        part_in = in_rest(in_two(in_one()))

        def halved(rows):
            return lax.dynamic_slice_in_dim(rows, chip * (rows_in // 2), rows_in // 2, 0)

        rejoined = both_chips

    grad_qkv = jnp.concatenate(grad_qkv, axis=1)
    result = (x_float + (mlp_result + nn(attended, w_att))).astype(bf16)
    grad_normed = mlp_normed + nn(grad_qkv, w_qkv)
    ln_grad = jnp.sum(grad_normed * x_hat, axis=0)
    grad_tokens = (
        grad_y.astype(f32) + norm_backward(grad_normed * ln_gain, x_hat, x_inverse)
    ).astype(bf16)

    wide_bits = bits(wide_count)
    halving = [("wide", wide_bits[0]), ("nar", 2)]
    full = [("wide", bit) for bit in wide_bits[1:]]
    gain_terms = jnp.concatenate([ln_grad, q_gain_grad, k_gain_grad])
    count = gain_terms.shape[0]
    half = D // 2
    extra = jnp.pad(gain_terms, (half, (extra_rows - 1) * half - count)).reshape(extra_rows, half)

    part_out = both_cores(part_out)
    half_out = lax.dynamic_slice_in_dim(mom_out, chip * (rows_out // 2), rows_out // 2, 0)
    folded_out = sum_over(
        folded_gram(muon_beta * half_out + part_out.astype(f32), jnp.zeros_like(extra), core), halving, full
    )
    grad_w_out = both_chips(part_out).astype(f32)
    mom_out_new = muon_beta * mom_out + grad_w_out

    part_in = both_cores(part_in)
    state = [folded_out, mom_out_new]

    def sweeps_out(opening):
        def fill(sent):
            state[:] = newton(after(state[0], sent), state[1], 1, opening=opening)
            return (state[1],)

        return fill

    folded_in = sum_over(
        folded_gram(muon_beta * halved(mom_in) + part_in.astype(f32), extra, core),
        halving,
        full,
        [sweeps_out(i == 0) for i in range(4)],
    )
    grad_w_in = rejoined(part_in).astype(f32)
    mom_in_new = muon_beta * mom_in + grad_w_in
    extra = (folded_in[half:, :half] + folded_in[half:, half:]).reshape(extra_rows * half)
    grad_gains = extra[half : half + count]
    w_out_new = newton(*state, 1, weights=w_out, rate=muon_rate * (FOUT / D) ** 0.5)
    w_in_new = newton(
        folded_in, mom_in_new, 5, opening=True, weights=w_in, rate=muon_rate * (FIN / D) ** 0.5
    )
    gain_m_new = adam_first * gain_m + (1 - adam_first) * grad_gains
    gain_v_new = adam_second * gain_v + (1 - adam_second) * grad_gains * grad_gains
    gains_new = gains - adam_rate * (gain_m_new / (1 - adam_first**STEP)) / (
        jnp.sqrt(gain_v_new / (1 - adam_second**STEP)) + adam_eps
    )
    return (
        result,
        grad_tokens,
        grad_w_in,
        grad_w_out,
        grad_gains,
        mom_in_new,
        mom_out_new,
        gain_m_new,
        gain_v_new,
        w_in_new,
        w_out_new,
        gains_new,
    )


def solution(mesh):
    rows = P(("nar", "wide"), None)
    wide = P("wide", None)
    return jax.shard_map(
        on_device,
        mesh=mesh,
        in_specs=(rows, rows, rows, wide, wide, P(), wide, wide, P(), P()),
        out_specs=(rows, rows, wide, wide, P(), wide, wide, P(), P(), wide, wide, P()),
        check_vma=False,
    )
```

time: 764 us -> 499 us (0.65)
  waiting for transfers between devices: 410 us -> 108 us
  starting transfers between devices: 9.45 us -> 69.4 us
  Pallas kernels: 167 us -> 204 us
  blocking collectives: 18.6 us -> 0 us
  matrix products: 41.2 us -> 23.1 us
  local copies, waits for them, and re-layouts: 47.6 us -> 32.5 us
  other arithmetic: 51.5 us -> 38.9 us
    reduce_scatter x2 -> x0, waiting for transfers between devices: 214 us -> none  [the longest x1 132 us: on_device(): lax.psum_scatter(grad_in_local, everyone, scatter_dimension=0, tiled=True)]
    all_gather x1 -> x0, waiting for transfers between devices: 62.9 us -> none  [on_device(): lax.all_gather(share(w_out, share_out), everyone, axis=0, tiled=True)]
    all_gather x1, waiting for transfers between devices: 70.4 us -> 16.9 us  [on_device(): lax.all_gather(share(w_in, share_in), everyone, axis=0, tiled=True)]
    pallas_call x3 -> x11, Pallas kernels: 126 us -> 164 us  [the longest x6 94.2 us: newton(): pl.pallas_call(partial(newton_kernel, sweeps=sweeps, opening=opening, clo...]
    ppermute x8 -> x41, starting transfers between devices: 9.29 us -> 46.2 us  [swap(): return lax.ppermute(values, axis, [(i, i ^ bit) for i in range(size)])]
    ppermute x0 -> x12, waiting for transfers between devices: none -> 23.7 us  [the longest x3 12.6 us: gather(): lax.ppermute(values, 'wide', pairs)]
    ppermute x0 -> x12, starting transfers between devices: none -> 23.1 us  [the longest x9 16.1 us: rest(): total = total + after(lax.ppermute(sent, 'wide', pairs), *fill).astype(f32)]
    all_gather x2 -> x0, blocking collectives: 18.6 us -> none  [the longest x1 10 us: on_device(): grad_w_in = lax.all_gather(part_in, 'nar', axis=0, tiled=True).astype(f32)]
  transfers between devices with their start and end apart: 12 -> 54, of which waited for: 11 -> 21; matrix products, arithmetic and copies ran while one was open for 8% -> 16% of each run, Pallas kernels for 0% -> 21%
where the time goes in v2:
time: 499 us; the launch traced here: 492 us
  Pallas kernels  204 us (41%)
  waiting for transfers between devices  108 us (22%)
  starting transfers between devices  69.4 us (14%)
  other arithmetic  38.9 us (8%)
  local copies, waits for them, and re-layouts  32.5 us (7%)
  matrix products  23.1 us (5%)
  between operations  15.8 us (3%)
    pallas_call x6, Pallas kernels, newton(): pl.pallas_call(partial(newton_kernel, sweeps=sweeps, opening=opening, clo...  94.2 us
    ppermute x41, waiting for transfers between devices, swap(): return lax.ppermute(values, axis, [(i, i ^ bit) for i in range(size)])  67.7 us
    ppermute x41, starting transfers between devices, swap(): return lax.ppermute(values, axis, [(i, i ^ bit) for i in range(size)])  46.2 us
    pallas_call x2, Pallas kernels, attention_backward(): pl.pallas_call(backward_kernel, grid=(count,), in_specs=[block(0), block(...  43.3 us
    pallas_call x1, Pallas kernels, mlp(): pl.pallas_call(mlp_kernel, grid=(hidden // tile,), in_specs=[whole, whole...  40.3 us
    pallas_call x1, Pallas kernels, attention_forward(): pl.pallas_call(forward_kernel, grid=(pairs,), in_specs=[block(0), block(1...  19.5 us
    all_gather x1, waiting for transfers between devices, on_device(): lax.all_gather(share(w_in, share_in), everyone, axis=0, tiled=True)  16.9 us
    ppermute x9, starting transfers between devices, rest(): total = total + after(lax.ppermute(sent, 'wide', pairs), *fill).astype(f32)  16.1 us
  transfers between devices with their start and end apart: 54, of which 21 were waited for; matrix products, arithmetic and copies ran while one was open for 16% of the time, Pallas kernels for 21%

profile of v2, /device:TPU:0, one launch (start us, length us, event | category | flops | bytes accessed | tf_op | source)
XLA Modules:
  0.0 491.8 jit_solution(15360912736406104373)
XLA Ops:
  10.0 3.1 collective-permute-start
  13.0 2.6 collective-permute-start.1
  17.0 3.7 collective-permute-done
  20.6 8.9 %collective-permute-done.1 = bf16[120,768]{1,0:T(8,128)(2,1)S(1)} collective-permute-done((bf16[120,768]{1,0:T(8,128)(2,1)S(1)}, bf16[120,768]{1,0:T(8,128)(2,1)S(1)}, u32[]{:S(2)}, u32[]{:S(2)}) %collective-permute-start.1) | collective-permute-done | bytes 184352 | tf_op jit(solution)/shard_map/ppermute | solution.py:575
  32.8 5.5 %collective-permute-done.3 = bf16[4,48,768]{2,1,0:T(8,128)(2,1)S(1)} collective-permute-done((bf16[4,48,768]{2,1,0:T(8,128)(2,1)S(1)}, bf16[4,48,768]{2,1,0:T(8,128)(2,1)S(1)}, u32[]{:S(2)}, u32[]{:S(2)}) %collective-permute-start.3) | collective-permute-done | bytes 294944 | tf_op jit(solution)/shard_map/ppermute | solution.py:476
  38.4 4.7 collective-permute-done.5
  45.2 19.2 %collective-permute-done.4 = bf16[4,2,48,768]{3,2,0,1:T(8,128)(2,1)S(1)} collective-permute-done((bf16[4,2,48,768]{3,2,0,1:T(8,128)(2,1)S(1)}, bf16[4,2,48,768]{3,2,0,1:T(8,128)(2,1)S(1)}, u32[]{:S(2)}, u32[]{:S(2)}) %collective-permute-start.4) | collective-permute-done | bytes 589856 | tf_op jit(solution)/shard_map/ppermute | solution.py:476
  64.6 2.5 collective-permute-done.6
  77.4 2.5 select_bitcast_fusion.1
  79.9 3.0 pad_maximum_fusion
  82.8 16.9 %all-gather.2.cloned.1.call-done.wu_ref = bf16[5376,768]{1,0:T(8,128)(2,1)} async-done(((bf16[168,768]{1,0:T(8,128)(2,1)}), bf16[5376,768]{1,0:T(8,128)(2,1)}) %all-gather.2.cloned.1.call-update) | async-done | bytes 8257552 | tf_op jit(solution)/shard_map/all_gather | solution.py:601
  99.8 7.4 %convolution_convert_fusion.q_ref.k_ref.v_ref = bf16[1024,2304]{1,0:T(8,128)(2,1)} fusion(bf16[1024,768]{1,0:T(8,128)(2,1)S(1)} %copy-done.21, bf16[5376,768]{1,0:T(8,128)(2,1)} %all-gather.2.cloned.1.call-done.wu_ref), kind=kOutput, calls=%fused_computation.1 | convolution fusion | flops 3626237952 | bytes 9830400 | tf_op jit(solution)/shard_map/dot_general | solution.py:57
  107.2 19.5 %attention_forward.1 = (bf16[1024,768]{1,0:T(8,128)(2,1)}, bf16[12,1024,1024]{2,1,0:T(8,128)(2,1)}, f32[768,1024]{1,0:T(8,128)}, f32[6,8,1024]{2,1,0:T(8,128)}, ...) custom-call(bf16[1024,2304]{1,0:T(8,128)(2,1)} %convolution_convert_fusion.q_ref.k_ref.v_ref, ...), custom_call_target="tpu_custom_call" | custom-call | flops 12884901888 | bytes 37748736 | tf_op jit(solution)/shard_map/attention_forward/pallas_call | solution.py:125
  126.7 40.3 %mlp.1 = (f32[1024,768]{1,0:T(8,128)}, f32[1024,768]{1,0:T(8,128)}, bf16[3072,384]{1,0:T(8,128)(2,1)}, bf16[3072,384]{1,0:T(8,128)(2,1)}, bf16[3072,384]{1,0:T(8,128)(2,1)}, /*index=5*/bf16[3072,384]{1,0:T(8,128)(2,1)}) custom-call(bf16[1024,768]{1,0:T(8,128)(2,1)} %fusion.6.x_ref, bf16[1024,768]{1,0:T(8,128)(2,1)} %broadcast_select_fusion.gy_ref, ...), custom_call_target="tpu_custom_call" | custom-call | flops 43486543872 | bytes 28311552 | tf_op jit(solution)/shard_map/mlp/pallas_call | solution.py:307
  167.9 2.1 constant_dynamic-slice_fusion
  170.9 3.9 convolution_convert_fusion.1.do_ref
  175.1 21.8 %attention_backward.2 = (bf16[1024,384]{1,0:T(8,128)(2,1)}, bf16[1024,384]{1,0:T(8,128)(2,1)}, bf16[1024,384]{1,0:T(8,128)(2,1)}, bf16[3,384,384]{2,1,0:T(8,128)...) custom-call(bf16[1024,2304]{1,0:T(8,128)(2,1)} %convolution_convert_fusion.q_ref.k_ref.v_ref, ...), custom_call_target="tpu_custom_call" | custom-call | flops 12884901888 | bytes 22020096 | tf_op jit(solution)/shard_map/attention_backward/pallas_call | solution.py:235
  197.5 2.3 constant_dynamic-update-slice_fusion.5
  200.0 2.3 add_convert_fusion.1
  208.5 21.5 %attention_backward.3 = (bf16[1024,384]{1,0:T(8,128)(2,1)}, bf16[1024,384]{1,0:T(8,128)(2,1)}, bf16[1024,384]{1,0:T(8,128)(2,1)}, bf16[3,384,384]{2,1,0:T(8,128)...) custom-call(bf16[1024,2304]{1,0:T(8,128)(2,1)} %convolution_convert_fusion.q_ref.k_ref.v_ref, ...), custom_call_target="tpu_custom_call" | custom-call | flops 12884901888 | bytes 22020096 | tf_op jit(solution)/shard_map/attention_backward/pallas_call | solution.py:235
  232.0 2.3 add_convert_fusion
  242.7 6.6 %fusion.12 = (f32[768]{0:T(1024)S(1)}, f32[1024]{0:T(1024)S(1)}, f32[1024]{0:T(1024)S(1)}, f32[1024,768]{1,0:T(8,128)S(1)}) fusion(bf16[1024,768]{1,0:T(8,128)(2,1)S(1)} %copy-done, f32[1024]{0:T(1024)S(1)} %add_rsqrt_fusion, f32[1024]{0:T(1024)S(1)} %broadcast_multiply_fusion.2, f32[768]{0:T(1024)S(1)} %bitcast.300, f32[1024,768]{1,0:T(8,128)S(1)} %copy-done.44, ...), kind=kOutput, calls=%fused_computation.19 | convolution fusion | flops 3631740160 | bytes 16144384 | tf_op jit(solution)/shard_map/dot_general | solution.py:53
  249.4 5.1 %fusion.11 = (bf16[1024,768]{1,0:T(8,128)(2,1)}, bf16[1024,768]{1,0:T(8,128)(2,1)}) fusion(bf16[1024,768]{1,0:T(8,128)(2,1)S(1)} %copy-done, bf16[1024,768]{1,0:T(8,128)(2,1)S(1)} %copy-done.20, f32[1024,768]{1,0:T(8,128)S(1)} %get-tuple-element.125, f32[1024]{0:T(1024)S(1)} %get-tuple-element.189, f32[1024]{0:T(1024)S(1)} %get-tuple-element.190, ...), kind=kOutput, calls=%fused_computation.18 | convolution fusion | flops 1218969600 | bytes 15354880 | tf_op jit(solution)/shard_map/dot_general | solution.py:53
  266.3 2.4 collective-permute-done.13
  280.5 2.1 collective-permute-start.22
  282.8 2.8 collective-permute-start.34
  292.0 6.2 %collective-permute-done.35 = bf16[240,384]{1,0:T(8,128)(2,1)S(1)} collective-permute-done((bf16[240,384]{1,0:T(8,128)(2,1)S(1)}, bf16[240,384]{1,0:T(8,128)(2,1)S(1)}, u32[]{:S(2)}, u32[]{:S(2)}) %collective-permute-start.35) | collective-permute-done | bytes 184352 | tf_op jit(solution)/shard_map/ppermute | solution.py:545
  302.3 2.8 gram.3
  307.4 4.5 collective-permute-start.24
  311.9 2.5 collective-permute-start.25
  318.4 3.2 collective-permute-done.25
  323.6 4.4 collective-permute-start.42
  328.2 3.2 collective-permute-done.42
  331.4 3.9 collective-permute-start.43
  335.5 5.1 %collective-permute-done.43 = f32[112,384]{1,0:T(8,128)S(1)} collective-permute-done((f32[112,384]{1,0:T(8,128)S(1)}, f32[112,384]{1,0:T(8,128)S(1)}, u32[]{:S(2)}, u32[]{:S(2)}) %collective-permute-start.43) | collective-permute-done | bytes 172064 | tf_op jit(solution)/shard_map/ppermute | solution.py:476
  344.1 2.1 collective-permute-done.44
  346.5 6.9 %collective-permute-done.45 = f32[224,384]{1,0:T(8,128)S(1)} collective-permute-done((f32[224,384]{1,0:T(8,128)S(1)}, f32[224,384]{1,0:T(8,128)S(1)}, u32[]{:S(2)}, u32[]{:S(2)}) %collective-permute-start.45) | collective-permute-done | bytes 344096 | tf_op jit(solution)/shard_map/ppermute | solution.py:476
  354.8 3.8 gram.2
  363.4 11.2 %newton.6 = (f32[768,768]{1,0:T(8,128)}, f32[480,768]{1,0:T(8,128)}) custom-call(f32[448,768]{1,0:T(8,128)} %bitcast.282, f32[480,768]{1,0:T(8,128)} %get-tuple-element.123.x_ref), custom_call_target="tpu_custom_call" | custom-call | flops 7134511104 | bytes 8404992 | tf_op jit(solution)/shard_map/newton/pallas_call | solution.py:420
  376.1 11.2 %newton.7 = (f32[768,768]{1,0:T(8,128)}, f32[480,768]{1,0:T(8,128)}) custom-call(f32[768,768]{1,0:T(8,128)} %get-tuple-element.102.g_ref, f32[480,768]{1,0:T(8,128)} %get-tuple-element.99.x_ref), custom_call_target="tpu_custom_call" | custom-call | flops 7134511104 | bytes 8404992 | tf_op jit(solution)/shard_map/newton/pallas_call | solution.py:420
  389.3 11.0 %newton.8 = (f32[768,768]{1,0:T(8,128)}, f32[480,768]{1,0:T(8,128)}) custom-call(f32[768,768]{1,0:T(8,128)} %get-tuple-element.106.g_ref, f32[480,768]{1,0:T(8,128)} %get-tuple-element.103.x_ref), custom_call_target="tpu_custom_call" | custom-call | flops 7134511104 | bytes 8404992 | tf_op jit(solution)/shard_map/newton/pallas_call | solution.py:420
  400.3 3.4 collective-permute-start.49
  403.8 11.2 %newton.9 = (f32[768,768]{1,0:T(8,128)}, f32[480,768]{1,0:T(8,128)}) custom-call(f32[768,768]{1,0:T(8,128)} %get-tuple-element.110.g_ref, f32[480,768]{1,0:T(8,128)} %get-tuple-element.107.x_ref), custom_call_target="tpu_custom_call" | custom-call | flops 7134511104 | bytes 8404992 | tf_op jit(solution)/shard_map/newton/pallas_call | solution.py:420
  415.7 4.8 collective-permute-done.50
  422.0 5.9 %collective-permute-done.51 = f32[224,384]{1,0:T(8,128)S(1)} collective-permute-done((f32[224,384]{1,0:T(8,128)S(1)}, f32[224,384]{1,0:T(8,128)S(1)}, u32[]{:S(2)}, u32[]{:S(2)}) %collective-permute-start.51) | collective-permute-done | bytes 344096 | tf_op jit(solution)/shard_map/ppermute | solution.py:476
  428.1 2.5 multiply_add_fusion
  430.6 7.3 %newton.11 = f32[480,768]{1,0:T(8,128)} custom-call(f32[768,768]{1,0:T(8,128)} %get-tuple-element.113.g_ref, f32[480,768]{1,0:T(8,128)} %get-tuple-element.111.x_ref, bf16[480,768]{1,0:T(8,128)(2,1)} %refs_0_.3), custom_call_target="tpu_custom_call" | custom-call | flops 7134511104 | bytes 8404992 | tf_op jit(solution)/shard_map/newton/pallas_call | solution.py:420
  441.6 42.3 %newton.10 = f32[672,768]{1,0:T(8,128)} custom-call(f32[448,768]{1,0:T(8,128)} %bitcast.276, f32[672,768]{1,0:T(8,128)} %get-tuple-element.121.x_ref, bf16[672,768]{1,0:T(8,128)(2,1)} %refs_0_.2), custom_call_target="tpu_custom_call" | custom-call | flops 39069941760 | bytes 9879552 | tf_op jit(solution)/shard_map/newton/pallas_call | solution.py:420
  (331 shorter events, 101.4 us)
Async XLA Ops:
  7.2 92.6 %all-gather.2.cloned.1.call-start = ((), (), s32[]{:S(2)}) async-start(), calls=%async_computation | async-start | bytes 8515584 | tf_op jit(solution)/shard_map/all_gather | solution.py:601
  10.0 10.7 %collective-permute-start = (bf16[120,768]{1,0:T(8,128)(2,1)S(1)}, bf16[120,768]{1,0:T(8,128)(2,1)S(1)}, u32[]{:S(2)}, u32[]{:S(2)}) collective-permute-start(bf16[120,768]{1,0:T(8,128)(2,1)S(1)} %get-tuple-element.127), channel_id=1, source_target_pairs={{0,2},{1,3},{2,4},{3,5},{4,6},{5,7},{6,0},{7,1},{8,10},{9,11},{10,... | collective-permute-start | bytes 552968 | tf_op jit(solution)/shard_map/ppermute | solution.py:575
  13.0 16.5 %collective-permute-start.1 = (bf16[120,768]{1,0:T(8,128)(2,1)S(1)}, bf16[120,768]{1,0:T(8,128)(2,1)S(1)}, u32[]{:S(2)}, u32[]{:S(2)}) collective-permute-start(bf16[120,768]{1,0:T(8,128)(2,1)S(1)} %get-tuple-element.127), channel_id=1, source_target_pairs={{0,4},{1,5},{2,6},{3,7},{4,0},{5,1},{6,2},{7,3},{8,12},{9,13},{10,... | collective-permute-start | bytes 552968 | tf_op jit(solution)/shard_map/ppermute | solution.py:575
  15.6 14.0 %collective-permute-start.2 = (bf16[120,768]{1,0:T(8,128)(2,1)S(1)}, bf16[120,768]{1,0:T(8,128)(2,1)S(1)}, u32[]{:S(2)}, u32[]{:S(2)}) collective-permute-start(bf16[120,768]{1,0:T(8,128)(2,1)S(1)} %get-tuple-element.127), channel_id=1, source_target_pairs={{0,6},{1,7},{2,0},{3,1},{4,2},{5,3},{6,4},{7,5},{8,14},{9,15},{10,... | collective-permute-start | bytes 552968 | tf_op jit(solution)/shard_map/ppermute | solution.py:575
  29.7 8.7 %collective-permute-start.3 = (bf16[4,48,768]{2,1,0:T(8,128)(2,1)S(1)}, bf16[4,48,768]{2,1,0:T(8,128)(2,1)S(1)}, u32[]{:S(2)}, u32[]{:S(2)}) collective-permute-start(bf16[4,48,768]{2,1,0:T(8,128)(2,1)S(1)} %slice.145), channel_id=1, source_target_pairs={{0,1},{1,0},{2,3},{3,2},{4,5},{5,4},{6,7},{7,6},{8,9},{9,8},{10,11... | collective-permute-start | bytes 884744 | tf_op jit(solution)/shard_map/ppermute | solution.py:476
  31.3 11.8 %collective-permute-start.5 = (bf16[4,72,768]{2,1,0:T(8,128)(2,1)S(1)}, bf16[4,72,768]{2,1,0:T(8,128)(2,1)S(1)}, u32[]{:S(2)}, u32[]{:S(2)}) collective-permute-start(bf16[4,72,768]{2,1,0:T(8,128)(2,1)S(1)} %slice.146), channel_id=1, source_target_pairs={{0,16},{8,24},{16,0},{24,8},{1,17},{9,25},{17,1},{25,9},{2,18},{10... | collective-permute-start | bytes 1327112 | tf_op jit(solution)/shard_map/ppermute | solution.py:476
  43.2 23.8 %collective-permute-start.6 = (bf16[4,2,72,768]{3,2,1,0:T(8,128)(2,1)S(1)}, bf16[4,2,72,768]{3,2,1,0:T(8,128)(2,1)S(1)}, u32[]{:S(2)}, u32[]{:S(2)}) collective-permute-start(bf16[4,2,72,768]{3,2,1,0:T(8,128)(2,1)S(1)} %pad_maximum_fusion.4), channel_id=1, source_target_pairs={{0,1},{1,0},{2,3},{3,2},{4,5},{5,4},{6,7},{7,6},{8,9},{9,8},{10,11... | collective-permute-start | bytes 2654216 | tf_op jit(solution)/shard_map/ppermute | solution.py:476
  43.6 20.8 %collective-permute-start.4 = (bf16[4,2,48,768]{3,2,0,1:T(8,128)(2,1)S(1)}, bf16[4,2,48,768]{3,2,0,1:T(8,128)(2,1)S(1)}, u32[]{:S(2)}, u32[]{:S(2)}) collective-permute-start(bf16[4,2,48,768]{3,2,0,1:T(8,128)(2,1)S(1)} %pad_maximum_fusion.9), channel_id=1, source_target_pairs={{0,16},{8,24},{16,0},{24,8},{1,17},{9,25},{17,1},{25,9},{2,18},{10... | collective-permute-start | bytes 1769480 | tf_op jit(solution)/shard_map/ppermute | solution.py:476
  69.0 8.3 %collective-permute-start.7 = (bf16[4,2,2,120,768]{4,3,2,1,0:T(8,128)(2,1)}, bf16[4,2,2,120,768]{4,3,2,1,0:T(8,128)(2,1)}, u32[]{:S(2)}, u32[]{:S(2)}) collective-permute-start(bf16[4,2,2,120,768]{4,3,2,1,0:T(8,128)(2,1)} %maximum_maximum_fusion), channel_id=1, source_target_pairs={{0,8},{8,0},{16,24},{24,16},{1,9},{9,1},{17,25},{25,17},{2,10},{10... | collective-permute-start | bytes 8847368 | tf_op jit(solution)/shard_map/ppermute | solution.py:476
  167.0 32.9 %collective-permute-start.9 = (bf16[3072,384]{1,0:T(8,128)(2,1)}, bf16[3072,384]{1,0:T(8,128)(2,1)}, u32[]{:S(2)}, u32[]{:S(2)}) collective-permute-start(bf16[3072,384]{1,0:T(8,128)(2,1)} %get-tuple-element.78), channel_id=1, source_target_pairs={{0,8},{8,0},{16,24},{24,16},{1,9},{9,1},{17,25},{25,17},{2,10},{10... | collective-permute-start | bytes 7077896 | tf_op jit(solution)/shard_map/ppermute | solution.py:476
  174.8 25.0 %collective-permute-start.8 = (bf16[768,384]{1,0:T(8,128)(2,1)S(1)}, bf16[768,384]{1,0:T(8,128)(2,1)S(1)}, u32[]{:S(2)}, u32[]{:S(2)}) collective-permute-start(bf16[768,384]{1,0:T(8,128)(2,1)S(1)} %copy-done.41), channel_id=1, source_target_pairs={{0,8},{8,0},{16,24},{24,16},{1,9},{9,1},{17,25},{25,17},{2,10},{10... | collective-permute-start | bytes 1769480 | tf_op jit(solution)/shard_map/ppermute | solution.py:476
  196.9 33.2 %collective-permute-start.10 = (bf16[3,384,384]{2,1,0:T(8,128)(2,1)}, bf16[3,384,384]{2,1,0:T(8,128)(2,1)}, u32[]{:S(2)}, u32[]{:S(2)}) collective-permute-start(bf16[3,384,384]{2,1,0:T(8,128)(2,1)} %get-tuple-element.86), channel_id=1, source_target_pairs={{0,8},{8,0},{16,24},{24,16},{1,9},{9,1},{17,25},{25,17},{2,10},{10... | collective-permute-start | bytes 2654216 | tf_op jit(solution)/shard_map/ppermute | solution.py:476
  197.2 34.5 %collective-permute-start.11 = (bf16[3072,384]{1,0:T(8,128)(2,1)}, bf16[3072,384]{1,0:T(8,128)(2,1)}, u32[]{:S(2)}, u32[]{:S(2)}) collective-permute-start(bf16[3072,384]{1,0:T(8,128)(2,1)} %get-tuple-element.89), channel_id=1, source_target_pairs={{0,8},{8,0},{16,24},{24,16},{1,9},{9,1},{17,25},{25,17},{2,10},{10... | collective-permute-start | bytes 7077896 | tf_op jit(solution)/shard_map/ppermute | solution.py:476
  204.9 55.5 %collective-permute-start.30 = (bf16[4,2,112,384]{3,2,0,1:T(8,128)(2,1)}, bf16[4,2,112,384]{3,2,0,1:T(8,128)(2,1)}, u32[]{:S(2)}, u32[]{:S(2)}) collective-permute-start(bf16[4,2,112,384]{3,2,0,1:T(8,128)(2,1)} %bitcast.252), channel_id=1, source_target_pairs={{0,1},{1,0},{2,3},{3,2},{4,5},{5,4},{6,7},{7,6},{8,9},{9,8},{10,11... | collective-permute-start | bytes 2064392 | tf_op jit(solution)/shard_map/ppermute | solution.py:476
  207.0 55.4 %collective-permute-start.32 = (bf16[4,2,128,384]{3,2,0,1:T(8,128)(2,1)}, bf16[4,2,128,384]{3,2,0,1:T(8,128)(2,1)}, u32[]{:S(2)}, u32[]{:S(2)}) collective-permute-start(bf16[4,2,128,384]{3,2,0,1:T(8,128)(2,1)} %bitcast.251), channel_id=1, source_target_pairs={{0,16},{8,24},{16,0},{24,8},{1,17},{9,25},{17,1},{25,9},{2,18},{10... | collective-permute-start | bytes 2359304 | tf_op jit(solution)/shard_map/ppermute | solution.py:476
  236.6 18.8 %collective-permute-start.14 = (bf16[4,2,96,384]{3,2,1,0:T(8,128)(2,1)}, bf16[4,2,96,384]{3,2,1,0:T(8,128)(2,1)}, u32[]{:S(2)}, u32[]{:S(2)}) collective-permute-start(bf16[4,2,96,384]{3,2,1,0:T(8,128)(2,1)} %dynamic-slice_bitcast_fusion), channel_id=1, source_target_pairs={{0,16},{8,24},{16,0},{24,8},{1,17},{9,25},{17,1},{25,9},{2,18},{10... | collective-permute-start | bytes 1769480 | tf_op jit(solution)/shard_map/ppermute | solution.py:476
  238.9 18.7 %collective-permute-start.12 = (bf16[4,2,96,384]{3,2,0,1:T(8,128)(2,1)}, bf16[4,2,96,384]{3,2,0,1:T(8,128)(2,1)}, u32[]{:S(2)}, u32[]{:S(2)}) collective-permute-start(bf16[4,2,96,384]{3,2,0,1:T(8,128)(2,1)} %bitcast.253), channel_id=1, source_target_pairs={{0,1},{1,0},{2,3},{3,2},{4,5},{5,4},{6,7},{7,6},{8,9},{9,8},{10,11... | collective-permute-start | bytes 1769480 | tf_op jit(solution)/shard_map/ppermute | solution.py:476
  240.2 31.4 %collective-permute-start.19 = (bf16[3,384,384]{2,1,0:T(8,128)(2,1)}, bf16[3,384,384]{2,1,0:T(8,128)(2,1)}, u32[]{:S(2)}, u32[]{:S(2)}) collective-permute-start(bf16[3,384,384]{2,1,0:T(8,128)(2,1)} %get-tuple-element.91), channel_id=1, source_target_pairs={{0,8},{8,0},{16,24},{24,16},{1,9},{9,1},{17,25},{25,17},{2,10},{10... | collective-permute-start | bytes 2654216 | tf_op jit(solution)/shard_map/ppermute | solution.py:476
  256.7 9.6 %collective-permute-start.15 = (bf16[4,96,384]{2,1,0:T(8,128)(2,1)S(1)}, bf16[4,96,384]{2,1,0:T(8,128)(2,1)S(1)}, u32[]{:S(2)}, u32[]{:S(2)}) collective-permute-start(bf16[4,96,384]{2,1,0:T(8,128)(2,1)S(1)} %dynamic-slice_bitcast_fusion.5), channel_id=1, source_target_pairs={{0,1},{1,0},{2,3},{3,2},{4,5},{5,4},{6,7},{7,6},{8,9},{9,8},{10,11... | collective-permute-start | bytes 884744 | tf_op jit(solution)/shard_map/ppermute | solution.py:476
  258.8 9.9 %collective-permute-start.13 = (bf16[4,96,384]{2,1,0:T(8,128)(2,1)S(1)}, bf16[4,96,384]{2,1,0:T(8,128)(2,1)S(1)}, u32[]{:S(2)}, u32[]{:S(2)}) collective-permute-start(bf16[4,96,384]{2,1,0:T(8,128)(2,1)S(1)} %dynamic-slice_bitcast_fusion.6), channel_id=1, source_target_pairs={{0,16},{8,24},{16,0},{24,8},{1,17},{9,25},{17,1},{25,9},{2,18},{10... | collective-permute-start | bytes 884744 | tf_op jit(solution)/shard_map/ppermute | solution.py:476
  261.8 17.0 %collective-permute-start.31 = (bf16[4,112,384]{2,1,0:T(8,128)(2,1)S(1)}, bf16[4,112,384]{2,1,0:T(8,128)(2,1)S(1)}, u32[]{:S(2)}, u32[]{:S(2)}) collective-permute-start(bf16[4,112,384]{2,1,0:T(8,128)(2,1)S(1)} %dynamic-slice_bitcast_fusion.4), channel_id=1, source_target_pairs={{0,16},{8,24},{16,0},{24,8},{1,17},{9,25},{17,1},{25,9},{2,18},{10... | collective-permute-start | bytes 1032200 | tf_op jit(solution)/shard_map/ppermute | solution.py:476
  263.8 18.9 %collective-permute-start.33 = (bf16[4,128,384]{2,1,0:T(8,128)(2,1)S(1)}, bf16[4,128,384]{2,1,0:T(8,128)(2,1)S(1)}, u32[]{:S(2)}, u32[]{:S(2)}) collective-permute-start(bf16[4,128,384]{2,1,0:T(8,128)(2,1)S(1)} %dynamic-slice_bitcast_fusion.1), channel_id=1, source_target_pairs={{0,1},{1,0},{2,3},{3,2},{4,5},{5,4},{6,7},{7,6},{8,9},{9,8},{10,11... | collective-permute-start | bytes 1179656 | tf_op jit(solution)/shard_map/ppermute | solution.py:476
  269.0 11.6 %collective-permute-start.16 = (bf16[192,384]{1,0:T(8,128)(2,1)S(1)}, bf16[192,384]{1,0:T(8,128)(2,1)S(1)}, u32[]{:S(2)}, u32[]{:S(2)}) collective-permute-start(bf16[192,384]{1,0:T(8,128)(2,1)S(1)} %get-tuple-element.169), channel_id=1, source_target_pairs={{0,2},{1,3},{2,4},{3,5},{4,6},{5,7},{6,0},{7,1},{8,10},{9,11},{10,... | collective-permute-start | bytes 442376 | tf_op jit(solution)/shard_map/ppermute | solution.py:545
  270.1 12.6 %collective-permute-start.17 = (bf16[192,384]{1,0:T(8,128)(2,1)S(1)}, bf16[192,384]{1,0:T(8,128)(2,1)S(1)}, u32[]{:S(2)}, u32[]{:S(2)}) collective-permute-start(bf16[192,384]{1,0:T(8,128)(2,1)S(1)} %get-tuple-element.170), channel_id=1, source_target_pairs={{0,4},{1,5},{2,6},{3,7},{4,0},{5,1},{6,2},{7,3},{8,12},{9,13},{10,... | collective-permute-start | bytes 442376 | tf_op jit(solution)/shard_map/ppermute | solution.py:545
  271.5 11.1 %collective-permute-start.18 = (bf16[192,384]{1,0:T(8,128)(2,1)S(1)}, bf16[192,384]{1,0:T(8,128)(2,1)S(1)}, u32[]{:S(2)}, u32[]{:S(2)}) collective-permute-start(bf16[192,384]{1,0:T(8,128)(2,1)S(1)} %get-tuple-element.171), channel_id=1, source_target_pairs={{0,6},{1,7},{2,0},{3,1},{4,2},{5,3},{6,4},{7,5},{8,14},{9,15},{10,... | collective-permute-start | bytes 442376 | tf_op jit(solution)/shard_map/ppermute | solution.py:545
  278.9 9.7 %collective-permute-start.20 = (bf16[4,2,64,384]{3,2,0,1:T(8,128)(2,1)S(1)}, bf16[4,2,64,384]{3,2,0,1:T(8,128)(2,1)S(1)}, u32[]{:S(2)}, u32[]{:S(2)}) collective-permute-start(bf16[4,2,64,384]{3,2,0,1:T(8,128)(2,1)S(1)} %bitcast.294), channel_id=1, source_target_pairs={{0,1},{1,0},{2,3},{3,2},{4,5},{5,4},{6,7},{7,6},{8,9},{9,8},{10,11... | collective-permute-start | bytes 1179656 | tf_op jit(solution)/shard_map/ppermute | solution.py:476
  280.5 17.9 %collective-permute-start.22 = (bf16[4,2,80,384]{3,2,0,1:T(8,128)(2,1)S(1)}, bf16[4,2,80,384]{3,2,0,1:T(8,128)(2,1)S(1)}, u32[]{:S(2)}, u32[]{:S(2)}) collective-permute-start(bf16[4,2,80,384]{3,2,0,1:T(8,128)(2,1)S(1)} %bitcast.293), channel_id=1, source_target_pairs={{0,16},{8,24},{16,0},{24,8},{1,17},{9,25},{17,1},{25,9},{2,18},{10... | collective-permute-start | bytes 1474568 | tf_op jit(solution)/shard_map/ppermute | solution.py:476
  282.8 9.2 %collective-permute-start.34 = (bf16[240,384]{1,0:T(8,128)(2,1)S(1)}, bf16[240,384]{1,0:T(8,128)(2,1)S(1)}, u32[]{:S(2)}, u32[]{:S(2)}) collective-permute-start(bf16[240,384]{1,0:T(8,128)(2,1)S(1)} %get-tuple-element.160), channel_id=1, source_target_pairs={{0,2},{1,3},{2,4},{3,5},{4,6},{5,7},{6,0},{7,1},{8,10},{9,11},{10,... | collective-permute-start | bytes 552968 | tf_op jit(solution)/shard_map/ppermute | solution.py:545
  285.6 12.6 %collective-permute-start.35 = (bf16[240,384]{1,0:T(8,128)(2,1)S(1)}, bf16[240,384]{1,0:T(8,128)(2,1)S(1)}, u32[]{:S(2)}, u32[]{:S(2)}) collective-permute-start(bf16[240,384]{1,0:T(8,128)(2,1)S(1)} %get-tuple-element.161), channel_id=1, source_target_pairs={{0,4},{1,5},{2,6},{3,7},{4,0},{5,1},{6,2},{7,3},{8,12},{9,13},{10,... | collective-permute-start | bytes 552968 | tf_op jit(solution)/shard_map/ppermute | solution.py:545
  286.3 11.9 %collective-permute-start.36 = (bf16[240,384]{1,0:T(8,128)(2,1)S(1)}, bf16[240,384]{1,0:T(8,128)(2,1)S(1)}, u32[]{:S(2)}, u32[]{:S(2)}) collective-permute-start(bf16[240,384]{1,0:T(8,128)(2,1)S(1)} %get-tuple-element.162), channel_id=1, source_target_pairs={{0,6},{1,7},{2,0},{3,1},{4,2},{5,3},{6,4},{7,5},{8,14},{9,15},{10,... | collective-permute-start | bytes 552968 | tf_op jit(solution)/shard_map/ppermute | solution.py:545
  288.7 11.7 %collective-permute-start.21 = (bf16[4,64,384]{2,1,0:T(8,128)(2,1)S(1)}, bf16[4,64,384]{2,1,0:T(8,128)(2,1)S(1)}, u32[]{:S(2)}, u32[]{:S(2)}) collective-permute-start(bf16[4,64,384]{2,1,0:T(8,128)(2,1)S(1)} %dynamic-slice_bitcast_fusion.8), channel_id=1, source_target_pairs={{0,16},{8,24},{16,0},{24,8},{1,17},{9,25},{17,1},{25,9},{2,18},{10... | collective-permute-start | bytes 589832 | tf_op jit(solution)/shard_map/ppermute | solution.py:476
  298.6 8.6 %collective-permute-start.23 = (bf16[4,80,384]{2,1,0:T(8,128)(2,1)S(1)}, bf16[4,80,384]{2,1,0:T(8,128)(2,1)S(1)}, u32[]{:S(2)}, u32[]{:S(2)}) collective-permute-start(bf16[4,80,384]{2,1,0:T(8,128)(2,1)S(1)} %dynamic-slice_bitcast_fusion.7), channel_id=1, source_target_pairs={{0,1},{1,0},{2,3},{3,2},{4,5},{5,4},{6,7},{7,6},{8,9},{9,8},{10,11... | collective-permute-start | bytes 737288 | tf_op jit(solution)/shard_map/ppermute | solution.py:476
  306.2 9.9 %collective-permute-start.40 = (f32[224,384]{1,0:T(8,128)S(1)}, f32[224,384]{1,0:T(8,128)S(1)}, u32[]{:S(2)}, u32[]{:S(2)}) collective-permute-start(f32[224,384]{1,0:T(8,128)S(1)} %dynamic-slice_bitcast_fusion.2), channel_id=1, source_target_pairs={{0,1},{1,0},{2,3},{3,2},{4,5},{5,4},{6,7},{7,6},{8,9},{9,8},{10,11... | collective-permute-start | bytes 1032200 | tf_op jit(solution)/shard_map/ppermute | solution.py:476
  307.4 11.0 %collective-permute-start.24 = (bf16[144,384]{1,0:T(8,128)(2,1)S(1)}, bf16[144,384]{1,0:T(8,128)(2,1)S(1)}, u32[]{:S(2)}, u32[]{:S(2)}) collective-permute-start(bf16[144,384]{1,0:T(8,128)(2,1)S(1)} %get-tuple-element.176), channel_id=1, source_target_pairs={{0,2},{1,3},{2,4},{3,5},{4,6},{5,7},{6,0},{7,1},{8,10},{9,11},{10,... | collective-permute-start | bytes 331784 | tf_op jit(solution)/shard_map/ppermute | solution.py:545
  311.9 9.8 %collective-permute-start.25 = (bf16[144,384]{1,0:T(8,128)(2,1)S(1)}, bf16[144,384]{1,0:T(8,128)(2,1)S(1)}, u32[]{:S(2)}, u32[]{:S(2)}) collective-permute-start(bf16[144,384]{1,0:T(8,128)(2,1)S(1)} %get-tuple-element.177), channel_id=1, source_target_pairs={{0,4},{1,5},{2,6},{3,7},{4,0},{5,1},{6,2},{7,3},{8,12},{9,13},{10,... | collective-permute-start | bytes 331784 | tf_op jit(solution)/shard_map/ppermute | solution.py:545
  316.1 7.4 %collective-permute-start.41 = (f32[112,384]{1,0:T(8,128)S(1)}, f32[112,384]{1,0:T(8,128)S(1)}, u32[]{:S(2)}, u32[]{:S(2)}) collective-permute-start(f32[112,384]{1,0:T(8,128)S(1)} %dynamic-slice_bitcast_fusion.10), channel_id=1, source_target_pairs={{0,16},{8,24},{16,0},{24,8},{1,17},{9,25},{17,1},{25,9},{2,18},{10... | collective-permute-start | bytes 516104 | tf_op jit(solution)/shard_map/ppermute | solution.py:476
  317.8 17.6 %collective-permute-start.38 = (bf16[240,768]{1,0:T(8,128)(2,1)S(1)}, bf16[240,768]{1,0:T(8,128)(2,1)S(1)}, u32[]{:S(2)}, u32[]{:S(2)}) collective-permute-start(bf16[240,768]{1,0:T(8,128)(2,1)S(1)} %bitcast.270), channel_id=1, source_target_pairs={{0,16},{8,24},{16,0},{24,8},{1,17},{9,25},{17,1},{25,9},{2,18},{10... | collective-permute-start | bytes 1105928 | tf_op jit(solution)/shard_map/ppermute | solution.py:476
  323.6 7.8 %collective-permute-start.42 = (f32[112,384]{1,0:T(8,128)S(1)}, f32[112,384]{1,0:T(8,128)S(1)}, u32[]{:S(2)}, u32[]{:S(2)}) collective-permute-start(f32[112,384]{1,0:T(8,128)S(1)} %bitcast_add_fusion.3), channel_id=1, source_target_pairs={{0,2},{1,3},{2,0},{3,1},{4,6},{5,7},{6,4},{7,5},{8,10},{9,11},{10,... | collective-permute-start | bytes 516104 | tf_op jit(solution)/shard_map/ppermute | solution.py:476
  328.1 18.1 %collective-permute-start.27 = (bf16[336,384]{1,0:T(8,128)(2,1)S(1)}, bf16[336,384]{1,0:T(8,128)(2,1)S(1)}, u32[]{:S(2)}, u32[]{:S(2)}) collective-permute-start(bf16[336,384]{1,0:T(8,128)(2,1)S(1)} %pad_maximum_fusion.14), channel_id=1, source_target_pairs={{0,8},{8,0},{16,24},{24,16},{1,9},{9,1},{17,25},{25,17},{2,10},{10... | collective-permute-start | bytes 774152 | tf_op jit(solution)/shard_map/ppermute | solution.py:476
  331.4 9.2 %collective-permute-start.43 = (f32[112,384]{1,0:T(8,128)S(1)}, f32[112,384]{1,0:T(8,128)S(1)}, u32[]{:S(2)}, u32[]{:S(2)}) collective-permute-start(f32[112,384]{1,0:T(8,128)S(1)} %add.428), channel_id=1, source_target_pairs={{0,4},{1,5},{2,6},{3,7},{4,0},{5,1},{6,2},{7,3},{8,12},{9,13},{10,... | collective-permute-start | bytes 516104 | tf_op jit(solution)/shard_map/ppermute | solution.py:476
  353.6 8.4 %collective-permute-start.46 = (f32[448,384]{1,0:T(8,128)S(1)}, f32[448,384]{1,0:T(8,128)S(1)}, u32[]{:S(2)}, u32[]{:S(2)}) collective-permute-start(f32[448,384]{1,0:T(8,128)S(1)} %bitcast.272), channel_id=1, source_target_pairs={{0,8},{8,0},{16,24},{24,16},{1,9},{9,1},{17,25},{25,17},{2,10},{10... | collective-permute-start | bytes 2064392 | tf_op jit(solution)/shard_map/ppermute | solution.py:476
  359.6 14.9 %collective-permute-start.39 = (f32[224,384]{1,0:T(8,128)S(1)}, f32[224,384]{1,0:T(8,128)S(1)}, u32[]{:S(2)}, u32[]{:S(2)}) collective-permute-start(f32[224,384]{1,0:T(8,128)S(1)} %dynamic-slice_bitcast_fusion.3), channel_id=1, source_target_pairs={{0,1},{1,0},{2,3},{3,2},{4,5},{5,4},{6,7},{7,6},{8,9},{9,8},{10,11... | collective-permute-start | bytes 1032200 | tf_op jit(solution)/shard_map/ppermute | solution.py:476
  359.7 55.9 %collective-permute-start.29 = (bf16[144,768]{1,0:T(8,128)(2,1)S(1)}, bf16[144,768]{1,0:T(8,128)(2,1)S(1)}, u32[]{:S(2)}, u32[]{:S(2)}) collective-permute-start(bf16[144,768]{1,0:T(8,128)(2,1)S(1)} %bitcast.287), channel_id=1, source_target_pairs={{0,16},{8,24},{16,0},{24,8},{1,17},{9,25},{17,1},{25,9},{2,18},{10... | collective-permute-start | bytes 663560 | tf_op jit(solution)/shard_map/ppermute | solution.py:476
  361.3 60.4 %collective-permute-start.28 = (bf16[192,768]{1,0:T(8,128)(2,1)S(1)}, bf16[192,768]{1,0:T(8,128)(2,1)S(1)}, u32[]{:S(2)}, u32[]{:S(2)}) collective-permute-start(bf16[192,768]{1,0:T(8,128)(2,1)S(1)} %bitcast.285), channel_id=1, source_target_pairs={{0,16},{8,24},{16,0},{24,8},{1,17},{9,25},{17,1},{25,9},{2,18},{10... | collective-permute-start | bytes 884744 | tf_op jit(solution)/shard_map/ppermute | solution.py:476
  374.6 12.7 %collective-permute-start.47 = (f32[112,384]{1,0:T(8,128)S(1)}, f32[112,384]{1,0:T(8,128)S(1)}, u32[]{:S(2)}, u32[]{:S(2)}) collective-permute-start(f32[112,384]{1,0:T(8,128)S(1)} %dynamic-slice_bitcast_fusion.9), channel_id=1, source_target_pairs={{0,16},{8,24},{16,0},{24,8},{1,17},{9,25},{17,1},{25,9},{2,18},{10... | collective-permute-start | bytes 516104 | tf_op jit(solution)/shard_map/ppermute | solution.py:476
  387.3 13.0 %collective-permute-start.48 = (f32[112,384]{1,0:T(8,128)S(1)}, f32[112,384]{1,0:T(8,128)S(1)}, u32[]{:S(2)}, u32[]{:S(2)}) collective-permute-start(f32[112,384]{1,0:T(8,128)S(1)} %bitcast_add_fusion.2), channel_id=1, source_target_pairs={{0,2},{1,3},{2,0},{3,1},{4,6},{5,7},{6,4},{7,5},{8,10},{9,11},{10,... | collective-permute-start | bytes 516104 | tf_op jit(solution)/shard_map/ppermute | solution.py:476
  400.3 14.7 %collective-permute-start.49 = (f32[112,384]{1,0:T(8,128)S(1)}, f32[112,384]{1,0:T(8,128)S(1)}, u32[]{:S(2)}, u32[]{:S(2)}) collective-permute-start(f32[112,384]{1,0:T(8,128)S(1)} %add.433), channel_id=1, source_target_pairs={{0,4},{1,5},{2,6},{3,7},{4,0},{5,1},{6,2},{7,3},{8,12},{9,13},{10,... | collective-permute-start | bytes 516104 | tf_op jit(solution)/shard_map/ppermute | solution.py:476
  428.0 9.9 %collective-permute-start.52 = (f32[448,384]{1,0:T(8,128)S(1)}, f32[448,384]{1,0:T(8,128)S(1)}, u32[]{:S(2)}, u32[]{:S(2)}) collective-permute-start(f32[448,384]{1,0:T(8,128)S(1)} %bitcast.273), channel_id=1, source_target_pairs={{0,8},{8,0},{16,24},{24,16},{1,9},{9,1},{17,25},{25,17},{2,10},{10... | collective-permute-start | bytes 2064392 | tf_op jit(solution)/shard_map/ppermute | solution.py:476
  (53 other events, 450.8 us)
Sparse Core Ops, SparseCore 0:
  11.5 88.2 all-gather.1

commit v3 on v2

--- a/solution.py
+++ b/solution.py
@@ -32,7 +32,7 @@
 penalty = 16384.0
 vmem_bytes = 60 * 1024 * 1024
 tile_rows = 256
-extra_rows = 64
+extra_rows = 32
 pair = 2 * HEAD
 
 
@@ -122,7 +122,7 @@
     def whole(shape):
         return pl.BlockSpec(shape, lambda p: (0, 0))
 
-    return pl.pallas_call(
+    call = pl.pallas_call(
         forward_kernel,
         grid=(pairs,),
         in_specs=[
@@ -156,16 +156,15 @@
             transcendentals=HEADS * length * length,
         ),
         name="attention_forward",
-    )(
-        joined, joined, joined, onek, penq, q_gain.reshape(HEAD, 1), k_gain.reshape(HEAD, 1), grad_y, core
-    )
+    )
+    return call(joined, joined, joined, onek, penq, q_gain.reshape(HEAD, 1), k_gain.reshape(HEAD, 1), grad_y, core)
 
 
 def backward_kernel(
-    q_ref, k_ref, v_ref, do_ref, terms_ref, exact_ref, sum_ref, gq_ref, gk_ref, x_ref, core_ref,
-    dq_ref, dk_ref, dv_ref, keep_ref, send_ref, ggq_ref, ggk_ref,
-    vaug, qnat, klow_t, doaug_t, donat,
+    q_ref, k_ref, v_ref, do_ref, terms_ref, exact_ref, sum_ref, gq_ref, gk_ref, x_ref,
+    core_ref, *refs,
 ):
+    grads_ref, keep_ref, send_ref, ggq_ref, ggk_ref, vaug, qnat, klow_t, doaug_t, donat = refs[-10:]
     length = q_ref.shape[0]
     step = pl.program_id(0)
     q_t = q_ref[...].T
@@ -207,9 +206,9 @@
         dv_parts.append(dvalue.T)
     grads = jnp.concatenate(dq_parts + dk_parts + dv_parts, 0).astype(bf16)
     halves(nn(grads, x_ref[...]).astype(bf16), core_ref, keep_ref, send_ref)
-    dq_ref[...] = grads[:pair].T
-    dk_ref[...] = grads[pair : 2 * pair].T
-    dv_ref[...] = grads[2 * pair :].T
+    grads_ref[0] = grads[:pair].T
+    grads_ref[1] = grads[pair : 2 * pair].T
+    grads_ref[2] = grads[2 * pair :].T
 
     @pl.when(step == 0)
     def _():
@@ -220,19 +219,20 @@
     ggk_ref[...] += jnp.broadcast_to(k_gain_grad, ggk_ref.shape)
 
 
-def attention_backward(joined, dattended, terms, exact, inverse_sum, q_gain, k_gain, x_low, core, first, count):
+def attention_backward(
+    joined, dattended, terms, exact, inverse_sum, q_gain, k_gain, x_low, core, first, count, room, place=0, into=()
+):
     length = joined.shape[0]
     pairs = D // pair
 
-    def block(part, offset=first):
-        return pl.BlockSpec((length, pair), lambda p: (0, part * pairs + offset + p))
+    def block(part):
+        return pl.BlockSpec((length, pair), lambda p: (0, part * pairs + first + p))
 
     def whole(shape):
         return pl.BlockSpec(shape, lambda p: (0, 0))
 
-    out = jax.ShapeDtypeStruct((length, count * pair), bf16)
     gain = jax.ShapeDtypeStruct((HEAD, 128), f32)
-    outs = pl.pallas_call(
+    call = pl.pallas_call(
         backward_kernel,
         grid=(count,),
         in_specs=[
@@ -241,11 +241,14 @@
             pl.BlockSpec((pair, length), lambda p: (first + p, 0)),
             pl.BlockSpec((1, 8, length), lambda p: (first + p, 0, 0)),
             whole((HEAD, 1)), whole((HEAD, 1)), whole((length, D)), core_spec,
+            *[pl.BlockSpec(memory_space=pl.ANY)] * len(into),
         ],
-        out_specs=[block(0, 0)] * 3
-        + [pl.BlockSpec((3, pair, D // 2), lambda p: (0, p, 0))] * 2
+        out_specs=[pl.BlockSpec((3, length, pair), lambda p: (0, 0, p))]
+        + [pl.BlockSpec((3, pair, D // 2), lambda p: (0, place + p, 0))] * 2
         + [whole((HEAD, 128))] * 2,
-        out_shape=[out] * 3 + [jax.ShapeDtypeStruct((3, count * pair, D // 2), bf16)] * 2 + [gain] * 2,
+        out_shape=[jax.ShapeDtypeStruct((3, length, count * pair), bf16)]
+        + [jax.ShapeDtypeStruct((3, room * pair, D // 2), bf16)] * 2 + [gain] * 2,
+        input_output_aliases={11 + i: 1 + i for i in range(len(into))},
         scratch_shapes=[
             pltpu.VMEM((2, length, HEAD + 16), bf16),
             pltpu.VMEM((2, length, HEAD), bf16),
@@ -260,11 +263,9 @@
             transcendentals=0,
         ),
         name="attention_backward",
-    )(
-        joined, joined, joined, dattended, terms, exact, inverse_sum,
-        q_gain.reshape(HEAD, 1), k_gain.reshape(HEAD, 1), x_low, core,
-    )
-    return (outs[:3], outs[3], outs[4], outs[5][:, 0], outs[6][:, 0])
+    )
+    outs = call(joined, joined, joined, dattended, terms, exact, inverse_sum, q_gain.reshape(HEAD, 1), k_gain.reshape(HEAD, 1), x_low, core, *into)
+    return (*outs[:3], outs[3][:, 0], outs[4][:, 0])
 
 
 def gelu_pair(u):
@@ -277,35 +278,55 @@
     return (u * phi, phi + u * (0.3989422804014327 * e))
 
 
-def mlp_kernel(
-    x_ref, gy_ref, wu_ref, wd_ref, core_ref, res_ref, gn_ref, keep_up, send_up, keep_down, send_down
-):
-    @pl.when(pl.program_id(0) == 0)
+def mlp_kernel(x_ref, gy_ref, wu_ref, wd_ref, core_ref, res_ref, gn_ref, keep_down, send_down, *refs, segments):
+    step = pl.program_id(0)
+    act_ref, dup_ref = refs[-2:]
+    tile = wu_ref.shape[0]
+
+    @pl.when(step == 0)
     def _():
         res_ref[...] = jnp.zeros_like(res_ref)
         gn_ref[...] = jnp.zeros_like(gn_ref)
 
-    x, grad_y, wu, wd = x_ref[...], gy_ref[...], wu_ref[...], wd_ref[...]
-    upward = contract(x, wu, 1, 1).astype(bf16).astype(f32)
-    grad_hidden = contract(grad_y, wd, 1, 1)
-    active, slope = gelu_pair(upward)
-    active = active.astype(bf16)
-    dupward = (grad_hidden * slope).astype(bf16)
-    res_ref[...] += contract(active, wd, 1, 0)
-    gn_ref[...] += contract(dupward, wu, 1, 0)
-    halves(contract(dupward, x, 0, 0).astype(bf16), core_ref, keep_up, send_up)
-    halves(contract(active, grad_y, 0, 0).astype(bf16), core_ref, keep_down, send_down)
-
-
-def mlp(x_low, grad_y, w_in_all, w_out_all, core):
+    for begin in range(0, tile, tile_rows):
+        units = slice(begin, begin + tile_rows)
+        upward = contract(x_ref[...], wu_ref[units], 1, 1).astype(bf16).astype(f32)
+        grad_hidden = contract(gy_ref[...], wd_ref[units], 1, 1)
+        active, slope = gelu_pair(upward)
+        act_ref[:, units] = active.astype(bf16)
+        dup_ref[:, units] = (grad_hidden * slope).astype(bf16)
+    active, dupward = act_ref[...], dup_ref[...]
+    res_ref[...] += nn(active, wd_ref[...])
+    gn_ref[...] += nn(dupward, wu_ref[...])
+    halves(contract(active, gy_ref[...], 0, 0).astype(bf16), core_ref, keep_down, send_down)
+    grad = contract(dupward, x_ref[...], 0, 0).astype(bf16)
+
+    def place(index):
+        filled = [0, 0]
+        for begin, end, array in segments:
+            low, high = max(begin, index * tile), min(end, (index + 1) * tile)
+            if low < high:
+                rows = slice(filled[array] + low - begin, filled[array] + high - begin)
+                keep_ref, send_ref = refs[2 * array], refs[2 * array + 1]
+                halves(
+                    grad[low - index * tile : high - index * tile], core_ref, keep_ref.at[rows], send_ref.at[rows]
+                )
+            filled[array] += end - begin
+
+    for index in range(segments[-1][1] // tile):
+        pl.when(step == index)(partial(place, index))
+
+
+def mlp(x_low, grad_y, w_in_all, w_out_all, core, segments):
     length = x_low.shape[0]
     hidden = w_in_all.shape[0] - QKV
     tile = D
     whole = pl.BlockSpec((length, D), lambda t: (0, 0))
     total = jax.ShapeDtypeStruct((length, D), f32)
-    grad = jax.ShapeDtypeStruct((hidden, D // 2), bf16)
-    return pl.pallas_call(
-        mlp_kernel,
+    sizes = [sum(end - begin for begin, end, array in segments if array == i) for i in range(2)]
+    sizes = [(size, D // 2) for size in sizes if size for _ in range(2)]
+    call = pl.pallas_call(
+        partial(mlp_kernel, segments=segments),
         grid=(hidden // tile,),
         in_specs=[
             whole,
@@ -314,8 +335,13 @@
             pl.BlockSpec((tile, D), lambda t: (t + D // tile, 0)),
             core_spec,
         ],
-        out_specs=[whole, whole] + [pl.BlockSpec((tile, D // 2), lambda t: (t, 0))] * 4,
-        out_shape=[total, total] + [grad] * 4,
+        out_specs=[whole, whole]
+        + [pl.BlockSpec((tile, D // 2), lambda t: (t, 0))] * 2
+        + [pl.BlockSpec(size, lambda t: (0, 0)) for size in sizes],
+        out_shape=[total, total]
+        + [jax.ShapeDtypeStruct((hidden, D // 2), bf16)] * 2
+        + [jax.ShapeDtypeStruct(size, bf16) for size in sizes],
+        scratch_shapes=[pltpu.VMEM((length, tile), bf16)] * 2,
         compiler_params=pltpu.CompilerParams(vmem_limit_bytes=vmem_bytes),
         cost_estimate=pl.CostEstimate(
             flops=18 * length * D * hidden,
@@ -323,7 +349,55 @@
             transcendentals=length * hidden,
         ),
         name="mlp",
-    )(x_low, grad_y, w_in_all, w_out_all, core)
+    )
+    return call(x_low, grad_y, w_in_all, w_out_all, core)
+
+
+def input_kernel(*refs, calls):
+    grads = refs[:calls]
+    w_ref, normed_ref, tokens_ref, gy_ref, gain_ref, out_ref, ln_ref, total = refs[calls:]
+    step = pl.program_id(0)
+
+    @pl.when(step == 0)
+    def _():
+        total[...] = normed_ref[...]
+
+    begin = 0
+    sums = []
+    for ref in grads:
+        sums.append(nn(ref[0], w_ref[begin : begin + ref.shape[2], :]))
+        begin += ref.shape[2]
+    total[...] += sum(sums)
+
+    @pl.when(step == pl.num_programs(0) - 1)
+    def _():
+        x_hat, x_inverse = normalize(tokens_ref[...].astype(f32))
+        grad_normed = total[...]
+        ln_ref[...] = jnp.sum(grad_normed * x_hat, axis=0, keepdims=True)
+        back = norm_backward(grad_normed * gain_ref[...], x_hat, x_inverse)
+        out_ref[...] = (gy_ref[...].astype(f32) + back).astype(bf16)
+
+
+def input_gradient(grads, w_in_all, normed, tokens, grad_y, gain):
+    length = tokens.shape[0]
+    whole = pl.BlockSpec((length, D), lambda p: (0, 0))
+    row = pl.BlockSpec((1, D), lambda p: (0, 0))
+    call = pl.pallas_call(
+        partial(input_kernel, calls=len(grads)),
+        grid=(3,),
+        in_specs=[pl.BlockSpec((1, length, grad.shape[2]), lambda p: (p, 0, 0)) for grad in grads]
+        + [pl.BlockSpec((D, D), lambda p: (p, 0)), whole, whole, whole, row],
+        out_specs=[whole, row],
+        out_shape=[jax.ShapeDtypeStruct((length, D), bf16), jax.ShapeDtypeStruct((1, D), f32)],
+        scratch_shapes=[pltpu.VMEM((length, D), f32)],
+        compiler_params=pltpu.CompilerParams(vmem_limit_bytes=vmem_bytes),
+        cost_estimate=pl.CostEstimate(
+            flops=2 * length * D * QKV, bytes_accessed=20 * length * D, transcendentals=length
+        ),
+        name="input_gradient",
+    )
+    out, ln_grad = call(*grads, w_in_all, normed, tokens, grad_y, gain.reshape(1, D))
+    return (out, ln_grad[0])
 
 
 def split(values):
@@ -331,11 +405,7 @@
     return (high, (values - high.astype(f32)).astype(bf16))
 
 
-def newton_kernel(g_ref, x_ref, *refs, sweeps, opening, closing, rate):
-    if closing:
-        w_ref, o_ref, gh, gl, sh, sl, ph, pw, g32, x32 = refs
-    else:
-        g32, x32, gh, gl, sh, sl, ph, pw = refs
+def newton_kernel(g_ref, x_ref, o_ref, gh, gl, sh, sl, ph, pw, g32, x32):
     count = D // tile_rows
 
     def span(i):
@@ -368,8 +438,6 @@
 
         def keep_gram(i, j, value):
             g32[span(i), span(j)] = value
-            if i != j:
-                g32[span(j), span(i)] = value.T
             store(gh, gl, i, j, value)
 
         symmetric(gh, gl, gh, gl, keep_factor)
@@ -379,56 +447,48 @@
             symmetric(gh, gl, ph, pw, partial(store, sh, sl))
             symmetric(sh, sl, ph, pw, keep_gram)
 
-    if opening:
-        half = D // 2
-        corner, side = g_ref[:half, :half], g_ref[:half, half:]
-        i = lax.broadcasted_iota(jnp.int32, (half, half), 0)
-        j = lax.broadcasted_iota(jnp.int32, (half, half), 1)
-        corner_t = corner.T
-        first = jnp.where(i <= j, corner, corner_t)
-        last = jnp.where(i > j, corner, jnp.where(i == j, g_ref[half : half + 1, :half], corner_t))
-        trace = jnp.sum(jnp.where(i == j, first + last, 0.0), axis=0, keepdims=True)
-        trace = jnp.sum(trace, axis=1, keepdims=True)
-        inverse = 1.0 / (jnp.sqrt(trace) + 1e-07)
-        square = inverse * inverse
-        g32[:half, :half] = first * square
-        g32[half:, half:] = last * square
-        g32[:half, half:] = side * square
-        g32[half:, :half] = side.T * square
-        x32[...] = x_ref[...] * inverse
-    else:
-        g32[...] = g_ref[...]
-        x32[...] = x_ref[...]
+    half = D // 2
+    corner, side = g_ref[:half, :half], g_ref[:half, half:]
+    i = lax.broadcasted_iota(jnp.int32, (half, half), 0)
+    j = lax.broadcasted_iota(jnp.int32, (half, half), 1)
+    corner_t = corner.T
+    first = jnp.where(i <= j, corner, corner_t)
+    last = jnp.where(i > j, corner, jnp.where(i == j, g_ref[half : half + 1, :half], corner_t))
+    trace = jnp.sum(jnp.where(i == j, first + last, 0.0), axis=0, keepdims=True)
+    trace = jnp.sum(trace, axis=1, keepdims=True)
+    inverse = 1.0 / (jnp.sqrt(trace) + 1e-07)
+    square = inverse * inverse
+    g32[:half, :half] = first * square
+    g32[half:, half:] = last * square
+    g32[:half, half:] = side * square
+    g32[half:, :half] = side.T * square
+    x32[...] = x_ref[...] * inverse
     gh[...], gl[...] = split(g32[...])
-    plain = sweeps - 1 if closing else sweeps
-    if plain > 1:
-        pl.loop(0, plain)(lambda k: sweep(False))
-    elif plain == 1:
+
+    @pl.loop(0, 4)
+    def _(k):
         sweep(False)
-    if closing:
-        sweep(True)
-        o_ref[...] = w_ref[...].astype(f32) * (1 - muon_rate * muon_decay) - rate * x32[...]
-
-
-def newton(gram, momentum, sweeps, opening=False, weights=None, rate=None):
+
+    sweep(True)
+    o_ref[...] = x32[...].astype(bf16)
+
+
+def newton(folded, momentum):
     rows = momentum.shape[0]
     whole = pl.BlockSpec(memory_space=pltpu.VMEM)
-    state = [pltpu.VMEM((D, D), f32), pltpu.VMEM((rows, D), f32)]
-    parts = [pltpu.VMEM((D, D), bf16)] * 6
-    closing = weights is not None
-    moved = jax.ShapeDtypeStruct((rows, D), f32)
-    return pl.pallas_call(
-        partial(newton_kernel, sweeps=sweeps, opening=opening, closing=closing, rate=rate),
-        in_specs=[whole] * (3 if closing else 2),
-        out_specs=whole if closing else [whole] * 2,
-        out_shape=moved if closing else [jax.ShapeDtypeStruct((D, D), f32), moved],
-        scratch_shapes=parts + state if closing else parts,
+    call = pl.pallas_call(
+        newton_kernel,
+        in_specs=[whole] * 2,
+        out_specs=whole,
+        out_shape=jax.ShapeDtypeStruct((rows, D), bf16),
+        scratch_shapes=[pltpu.VMEM((D, D), bf16)] * 6 + [pltpu.VMEM((D, D), f32), pltpu.VMEM((rows, D), f32)],
         compiler_params=pltpu.CompilerParams(vmem_limit_bytes=vmem_bytes),
         cost_estimate=pl.CostEstimate(
-            flops=6 * D * D * (2 * D + rows) * sweeps, bytes_accessed=8 * D * D + 10 * rows * D, transcendentals=0
+            flops=30 * D * D * (2 * D + rows), bytes_accessed=4 * D * D + 6 * rows * D, transcendentals=0
         ),
         name="newton",
-    )(gram, momentum, *([weights] if closing else []))
+    )
+    return call(folded, momentum)
 
 
 def gram_kernel(m_ref, extra_ref, core_ref, o_ref):
@@ -458,7 +518,7 @@
 def folded_gram(rows, extra, core):
     rows = jnp.pad(rows, ((0, -rows.shape[0] % 16), (0, 0)))
     whole = pl.BlockSpec(memory_space=pltpu.VMEM)
-    return pl.pallas_call(
+    call = pl.pallas_call(
         gram_kernel,
         in_specs=[whole, whole, core_spec],
         out_specs=whole,
@@ -468,12 +528,8 @@
             flops=4 * rows.shape[0] * D * D, bytes_accessed=8 * rows.shape[0] * D, transcendentals=0
         ),
         name="gram",
-    )(rows, extra, core)
-
-
-def swap(values, axis, bit):
-    size = lax.axis_size(axis)
-    return lax.ppermute(values, axis, [(i, i ^ bit) for i in range(size)])
+    )
+    return call(rows, extra, core)
 
 
 def bits(size):
@@ -489,72 +545,90 @@
 
 
 def exchange(values, axis, bit, fill=()):
-    return after(swap(values, axis, bit), *fill)
-
-
-def sum_over(values, halving, full, fills=()):
-    fills = list(fills)
-
-    def step(sent, axis, bit):
-        fill = fills.pop(0)(sent) if fills else ()
-        return exchange(sent, axis, bit, fill)
-
+    size = lax.axis_size(axis)
+    return after(lax.ppermute(values, axis, [(i, i ^ bit) for i in range(size)]), *fill)
+
+
+def sum_steps(values, halving, full):
+    columns = values.shape[1]
+    fill = yield values
     sides = []
     for axis, bit in halving:
         side = (lax.axis_index(axis) // bit) % 2
-        pieces = values.reshape(2, values.shape[0] // 2, values.shape[1])
-        values = take(pieces, side, 0) + step(take(pieces, 1 - side, 0), axis, bit)
+        pieces = values.reshape(2, values.shape[0] // 2, columns)
+        values = take(pieces, side, 0) + exchange(take(pieces, 1 - side, 0), axis, bit, fill)
         sides.append(side)
+        fill = yield values
     for axis, bit in full:
-        values = values + step(values, axis, bit)
+        values = values + exchange(values, axis, bit, fill)
+        fill = yield values
     for (axis, bit), side in zip(reversed(halving), reversed(sides), strict=True):
-        values = join(values, step(values, axis, bit), side, 0).reshape(-1, values.shape[1])
-    return join(values, step(values, "nar", 1), lax.axis_index("nar") % 2, 1).reshape(values.shape[0], -1)
-
-
-def halve(values, axis, name, bit, fill):
+        values = join(values, exchange(values, axis, bit, fill), side, 0).reshape(-1, columns)
+        fill = yield values
+    other = exchange(values, "nar", 1, fill)
+    yield join(values, other, lax.axis_index("nar") % 2, 1).reshape(values.shape[0], -1)
+
+
+def halve(parts, axis, name, bit):
     side = (lax.axis_index(name) // bit) % 2
-    other = exchange(take(values, 1 - side, axis), name, bit, fill)
-    return (take(values, side, axis).astype(f32) + other.astype(f32)).astype(bf16)
-
-
-def scatter_stages(values):
+    sent = [take(part, 1 - side, axis) for part in parts]
+
+    def receive(*fill):
+        kept = jnp.concatenate([take(part, side, axis) for part in parts], axis=0)
+        return (kept, exchange(jnp.concatenate(sent, axis=0), name, bit, fill))
+
+    return sent, receive
+
+
+def added(kept, other):
+    return (kept.astype(f32) + other.astype(f32)).astype(bf16)
+
+
+def scatter_one(*parts):
+    wide = lax.axis_size("wide")
+    columns = parts[0].shape[-1]
+    rows = sum(part.size for part in parts) // (2 * wide * columns)
+    cut = rows // 32 * 16
+    parts = [part.reshape(-1, 2, 2, rows, columns) for part in parts]
+    sent_a, receive_a = halve([part[:, :, :, :cut] for part in parts], 1, "wide", 1)
+    sent_b, receive_b = halve([part[:, :, :, cut:] for part in parts], 2, "nar", 2)
+    return sent_a + sent_b, lambda *fill: (added(*receive_a(*fill)), added(*receive_b(*fill)))
+
+
+def scatter_two(held):
+    sent_a, receive_a = halve(held[:1], 1, "nar", 2)
+    sent_b, receive_b = halve(held[1:], 1, "wide", 1)
+
+    def receive(*fill):
+        kept, other = zip(receive_a(*fill), receive_b(*fill), strict=True)
+        return added(jnp.concatenate(kept, axis=1), jnp.concatenate(other, axis=1))
+
+    return sent_a + sent_b, receive
+
+
+def scatter_rest(held):
     wide = lax.axis_size("wide")
     far = wide // 2
-    rows, columns = values.shape[0] // (2 * wide), values.shape[1]
-    cut = rows // 32 * 16
     place = lax.axis_index("wide") // 2
-    values = values.reshape(far, 2, 2, rows, columns)
-
-    def one(*fill):
-        return (
-            halve(values[:, :, :, :cut], 1, "wide", 1, fill),
-            halve(values[:, :, :, cut:], 2, "nar", 2, fill),
-        )
-
-    def two(held, *fill):
-        return jnp.concatenate(
-            [halve(held[0], 1, "nar", 2, fill), halve(held[1], 1, "wide", 1, fill)], axis=1
-        )
-
-    def rest(held, *fill):
+    sent = [take(held, (place + shift) % far, 0) for shift in range(1, far)]
+
+    def receive(*fill):
         total = take(held, place, 0).astype(f32)
         for shift in range(1, far):
             pairs = [(i, (i // 2 + shift) % far * 2 + i % 2) for i in range(wide)]
-            sent = take(held, (place + shift) % far, 0)
-            total = total + after(lax.ppermute(sent, "wide", pairs), *fill).astype(f32)
+            total = total + after(lax.ppermute(sent[shift - 1], "wide", pairs), *fill).astype(f32)
         return total.astype(bf16)
 
-    return one, two, rest
-
-
-def both_cores(values):
-    other = swap(values, "nar", 1)
+    return sent, receive
+
+
+def both_cores(values, *fill):
+    other = exchange(values, "nar", 1, fill)
     return join(values, other, lax.axis_index("nar") % 2, 1).reshape(values.shape[0], D)
 
 
 def both_chips(values):
-    return join(values, swap(values, "nar", 2), lax.axis_index("nar") // 2, 0).reshape(-1, D)
+    return join(values, exchange(values, "nar", 2), lax.axis_index("nar") // 2, 0).reshape(-1, D)
 
 
 def join(values, other, side, axis):
@@ -576,12 +650,12 @@
         )
     cut = rows // 32 * 16
     first, second = held[:, :cut], held[:, cut:]
-    first = join(first, swap(first, "wide", 1), side, 1)
-    second = join(second, swap(second, "nar", 2), chip, 1)
-    first = join(first, swap(first, "nar", 2), chip, 2)
-    second = join(second, swap(second, "wide", 1), side, 1)
+    first = join(first, exchange(first, "wide", 1), side, 1)
+    second = join(second, exchange(second, "nar", 2), chip, 1)
+    first = join(first, exchange(first, "nar", 2), chip, 2)
+    second = join(second, exchange(second, "wide", 1), side, 1)
     held = jnp.concatenate([first, second], axis=3)
-    return join(held, swap(held, "nar", 1), core, 3).reshape(-1, D)
+    return join(held, exchange(held, "nar", 1), core, 3).reshape(-1, D)
 
 
 def on_device(tokens, cotangent, image_ids, w_in, w_out, gains, mom_in, mom_out, gain_m, gain_v):
@@ -610,54 +684,78 @@
 
     core = (nar_place % 2).reshape(1)
     chip = nar_place // 2
-    w_qkv = w_in_all[:QKV]
-    w_att = w_out_all[:D]
-    joined = contract(x_low, w_qkv, 1, 1).astype(bf16)
-    dattended = contract(grad_y, w_att, 1, 1).astype(bf16)
+    half = D // 2
+    pairs = D // pair
     q_gain, k_gain = gains[D : D + HEAD], gains[D + HEAD :]
-    attended, terms, exact, inverse_sum, keep_att, send_att = attention_forward(
-        joined, image_ids.reshape(row_count), q_gain, k_gain, grad_y, core
-    )
-    mlp_result, mlp_normed, keep_up, send_up, keep_down, send_down = mlp(
-        after(x_low, keep_att), grad_y, w_in_all, w_out_all, core
-    )
-
-    def backward(begin, count, *earlier):
-        return attention_backward(
-            joined, dattended, terms, exact, inverse_sum, q_gain, k_gain, after(x_low, *earlier), core, begin, count
-        )
-
-    def cores(keep, send, *fill):
-        other = exchange(send, "nar", 1, fill)
-        return (keep.astype(f32) + other.astype(f32)).astype(bf16).reshape(-1, D // 2)
-
-    pairs = D // pair
+    dattended = contract(grad_y, w_out_all[:D], 1, 1).astype(bf16)
+    w_in_all = after(w_in_all, dattended)
+    joined = contract(x_low, w_in_all[:QKV], 1, 1).astype(bf16)
     first = rows_in * 4 // 7
     second = rows_in - first
-    parted = wide_count == 8 and first == D // 2 and rows_in == 672
+    parted = wide_count == 8 and first == half and rows_in == 672
+    segments = [(0, FIN - QKV, 0)]
+    if parted:
+        segments = [(0, first, 0)]
+        for i in range(4):
+            segments += [(rows_in * i + first, rows_in * (i + 1), 1), (rows_in * (i + 1), rows_in * (i + 1) + first, 0)]
+    mlp_result, mlp_normed, keep_down, send_down, *up_parts = mlp(
+        x_low, grad_y, w_in_all, w_out_all, core, segments
+    )
+    attended, terms, exact, inverse_sum, keep_att, send_att = attention_forward(
+        after(joined, keep_down), image_ids.reshape(row_count), q_gain, k_gain, grad_y, core
+    )
+
+    def backward(begin, count, earlier=(), **buffers):
+        return attention_backward(
+            joined, dattended, terms, exact, inverse_sum, q_gain, k_gain, after(x_low, *earlier), core, begin, count,
+            **buffers,
+        )
+
+    def cores(keep, send, *fill):
+        return added(keep, exchange(send, "nar", 1, fill)).reshape(-1, half)
+
     start = 96 * jnp.minimum(lax.axis_index("wide"), 3)
     row = lax.broadcasted_iota(jnp.int32, (rows_in, 1), 0)
-    hidden = keep_up.shape[0]
+    half_out = lax.dynamic_slice_in_dim(mom_out, chip * (rows_out // 2), rows_out // 2, 0)
+    wide_bits = bits(wide_count)
+    halving = [("wide", wide_bits[0]), ("nar", 2)]
+    full = [("wide", bit) for bit in wide_bits[1:]]
+
+    def begin_out(part):
+        zeros = jnp.zeros((extra_rows, half), f32)
+        steps = sum_steps(folded_gram(muon_beta * half_out + part.astype(f32), zeros, core), halving, full)
+        return (steps, next(steps))
+
     if parted:
-        grads_a, keep_a, send_a, q_grad_a, k_grad_a = backward(0, pairs // 2, keep_up)
-        up = cores(keep_up, send_up, keep_a)
-        out = jnp.concatenate([cores(keep_att, send_att, keep_a), cores(keep_down, send_down, keep_a)], axis=0)
-        out_one, out_two, out_rest = scatter_stages(out)
-        grads_b, keep_b, send_b, q_grad_b, k_grad_b = backward(pairs // 2, pairs // 2, keep_a, out)
-        held_a = cores(keep_a, send_a, keep_b)
-        held_a = [held_a, up[:first]] + [up[rows_in * i : rows_in * i + first] for i in range(1, 5)]
-        a_one, a_two, a_rest = scatter_stages(jnp.concatenate(held_a, axis=0))
-        held_out = out_one(keep_b)
-        held_b = cores(keep_b, send_b)
-        held_b = [held_b] + [up[rows_in * i + first : rows_in * (i + 1)] for i in range(4)]
-        b_one, b_two, b_rest = scatter_stages(jnp.concatenate(held_b, axis=0))
-        held_out = out_two(held_out)
-        held_a = a_one()
-        part_out = out_rest(held_out)
-        part_a = a_rest(a_two(held_a))
-        part_b = b_rest(b_two(b_one()))
-        q_gain_grad, k_gain_grad = q_grad_a + q_grad_b, k_grad_a + k_grad_b
-        grad_qkv = [a for pieces in zip(grads_a, grads_b, strict=True) for a in pieces]
+        keep_up_a, send_up_a, keep_up_b, send_up_b = up_parts
+        down = cores(keep_down, send_down, keep_att)
+        up_a = cores(keep_up_a, send_up_a, keep_att)
+        up_b = cores(keep_up_b, send_up_b, keep_att)
+        att = cores(keep_att, send_att)
+        sent, receive = scatter_one(jnp.concatenate([att, down], axis=0))
+        dqkv_a, keep_a, send_a, q_grad_a, k_grad_a = backward(0, 3, [up_a, up_b, *sent], room=3)
+        sent, receive = scatter_two(receive(keep_a))
+        dqkv_b, keep_b, send_b, q_grad_b, k_grad_b = backward(3, 1, [keep_a, *sent], room=3)
+        sent_o, receive_o = scatter_rest(receive(keep_b))
+        added_a = cores(keep_a, send_a, keep_b)
+        sent_a, receive_a = scatter_one(jnp.concatenate([added_a, up_a], axis=0))
+        dqkv_c, keep_b, send_b, q_grad_c, k_grad_c = backward(
+            4, 2, [*sent_a, *sent_o], room=3, place=1, into=(keep_b, send_b)
+        )
+        sent_a, receive_a = scatter_two(receive_a(keep_b))
+        added_b = cores(keep_b, send_b, *sent_a)
+        sent_b, receive_b = scatter_one(added_b, up_b)
+        sent_a, receive_a = scatter_rest(receive_a(*sent_b))
+        part_out = both_cores(receive_o(*sent_a), *sent_a)
+        sent_b, receive_b = scatter_two(receive_b(*sent_a))
+        steps_out, folded_out = begin_out(after(part_out, *sent_b))
+        sent_b, receive_b = scatter_rest(receive_b(folded_out))
+        dqkv = [dqkv_a, dqkv_b, dqkv_c]
+        grad_tokens, ln_grad = input_gradient(dqkv, w_in_all, after(mlp_normed, *sent_b), tokens, grad_y, ln_gain)
+        part_a = receive_a(grad_tokens)
+        part_b = receive_b(grad_tokens)
+        folded_out = steps_out.send((part_b,))
+        q_gain_grad, k_gain_grad = q_grad_a + q_grad_b + q_grad_c, k_grad_a + k_grad_b + k_grad_c
         part_in = jnp.concatenate([part_a, part_b], axis=0)
 
         def halved(rows):
@@ -681,67 +779,67 @@
             return jnp.where(inside, a, jnp.where(row < start, below, above))
 
     else:
-        grad_qkv, keep_a, send_a, q_gain_grad, k_gain_grad = backward(0, pairs, keep_up)
-        out = jnp.concatenate([cores(keep_att, send_att), cores(keep_down, send_down)], axis=0)
-        out_one, out_two, out_rest = scatter_stages(out)
-        part_out = out_rest(out_two(out_one()))
-        both = jnp.concatenate([cores(keep_a, send_a), cores(keep_up, send_up)], axis=0)
-        in_one, in_two, in_rest = scatter_stages(both)
-        part_in = in_rest(in_two(in_one()))
+        keep_up, send_up = up_parts
+        dqkv, keep_a, send_a, q_gain_grad, k_gain_grad = backward(0, pairs, room=pairs)
+        grad_tokens, ln_grad = input_gradient([dqkv], w_in_all, mlp_normed, tokens, grad_y, ln_gain)
+
+        def scattered(*parts):
+            held = scatter_one(jnp.concatenate(parts, axis=0))[1]()
+            return scatter_rest(scatter_two(held)[1]())[1]()
+
+        part_out = both_cores(scattered(cores(keep_att, send_att), cores(keep_down, send_down)))
+        steps_out, folded_out = begin_out(part_out)
+        part_in = scattered(cores(keep_a, send_a), cores(keep_up, send_up))
 
         def halved(rows):
             return lax.dynamic_slice_in_dim(rows, chip * (rows_in // 2), rows_in // 2, 0)
 
         rejoined = both_chips
 
-    grad_qkv = jnp.concatenate(grad_qkv, axis=1)
-    result = (x_float + (mlp_result + nn(attended, w_att))).astype(bf16)
-    grad_normed = mlp_normed + nn(grad_qkv, w_qkv)
-    ln_grad = jnp.sum(grad_normed * x_hat, axis=0)
-    grad_tokens = (
-        grad_y.astype(f32) + norm_backward(grad_normed * ln_gain, x_hat, x_inverse)
-    ).astype(bf16)
-
-    wide_bits = bits(wide_count)
-    halving = [("wide", wide_bits[0]), ("nar", 2)]
-    full = [("wide", bit) for bit in wide_bits[1:]]
+    part_in = both_cores(part_in)
     gain_terms = jnp.concatenate([ln_grad, q_gain_grad, k_gain_grad])
     count = gain_terms.shape[0]
-    half = D // 2
     extra = jnp.pad(gain_terms, (half, (extra_rows - 1) * half - count)).reshape(extra_rows, half)
-
-    part_out = both_cores(part_out)
-    half_out = lax.dynamic_slice_in_dim(mom_out, chip * (rows_out // 2), rows_out // 2, 0)
-    folded_out = sum_over(
-        folded_gram(muon_beta * half_out + part_out.astype(f32), jnp.zeros_like(extra), core), halving, full
-    )
-    grad_w_out = both_chips(part_out).astype(f32)
+    steps_in = sum_steps(folded_gram(muon_beta * halved(mom_in) + part_in.astype(f32), extra, core), halving, full)
+    folded_in = next(steps_in)
+    summed = []
+    while folded_in.shape[1] < D:
+        folded_in = steps_in.send(())
+        summed.append(folded_in)
+        if folded_out.shape[1] < D:
+            folded_out = steps_out.send((folded_in,))
+    grad_w_out = both_chips(after(part_out, summed[0])).astype(f32)
     mom_out_new = muon_beta * mom_out + grad_w_out
-
-    part_in = both_cores(part_in)
-    state = [folded_out, mom_out_new]
-
-    def sweeps_out(opening):
-        def fill(sent):
-            state[:] = newton(after(state[0], sent), state[1], 1, opening=opening)
-            return (state[1],)
-
-        return fill
-
-    folded_in = sum_over(
-        folded_gram(muon_beta * halved(mom_in) + part_in.astype(f32), extra, core),
-        halving,
-        full,
-        [sweeps_out(i == 0) for i in range(4)],
-    )
-    grad_w_in = rejoined(part_in).astype(f32)
+    grad_w_in = rejoined(after(part_in, summed[1])).astype(f32)
     mom_in_new = muon_beta * mom_in + grad_w_in
     extra = (folded_in[half:, :half] + folded_in[half:, half:]).reshape(extra_rows * half)
     grad_gains = extra[half : half + count]
-    w_out_new = newton(*state, 1, weights=w_out, rate=muon_rate * (FOUT / D) ** 0.5)
-    w_in_new = newton(
-        folded_in, mom_in_new, 5, opening=True, weights=w_in, rate=muon_rate * (FIN / D) ** 0.5
-    )
+
+    half_in, half_out = rows_in // 2, rows_out // 2
+    rows = jnp.where(
+        chip == 0,
+        lax.dynamic_slice_in_dim(mom_in_new, core[0] * half_in, half_in, 0),
+        jnp.pad(
+            lax.dynamic_slice_in_dim(mom_out_new, core[0] * half_out, half_out, 0), ((0, half_in - half_out), (0, 0))
+        ),
+    )
+    ortho = newton(jnp.where(chip == 0, folded_in, folded_out), rows)
+    branch = mlp_result + nn(after(attended, ortho), w_out_all[:D])
+    result = (tokens.astype(f32) + branch).astype(bf16)
+    other = exchange(ortho, "nar", 2, (result,))
+    ortho_in = jnp.where(chip == 0, ortho, other)
+    ortho_out = jnp.where(chip == 0, other, ortho)[:half_out]
+    ortho = jnp.concatenate([ortho_in, ortho_out], axis=0)
+    other = exchange(ortho, "nar", 1)
+    ortho_in = join(ortho[:half_in], other[:half_in], core[0], 0).reshape(rows_in, D)
+    ortho_out = join(ortho[half_in:], other[half_in:], core[0], 0).reshape(rows_out, D)
+
+    def updated(weights, ortho, size):
+        rate = muon_rate * (size / D) ** 0.5
+        return weights.astype(f32) * (1 - muon_rate * muon_decay) - rate * ortho.astype(f32)
+
+    w_in_new = updated(w_in, ortho_in, FIN)
+    w_out_new = updated(w_out, ortho_out, FOUT)
     gain_m_new = adam_first * gain_m + (1 - adam_first) * grad_gains
     gain_v_new = adam_second * gain_v + (1 - adam_second) * grad_gains * grad_gains
     gains_new = gains - adam_rate * (gain_m_new / (1 - adam_first**STEP)) / (

time: 499 us -> 470 us (0.942)
  Pallas kernels: 204 us -> 167 us
  other arithmetic: 38.9 us -> 50.7 us
  waiting for transfers between devices: 108 us -> 119 us
  starting transfers between devices: 69.4 us -> 61.5 us
  matrix products: 23.1 us -> 16.7 us
    pallas_call x12 -> x9, Pallas kernels: 204 us -> 167 us  [the longest x3 47.5 us: attention_backward(): call(joined, joined, joined, dattended, terms, exact, inverse_sum, q_gain...]
    ppermute x50 -> x53, waiting for transfers between devices: 78.8 us -> 92.6 us  [the longest x44 89.8 us: exchange(): lax.ppermute(values, axis, [(i, i ^ bit) for i in range(size)])]
    squeeze x11 -> x21, local copies, waits for them, and re-layouts: 3.23 us -> 12.9 us  [take(): return lax.dynamic_index_in_dim(values, index, axis, keepdims=False)]
    ppermute x50 -> x53, starting transfers between devices: 62.3 us -> 54.4 us  [the longest x44 37.7 us: exchange(): lax.ppermute(values, axis, [(i, i ^ bit) for i in range(size)])]
    dot_general x2 -> x1, matrix products: 11.8 us -> 5.31 us  [nn(): return jnp.dot(a, b, preferred_element_type=f32)]
    convert_element_type x20 -> x18, other arithmetic: 13.8 us -> 19.2 us  [the longest x15 17 us: added(): return (kept.astype(f32) + other.astype(f32)).astype(bf16)]
    unnamed x114 -> x105, local copies, waits for them, and re-layouts: 13.1 us -> 8.81 us
    another operation x27 -> x29, other arithmetic: 8.07 us -> 10 us  [join(): return jnp.stack(ordered, axis)]
  transfers between devices with their start and end apart: 54 -> 57, of which waited for: 21 -> 24; matrix products, arithmetic and copies ran while one was open for 16% -> 15% of each run, Pallas kernels for 21% -> 18%
where the time goes in v3:
time: 470 us; the launch traced here: 463 us
  Pallas kernels  167 us (36%)
  waiting for transfers between devices  119 us (25%)
  starting transfers between devices  61.5 us (13%)
  other arithmetic  50.7 us (11%)
  local copies, waits for them, and re-layouts  32.3 us (7%)
  matrix products  16.7 us (4%)
  between operations  15.8 us (3%)
    ppermute x44, waiting for transfers between devices, exchange(): lax.ppermute(values, axis, [(i, i ^ bit) for i in range(size)])  89.8 us
    pallas_call x3, Pallas kernels, attention_backward(): call(joined, joined, joined, dattended, terms, exact, inverse_sum, q_gain...  47.5 us
    pallas_call x1, Pallas kernels, mlp(): return call(x_low, grad_y, w_in_all, w_out_all, core)  44.9 us
    ppermute x44, starting transfers between devices, exchange(): lax.ppermute(values, axis, [(i, i ^ bit) for i in range(size)])  37.7 us
    pallas_call x1, Pallas kernels, newton(): return call(folded, momentum)  36 us
    pallas_call x1, Pallas kernels, attention_forward(): call(joined, joined, joined, onek, penq, q_gain.reshape(HEAD, 1), k_gain....  19.8 us
    convert_element_type x15, other arithmetic, added(): return (kept.astype(f32) + other.astype(f32)).astype(bf16)  17 us
    ppermute x9, starting transfers between devices, receive(): lax.ppermute(sent[shift - 1], 'wide', pairs)  16.7 us
  transfers between devices with their start and end apart: 57, of which 24 were waited for; matrix products, arithmetic and copies ran while one was open for 15% of the time, Pallas kernels for 18%

profile of v3, /device:TPU:0, one launch (start us, length us, event | category | flops | bytes accessed | tf_op | source)
XLA Modules:
  0.0 463.2 jit_solution(6335211854833938998)
XLA Ops:
  10.0 3.1 collective-permute-start
  13.0 2.6 collective-permute-start.1
  17.0 3.7 collective-permute-done
  20.6 8.9 %collective-permute-done.1 = bf16[120,768]{1,0:T(8,128)(2,1)S(1)} collective-permute-done((bf16[120,768]{1,0:T(8,128)(2,1)S(1)}, bf16[120,768]{1,0:T(8,128)(2,1)S(1)}, u32[]{:S(2)}, u32[]{:S(2)}) %collective-permute-start.1) | collective-permute-done | bytes 184352 | tf_op jit(solution)/shard_map/ppermute | solution.py:649
  32.8 5.5 %collective-permute-done.3 = bf16[4,48,768]{2,1,0:T(8,128)(2,1)S(1)} collective-permute-done((bf16[4,48,768]{2,1,0:T(8,128)(2,1)S(1)}, bf16[4,48,768]{2,1,0:T(8,128)(2,1)S(1)}, u32[]{:S(2)}, u32[]{:S(2)}) %collective-permute-start.3) | collective-permute-done | bytes 294944 | tf_op jit(solution)/shard_map/ppermute | solution.py:549
  38.4 4.7 %collective-permute-done.5 = bf16[4,72,768]{2,1,0:T(8,128)(2,1)S(1)} collective-permute-done((bf16[4,72,768]{2,1,0:T(8,128)(2,1)S(1)}, bf16[4,72,768]{2,1,0:T(8,128)(2,1)S(1)}, u32[]{:S(2)}, u32[]{:S(2)}) %collective-permute-start.5) | collective-permute-done | bytes 442400 | tf_op jit(solution)/shard_map/ppermute | solution.py:549
  45.2 19.2 %collective-permute-done.4 = bf16[4,2,48,768]{3,2,0,1:T(8,128)(2,1)S(1)} collective-permute-done((bf16[4,2,48,768]{3,2,0,1:T(8,128)(2,1)S(1)}, bf16[4,2,48,768]{3,2,0,1:T(8,128)(2,1)S(1)}, u32[]{:S(2)}, u32[]{:S(2)}) %collective-permute-start.4) | collective-permute-done | bytes 589856 | tf_op jit(solution)/shard_map/ppermute | solution.py:549
  64.6 2.5 collective-permute-done.6
  76.9 2.5 select_bitcast_fusion.1
  79.4 3.0 pad_maximum_fusion
  82.3 3.9 convolution_convert_fusion.1.do_ref
  86.2 13.7 %all-gather.2.cloned.1.call-done.wu_ref.refs_3_ = bf16[5376,768]{1,0:T(8,128)(2,1)} async-done(((bf16[168,768]{1,0:T(8,128)(2,1)}), bf16[5376,768]{1,0:T(8,128)(2,1)}) %all-gather.2.cloned.1.call-update) | async-done | bytes 8257552 | tf_op jit(solution)/shard_map/all_gather | solution.py:675
  99.9 7.5 %convolution_convert_fusion.q_ref.k_ref.v_ref = bf16[1024,2304]{1,0:T(8,128)(2,1)} fusion(bf16[1024,768]{1,0:T(8,128)(2,1)S(1)} %fusion.5.x_ref, bf16[5376,768]{1,0:T(8,128)(2,1)} %all-gather.2.cloned.1.call-done.wu_ref.refs_3_), kind=kOutput, calls=%fused_computation.1 | convolution fusion | flops 3626237952 | bytes 9830400 | tf_op jit(solution)/shard_map/dot_general | solution.py:57
  107.4 44.9 %mlp.1 = (f32[1024,768]{1,0:T(8,128)}, f32[1024,768]{1,0:T(8,128)}, bf16[3072,384]{1,0:T(8,128)(2,1)}, bf16[3072,384]{1,0:T(8,128)(2,1)}, bf16[1920,384]{1,0:T(8...) custom-call(bf16[1024,768]{1,0:T(8,128)(2,1)} %copy-done.2, ...), custom_call_target="tpu_custom_call" | custom-call | flops 43486543872 | bytes 28311552 | tf_op jit(solution)/shard_map/mlp/pallas_call | solution.py:353
  152.6 19.8 %attention_forward.1 = (bf16[1024,768]{1,0:T(8,128)(2,1)}, bf16[12,1024,1024]{2,1,0:T(8,128)(2,1)}, f32[768,1024]{1,0:T(8,128)}, f32[6,8,1024]{2,1,0:T(8,128)}, ...) custom-call(bf16[1024,2304]{1,0:T(8,128)(2,1)} %convolution_convert_fusion.q_ref.k_ref.v_ref, ...), custom_call_target="tpu_custom_call" | custom-call | flops 12884901888 | bytes 37748736 | tf_op jit(solution)/shard_map/attention_forward/pallas_call | solution.py:160
  180.9 1.9 add_convert_fusion.1
  183.0 2.3 add_convert_fusion
  187.2 2.0 collective-permute-start.14
  190.5 21.7 %attention_backward.3 = (bf16[3,1024,384]{2,1,0:T(8,128)(2,1)}, bf16[3,384,384]{2,1,0:T(8,128)(2,1)}, bf16[3,384,384]{2,1,0:T(8,128)(2,1)}, f32[64,128]{1,0:T(8,128)}, f32[64,128]{1,0:T(8,128)}) custom-call(bf16[1024,2304]{1,0:T(8,128)(2,1)} %convolution_convert_fusion.q_ref.k_ref.v_ref, bf16[1024,2304]{1,0:T(8,128)(2,1)} %convolution_convert_fusion.q_ref.k_ref.v_ref, ...), custom_call_target="tpu_custom_call" | custom-call | flops 12884901888 | bytes 22020096 | tf_op jit(solution)/shard_map/attention_backward/pallas_call | solution.py:267
  219.3 9.9 %attention_backward.4 = (bf16[3,1024,128]{2,1,0:T(8,128)(2,1)}, bf16[3,384,384]{2,1,0:T(8,128)(2,1)}, bf16[3,384,384]{2,1,0:T(8,128)(2,1)}, f32[64,128]{1,0:T(8,128)}, f32[64,128]{1,0:T(8,128)}) custom-call(bf16[1024,2304]{1,0:T(8,128)(2,1)} %convolution_convert_fusion.q_ref.k_ref.v_ref, bf16[1024,2304]{1,0:T(8,128)(2,1)} %convolution_convert_fusion.q_ref.k_ref.v_ref, ...), custom_call_target="tpu_custom_call" | custom-call | flops 4294967296 | bytes 7340032 | tf_op jit(solution)/shard_map/attention_backward/pallas_call | solution.py:267
  237.5 15.9 %attention_backward.5 = (bf16[3,1024,256]{2,1,0:T(8,128)(2,1)}, bf16[3,384,384]{2,1,0:T(8,128)(2,1)}, bf16[3,384,384]{2,1,0:T(8,128)(2,1)}, f32[64,128]{1,0:T(8,128)}, f32[64,128]{1,0:T(8,128)}) custom-call(bf16[1024,2304]{1,0:T(8,128)(2,1)} %convolution_convert_fusion.q_ref.k_ref.v_ref, ...), custom_call_target="tpu_custom_call", output_to_operand_aliasing={{1}: (11, {}), {2}: (12, {})} | custom-call | flops 8589934592 | bytes 14680064 | tf_op jit(solution)/shard_map/attention_backward/pallas_call | solution.py:267
  254.8 4.7 %collective-permute-start.26 = (bf16[240,384]{1,0:T(8,128)(2,1)}, bf16[240,384]{1,0:T(8,128)(2,1)S(1)}, u32[]{:S(2)}, u32[]{:S(2)}) collective-permute-start(bf16[240,384]{1,0:T(8,128)(2,1)} %get-tuple-element.206), channel_id=1, source_target_pairs={{0,2},{1,3},{2,4},{3,5},{4,6},{5,7},{6,0},{7,1},{8,10},{9,11},{10,... | collective-permute-start | bytes 552968 | tf_op jit(solution)/shard_map/ppermute | solution.py:619
  259.5 2.4 collective-permute-start.28
  265.2 2.0 collective-permute-start.21
  267.6 4.5 collective-permute-done.19
  272.1 1.9 collective-permute-done.21
  277.9 1.8 collective-permute-start.22
  279.8 3.3 collective-permute-start.31
  283.6 4.0 collective-permute-done.23
  290.0 7.1 %collective-permute-done.24 = bf16[4,2,80,384]{3,2,1,0:T(8,128)(2,1)S(1)} collective-permute-done((bf16[4,2,80,384]{3,2,1,0:T(8,128)(2,1)S(1)}, bf16[4,2,80,384]{3,2,1,0:T(8,128)(2,1)S(1)}, u32[]{:S(2)}, u32[]{:S(2)}) %collective-permute-start.24) | collective-permute-done | bytes 491552 | tf_op jit(solution)/shard_map/ppermute | solution.py:549
  299.7 2.8 gram.2
  304.1 2.0 collective-permute-start.44
  308.7 2.0 collective-permute-start.33
  310.8 12.8 %input_gradient.1 = (bf16[1024,768]{1,0:T(8,128)(2,1)}, f32[1,768]{1,0:T(1,128)}) custom-call(bf16[3,1024,384]{2,1,0:T(8,128)(2,1)} %get-tuple-element.125.refs_0_, bf16[3,1024,128]{2,1,0:T(8,128)(2,1)} %get-tuple-element.126.refs_1_, bf16[3,1024,256]{2,1,0:T(8,128)(2,1)} %get-tuple-element.127.refs_2_, ...), custom_call_target="tpu_custom_call" | custom-call | flops 3623878656 | bytes 15728640 | tf_op jit(solution)/shard_map/input_gradient/pallas_call | solution.py:399
  323.8 2.4 collective-permute-start.35
  327.3 2.7 collective-permute-done.34
  334.0 3.6 gram.3
  341.0 6.8 %collective-permute-done.37 = f32[208,384]{1,0:T(8,128)S(1)} collective-permute-done((f32[208,384]{1,0:T(8,128)S(1)}, f32[208,384]{1,0:T(8,128)S(1)}, u32[]{:S(2)}, u32[]{:S(2)}) %collective-permute-start.37) | collective-permute-done | bytes 319520 | tf_op jit(solution)/shard_map/ppermute | solution.py:549
  351.8 3.2 collective-permute-done.38
  361.5 2.2 collective-permute-start.40
  363.7 7.0 %collective-permute-done.47 = f32[104,384]{1,0:T(8,128)} collective-permute-done((f32[104,384]{1,0:T(8,128)S(1)}, f32[104,384]{1,0:T(8,128)}, u32[]{:S(2)}, u32[]{:S(2)}) %collective-permute-start.47) | collective-permute-done | bytes 159776 | tf_op jit(solution)/shard_map/ppermute | solution.py:549
  378.3 3.5 collective-permute-done.41
  382.3 3.3 collective-permute-done.49
  385.8 3.2 collective-permute-done.42
  396.5 36.0 %newton.1 = bf16[336,768]{1,0:T(8,128)(2,1)} custom-call(f32[416,768]{1,0:T(8,128)} %broadcast_select_fusion.1.g_ref, f32[336,768]{1,0:T(8,128)} %pad_select_fusion.x_ref), custom_call_target="tpu_custom_call" | custom-call | flops 33124515840 | bytes 3907584 | tf_op jit(solution)/shard_map/newton/pallas_call | solution.py:491
  433.7 5.3 %fusion.6 = bf16[1024,768]{1,0:T(8,128)(2,1)} fusion(bf16[1024,768]{1,0:T(8,128)(2,1)S(1)} %copy-done.1, f32[1024,768]{1,0:T(8,128)} %get-tuple-element.89, bf16[1024,768]{1,0:T(8,128)(2,1)} %get-tuple-element.162, bf16[3840,768]{1,0:T(8,128)(2,1)} %bitcast.18.wd_ref), kind=kOutput, calls=%fused_computation.12 | convolution fusion | flops 1211105280 | bytes 9043968 | tf_op jit(solution)/shard_map/dot_general | solution.py:53
  439.0 7.9 %collective-permute-done.54 = bf16[336,768]{1,0:T(8,128)(2,1)S(1)} collective-permute-done((bf16[336,768]{1,0:T(8,128)(2,1)}, bf16[336,768]{1,0:T(8,128)(2,1)S(1)}, u32[]{:S(2)}, u32[]{:S(2)}) %collective-permute-start.54) | collective-permute-done | bytes 516128 | tf_op jit(solution)/shard_map/ppermute | solution.py:549
  448.6 2.0 collective-permute-done.55
  (336 shorter events, 108.0 us)
Async XLA Ops:
  7.2 92.7 %all-gather.2.cloned.1.call-start = ((), (), s32[]{:S(2)}) async-start(), calls=%async_computation | async-start | bytes 8515584 | tf_op jit(solution)/shard_map/all_gather | solution.py:675
  10.0 10.7 %collective-permute-start = (bf16[120,768]{1,0:T(8,128)(2,1)S(1)}, bf16[120,768]{1,0:T(8,128)(2,1)S(1)}, u32[]{:S(2)}, u32[]{:S(2)}) collective-permute-start(bf16[120,768]{1,0:T(8,128)(2,1)S(1)} %get-tuple-element.173), channel_id=1, source_target_pairs={{0,2},{1,3},{2,4},{3,5},{4,6},{5,7},{6,0},{7,1},{8,10},{9,11},{10,... | collective-permute-start | bytes 552968 | tf_op jit(solution)/shard_map/ppermute | solution.py:649
  13.0 16.5 %collective-permute-start.1 = (bf16[120,768]{1,0:T(8,128)(2,1)S(1)}, bf16[120,768]{1,0:T(8,128)(2,1)S(1)}, u32[]{:S(2)}, u32[]{:S(2)}) collective-permute-start(bf16[120,768]{1,0:T(8,128)(2,1)S(1)} %get-tuple-element.173), channel_id=1, source_target_pairs={{0,4},{1,5},{2,6},{3,7},{4,0},{5,1},{6,2},{7,3},{8,12},{9,13},{10,... | collective-permute-start | bytes 552968 | tf_op jit(solution)/shard_map/ppermute | solution.py:649
  15.6 14.0 %collective-permute-start.2 = (bf16[120,768]{1,0:T(8,128)(2,1)S(1)}, bf16[120,768]{1,0:T(8,128)(2,1)S(1)}, u32[]{:S(2)}, u32[]{:S(2)}) collective-permute-start(bf16[120,768]{1,0:T(8,128)(2,1)S(1)} %get-tuple-element.173), channel_id=1, source_target_pairs={{0,6},{1,7},{2,0},{3,1},{4,2},{5,3},{6,4},{7,5},{8,14},{9,15},{10,... | collective-permute-start | bytes 552968 | tf_op jit(solution)/shard_map/ppermute | solution.py:649
  29.7 8.7 %collective-permute-start.3 = (bf16[4,48,768]{2,1,0:T(8,128)(2,1)S(1)}, bf16[4,48,768]{2,1,0:T(8,128)(2,1)S(1)}, u32[]{:S(2)}, u32[]{:S(2)}) collective-permute-start(bf16[4,48,768]{2,1,0:T(8,128)(2,1)S(1)} %slice.129), channel_id=1, source_target_pairs={{0,1},{1,0},{2,3},{3,2},{4,5},{5,4},{6,7},{7,6},{8,9},{9,8},{10,11... | collective-permute-start | bytes 884744 | tf_op jit(solution)/shard_map/ppermute | solution.py:549
  31.3 11.8 %collective-permute-start.5 = (bf16[4,72,768]{2,1,0:T(8,128)(2,1)S(1)}, bf16[4,72,768]{2,1,0:T(8,128)(2,1)S(1)}, u32[]{:S(2)}, u32[]{:S(2)}) collective-permute-start(bf16[4,72,768]{2,1,0:T(8,128)(2,1)S(1)} %slice.130), channel_id=1, source_target_pairs={{0,16},{8,24},{16,0},{24,8},{1,17},{9,25},{17,1},{25,9},{2,18},{10... | collective-permute-start | bytes 1327112 | tf_op jit(solution)/shard_map/ppermute | solution.py:549
  43.2 23.8 %collective-permute-start.6 = (bf16[4,2,72,768]{3,2,1,0:T(8,128)(2,1)S(1)}, bf16[4,2,72,768]{3,2,1,0:T(8,128)(2,1)S(1)}, u32[]{:S(2)}, u32[]{:S(2)}) collective-permute-start(bf16[4,2,72,768]{3,2,1,0:T(8,128)(2,1)S(1)} %pad_maximum_fusion.5), channel_id=1, source_target_pairs={{0,1},{1,0},{2,3},{3,2},{4,5},{5,4},{6,7},{7,6},{8,9},{9,8},{10,11... | collective-permute-start | bytes 2654216 | tf_op jit(solution)/shard_map/ppermute | solution.py:549
  43.6 20.8 %collective-permute-start.4 = (bf16[4,2,48,768]{3,2,0,1:T(8,128)(2,1)S(1)}, bf16[4,2,48,768]{3,2,0,1:T(8,128)(2,1)S(1)}, u32[]{:S(2)}, u32[]{:S(2)}) collective-permute-start(bf16[4,2,48,768]{3,2,0,1:T(8,128)(2,1)S(1)} %pad_maximum_fusion.10), channel_id=1, source_target_pairs={{0,16},{8,24},{16,0},{24,8},{1,17},{9,25},{17,1},{25,9},{2,18},{10... | collective-permute-start | bytes 1769480 | tf_op jit(solution)/shard_map/ppermute | solution.py:549
  152.2 30.6 %collective-permute-start.11 = (bf16[3072,384]{1,0:T(8,128)(2,1)}, bf16[3072,384]{1,0:T(8,128)(2,1)}, u32[]{:S(2)}, u32[]{:S(2)}) collective-permute-start(bf16[3072,384]{1,0:T(8,128)(2,1)} %get-tuple-element.104), channel_id=1, source_target_pairs={{0,8},{8,0},{16,24},{24,16},{1,9},{9,1},{17,25},{25,17},{2,10},{10... | collective-permute-start | bytes 7077896 | tf_op jit(solution)/shard_map/ppermute | solution.py:549
  187.2 28.2 %collective-permute-start.14 = (bf16[4,2,128,384]{3,2,1,0:T(8,128)(2,1)}, bf16[4,2,128,384]{3,2,1,0:T(8,128)(2,1)}, u32[]{:S(2)}, u32[]{:S(2)}) collective-permute-start(bf16[4,2,128,384]{3,2,1,0:T(8,128)(2,1)} %dynamic-slice_bitcast_fusion), channel_id=1, source_target_pairs={{0,16},{8,24},{16,0},{24,8},{1,17},{9,25},{17,1},{25,9},{2,18},{10... | collective-permute-start | bytes 2359304 | tf_op jit(solution)/shard_map/ppermute | solution.py:549
  190.1 22.2 %collective-permute-start.13 = (bf16[4,2,112,384]{3,2,1,0:T(8,128)(2,1)}, bf16[4,2,112,384]{3,2,1,0:T(8,128)(2,1)}, u32[]{:S(2)}, u32[]{:S(2)}) collective-permute-start(bf16[4,2,112,384]{3,2,1,0:T(8,128)(2,1)} %dynamic-slice_bitcast_fusion.1), channel_id=1, source_target_pairs={{0,1},{1,0},{2,3},{3,2},{4,5},{5,4},{6,7},{7,6},{8,9},{9,8},{10,11... | collective-permute-start | bytes 2064392 | tf_op jit(solution)/shard_map/ppermute | solution.py:549
  212.3 16.9 %collective-permute-start.12 = (bf16[3,384,384]{2,1,0:T(8,128)(2,1)}, bf16[3,384,384]{2,1,0:T(8,128)(2,1)}, u32[]{:S(2)}, u32[]{:S(2)}) collective-permute-start(bf16[3,384,384]{2,1,0:T(8,128)(2,1)} %get-tuple-element.108), channel_id=1, source_target_pairs={{0,8},{8,0},{16,24},{24,16},{1,9},{9,1},{17,25},{25,17},{2,10},{10... | collective-permute-start | bytes 2654216 | tf_op jit(solution)/shard_map/ppermute | solution.py:549
  215.0 20.2 %collective-permute-start.16 = (bf16[4,112,384]{2,1,0:T(8,128)(2,1)}, bf16[4,112,384]{2,1,0:T(8,128)(2,1)}, u32[]{:S(2)}, u32[]{:S(2)}) collective-permute-start(bf16[4,112,384]{2,1,0:T(8,128)(2,1)} %get-tuple-element.208), channel_id=1, source_target_pairs={{0,16},{8,24},{16,0},{24,8},{1,17},{9,25},{17,1},{25,9},{2,18},{10... | collective-permute-start | bytes 1032200 | tf_op jit(solution)/shard_map/ppermute | solution.py:549
  217.7 17.5 %collective-permute-start.17 = (bf16[4,128,384]{2,1,0:T(8,128)(2,1)}, bf16[4,128,384]{2,1,0:T(8,128)(2,1)}, u32[]{:S(2)}, u32[]{:S(2)}) collective-permute-start(bf16[4,128,384]{2,1,0:T(8,128)(2,1)} %get-tuple-element.199), channel_id=1, source_target_pairs={{0,1},{1,0},{2,3},{3,2},{4,5},{5,4},{6,7},{7,6},{8,9},{9,8},{10,11... | collective-permute-start | bytes 1179656 | tf_op jit(solution)/shard_map/ppermute | solution.py:549
  232.3 27.2 %collective-permute-start.18 = (bf16[4,2,96,384]{3,2,1,0:T(8,128)(2,1)}, bf16[4,2,96,384]{3,2,1,0:T(8,128)(2,1)}, u32[]{:S(2)}, u32[]{:S(2)}) collective-permute-start(bf16[4,2,96,384]{3,2,1,0:T(8,128)(2,1)} %dynamic-slice_bitcast_fusion.2), channel_id=1, source_target_pairs={{0,16},{8,24},{16,0},{24,8},{1,17},{9,25},{17,1},{25,9},{2,18},{10... | collective-permute-start | bytes 1769480 | tf_op jit(solution)/shard_map/ppermute | solution.py:549
  234.8 27.2 %collective-permute-start.15 = (bf16[4,2,96,384]{3,2,1,0:T(8,128)(2,1)}, bf16[4,2,96,384]{3,2,1,0:T(8,128)(2,1)}, u32[]{:S(2)}, u32[]{:S(2)}) collective-permute-start(bf16[4,2,96,384]{3,2,1,0:T(8,128)(2,1)} %dynamic-slice_bitcast_fusion.3), channel_id=1, source_target_pairs={{0,1},{1,0},{2,3},{3,2},{4,5},{5,4},{6,7},{7,6},{8,9},{9,8},{10,11... | collective-permute-start | bytes 1769480 | tf_op jit(solution)/shard_map/ppermute | solution.py:549
  253.5 11.7 %collective-permute-start.20 = (bf16[3,384,384]{2,1,0:T(8,128)(2,1)}, bf16[3,384,384]{2,1,0:T(8,128)(2,1)S(1)}, u32[]{:S(2)}, u32[]{:S(2)}) collective-permute-start(bf16[3,384,384]{2,1,0:T(8,128)(2,1)} %get-tuple-element.121), channel_id=1, source_target_pairs={{0,8},{8,0},{16,24},{24,16},{1,9},{9,1},{17,25},{25,17},{2,10},{10... | collective-permute-start | bytes 2654216 | tf_op jit(solution)/shard_map/ppermute | solution.py:549
  254.8 20.1 %collective-permute-start.26 = (bf16[240,384]{1,0:T(8,128)(2,1)}, bf16[240,384]{1,0:T(8,128)(2,1)S(1)}, u32[]{:S(2)}, u32[]{:S(2)}) collective-permute-start(bf16[240,384]{1,0:T(8,128)(2,1)} %get-tuple-element.206), channel_id=1, source_target_pairs={{0,2},{1,3},{2,4},{3,5},{4,6},{5,7},{6,0},{7,1},{8,10},{9,11},{10,... | collective-permute-start | bytes 552968 | tf_op jit(solution)/shard_map/ppermute | solution.py:619
  259.5 15.4 %collective-permute-start.27 = (bf16[240,384]{1,0:T(8,128)(2,1)}, bf16[240,384]{1,0:T(8,128)(2,1)S(1)}, u32[]{:S(2)}, u32[]{:S(2)}) collective-permute-start(bf16[240,384]{1,0:T(8,128)(2,1)} %get-tuple-element.205), channel_id=1, source_target_pairs={{0,4},{1,5},{2,6},{3,7},{4,0},{5,1},{6,2},{7,3},{8,12},{9,13},{10,... | collective-permute-start | bytes 552968 | tf_op jit(solution)/shard_map/ppermute | solution.py:619
  259.5 15.4 %collective-permute-start.28 = (bf16[240,384]{1,0:T(8,128)(2,1)}, bf16[240,384]{1,0:T(8,128)(2,1)S(1)}, u32[]{:S(2)}, u32[]{:S(2)}) collective-permute-start(bf16[240,384]{1,0:T(8,128)(2,1)} %get-tuple-element.204), channel_id=1, source_target_pairs={{0,6},{1,7},{2,0},{3,1},{4,2},{5,3},{6,4},{7,5},{8,14},{9,15},{10,... | collective-permute-start | bytes 552968 | tf_op jit(solution)/shard_map/ppermute | solution.py:619
  263.3 8.8 %collective-permute-start.19 = (bf16[4,96,384]{2,1,0:T(8,128)(2,1)S(1)}, bf16[4,96,384]{2,1,0:T(8,128)(2,1)S(1)}, u32[]{:S(2)}, u32[]{:S(2)}) collective-permute-start(bf16[4,96,384]{2,1,0:T(8,128)(2,1)S(1)} %get-tuple-element.217), channel_id=1, source_target_pairs={{0,16},{8,24},{16,0},{24,8},{1,17},{9,25},{17,1},{25,9},{2,18},{10... | collective-permute-start | bytes 884744 | tf_op jit(solution)/shard_map/ppermute | solution.py:549
  265.2 8.8 %collective-permute-start.21 = (bf16[4,96,384]{2,1,0:T(8,128)(2,1)S(1)}, bf16[4,96,384]{2,1,0:T(8,128)(2,1)S(1)}, u32[]{:S(2)}, u32[]{:S(2)}) collective-permute-start(bf16[4,96,384]{2,1,0:T(8,128)(2,1)S(1)} %get-tuple-element.219), channel_id=1, source_target_pairs={{0,1},{1,0},{2,3},{3,2},{4,5},{5,4},{6,7},{7,6},{8,9},{9,8},{10,11... | collective-permute-start | bytes 884744 | tf_op jit(solution)/shard_map/ppermute | solution.py:549
  275.9 7.1 %collective-permute-start.29 = (bf16[240,384]{1,0:T(8,128)(2,1)S(1)}, bf16[240,384]{1,0:T(8,128)(2,1)S(1)}, u32[]{:S(2)}, u32[]{:S(2)}) collective-permute-start(bf16[240,384]{1,0:T(8,128)(2,1)S(1)} %fusion.17), channel_id=1, source_target_pairs={{0,8},{8,0},{16,24},{24,16},{1,9},{9,1},{17,25},{25,17},{2,10},{10... | collective-permute-start | bytes 552968 | tf_op jit(solution)/shard_map/ppermute | solution.py:549
  276.1 11.6 %collective-permute-start.23 = (bf16[4,2,64,384]{3,2,1,0:T(8,128)(2,1)S(1)}, bf16[4,2,64,384]{3,2,1,0:T(8,128)(2,1)S(1)}, u32[]{:S(2)}, u32[]{:S(2)}) collective-permute-start(bf16[4,2,64,384]{3,2,1,0:T(8,128)(2,1)S(1)} %pad_maximum_fusion.14), channel_id=1, source_target_pairs={{0,1},{1,0},{2,3},{3,2},{4,5},{5,4},{6,7},{7,6},{8,9},{9,8},{10,11... | collective-permute-start | bytes 1179656 | tf_op jit(solution)/shard_map/ppermute | solution.py:549
  277.9 45.8 %collective-permute-start.22 = (bf16[192,384]{1,0:T(8,128)(2,1)}, bf16[192,384]{1,0:T(8,128)(2,1)}, u32[]{:S(2)}, u32[]{:S(2)}) collective-permute-start(bf16[192,384]{1,0:T(8,128)(2,1)} %get-tuple-element.215), channel_id=1, source_target_pairs={{0,2},{1,3},{2,4},{3,5},{4,6},{5,7},{6,0},{7,1},{8,10},{9,11},{10,... | collective-permute-start | bytes 442376 | tf_op jit(solution)/shard_map/ppermute | solution.py:619
  279.8 44.0 %collective-permute-start.31 = (bf16[192,384]{1,0:T(8,128)(2,1)}, bf16[192,384]{1,0:T(8,128)(2,1)}, u32[]{:S(2)}, u32[]{:S(2)}) collective-permute-start(bf16[192,384]{1,0:T(8,128)(2,1)} %get-tuple-element.214), channel_id=1, source_target_pairs={{0,4},{1,5},{2,6},{3,7},{4,0},{5,1},{6,2},{7,3},{8,12},{9,13},{10,... | collective-permute-start | bytes 442376 | tf_op jit(solution)/shard_map/ppermute | solution.py:619
  283.0 43.2 %collective-permute-start.32 = (bf16[192,384]{1,0:T(8,128)(2,1)}, bf16[192,384]{1,0:T(8,128)(2,1)}, u32[]{:S(2)}, u32[]{:S(2)}) collective-permute-start(bf16[192,384]{1,0:T(8,128)(2,1)} %get-tuple-element.213), channel_id=1, source_target_pairs={{0,6},{1,7},{2,0},{3,1},{4,2},{5,3},{6,4},{7,5},{8,14},{9,15},{10,... | collective-permute-start | bytes 442376 | tf_op jit(solution)/shard_map/ppermute | solution.py:619
  283.0 14.1 %collective-permute-start.24 = (bf16[4,2,80,384]{3,2,1,0:T(8,128)(2,1)S(1)}, bf16[4,2,80,384]{3,2,1,0:T(8,128)(2,1)S(1)}, u32[]{:S(2)}, u32[]{:S(2)}) collective-permute-start(bf16[4,2,80,384]{3,2,1,0:T(8,128)(2,1)S(1)} %pad_maximum_fusion.12), channel_id=1, source_target_pairs={{0,16},{8,24},{16,0},{24,8},{1,17},{9,25},{17,1},{25,9},{2,18},{10... | collective-permute-start | bytes 1474568 | tf_op jit(solution)/shard_map/ppermute | solution.py:549
  288.5 15.7 %collective-permute-start.25 = (bf16[4,64,384]{2,1,0:T(8,128)(2,1)}, bf16[4,64,384]{2,1,0:T(8,128)(2,1)}, u32[]{:S(2)}, u32[]{:S(2)}) collective-permute-start(bf16[4,64,384]{2,1,0:T(8,128)(2,1)} %get-tuple-element.231), channel_id=1, source_target_pairs={{0,16},{8,24},{16,0},{24,8},{1,17},{9,25},{17,1},{25,9},{2,18},{10... | collective-permute-start | bytes 589832 | tf_op jit(solution)/shard_map/ppermute | solution.py:549
  298.1 8.1 %collective-permute-start.30 = (bf16[4,80,384]{2,1,0:T(8,128)(2,1)}, bf16[4,80,384]{2,1,0:T(8,128)(2,1)S(1)}, u32[]{:S(2)}, u32[]{:S(2)}) collective-permute-start(bf16[4,80,384]{2,1,0:T(8,128)(2,1)} %get-tuple-element.222), channel_id=1, source_target_pairs={{0,1},{1,0},{2,3},{3,2},{4,5},{5,4},{6,7},{7,6},{8,9},{9,8},{10,11... | collective-permute-start | bytes 737288 | tf_op jit(solution)/shard_map/ppermute | solution.py:549
  304.1 27.1 %collective-permute-start.44 = (f32[208,384]{1,0:T(8,128)}, f32[208,384]{1,0:T(8,128)}, u32[]{:S(2)}, u32[]{:S(2)}) collective-permute-start(f32[208,384]{1,0:T(8,128)} %dynamic-slice_bitcast_fusion.8), channel_id=1, source_target_pairs={{0,1},{1,0},{2,3},{3,2},{4,5},{5,4},{6,7},{7,6},{8,9},{9,8},{10,11... | collective-permute-start | bytes 958472 | tf_op jit(solution)/shard_map/ppermute | solution.py:549
  308.7 18.6 %collective-permute-start.33 = (bf16[144,384]{1,0:T(8,128)(2,1)}, bf16[144,384]{1,0:T(8,128)(2,1)S(1)}, u32[]{:S(2)}, u32[]{:S(2)}) collective-permute-start(bf16[144,384]{1,0:T(8,128)(2,1)} %get-tuple-element.230), channel_id=1, source_target_pairs={{0,2},{1,3},{2,4},{3,5},{4,6},{5,7},{6,0},{7,1},{8,10},{9,11},{10,... | collective-permute-start | bytes 331784 | tf_op jit(solution)/shard_map/ppermute | solution.py:619
  323.7 6.4 %collective-permute-start.34 = (bf16[144,384]{1,0:T(8,128)(2,1)S(1)}, bf16[144,384]{1,0:T(8,128)(2,1)S(1)}, u32[]{:S(2)}, u32[]{:S(2)}) collective-permute-start(bf16[144,384]{1,0:T(8,128)(2,1)S(1)} %get-tuple-element.228), channel_id=1, source_target_pairs={{0,4},{1,5},{2,6},{3,7},{4,0},{5,1},{6,2},{7,3},{8,12},{9,13},{10,... | collective-permute-start | bytes 331784 | tf_op jit(solution)/shard_map/ppermute | solution.py:619
  323.8 6.3 %collective-permute-start.35 = (bf16[144,384]{1,0:T(8,128)(2,1)S(1)}, bf16[144,384]{1,0:T(8,128)(2,1)S(1)}, u32[]{:S(2)}, u32[]{:S(2)}) collective-permute-start(bf16[144,384]{1,0:T(8,128)(2,1)S(1)} %get-tuple-element.229), channel_id=1, source_target_pairs={{0,6},{1,7},{2,0},{3,1},{4,2},{5,3},{6,4},{7,5},{8,14},{9,15},{10,... | collective-permute-start | bytes 331784 | tf_op jit(solution)/shard_map/ppermute | solution.py:619
  338.7 9.1 %collective-permute-start.37 = (f32[208,384]{1,0:T(8,128)S(1)}, f32[208,384]{1,0:T(8,128)S(1)}, u32[]{:S(2)}, u32[]{:S(2)}) collective-permute-start(f32[208,384]{1,0:T(8,128)S(1)} %dynamic-slice_bitcast_fusion.9), channel_id=1, source_target_pairs={{0,1},{1,0},{2,3},{3,2},{4,5},{5,4},{6,7},{7,6},{8,9},{9,8},{10,11... | collective-permute-start | bytes 958472 | tf_op jit(solution)/shard_map/ppermute | solution.py:549
  339.9 10.1 %collective-permute-start.45 = (f32[104,384]{1,0:T(8,128)S(1)}, f32[104,384]{1,0:T(8,128)S(1)}, u32[]{:S(2)}, u32[]{:S(2)}) collective-permute-start(f32[104,384]{1,0:T(8,128)S(1)} %dynamic-slice_bitcast_fusion.29), channel_id=1, source_target_pairs={{0,16},{8,24},{16,0},{24,8},{1,17},{9,25},{17,1},{25,9},{2,18},{10... | collective-permute-start | bytes 479240 | tf_op jit(solution)/shard_map/ppermute | solution.py:549
  347.9 7.1 %collective-permute-start.38 = (f32[104,384]{1,0:T(8,128)S(1)}, f32[104,384]{1,0:T(8,128)S(1)}, u32[]{:S(2)}, u32[]{:S(2)}) collective-permute-start(f32[104,384]{1,0:T(8,128)S(1)} %dynamic-slice_bitcast_fusion.30), channel_id=1, source_target_pairs={{0,16},{8,24},{16,0},{24,8},{1,17},{9,25},{17,1},{25,9},{2,18},{10... | collective-permute-start | bytes 479240 | tf_op jit(solution)/shard_map/ppermute | solution.py:549
  348.8 23.8 %collective-permute-start.53 = (bf16[240,768]{1,0:T(8,128)(2,1)S(1)}, bf16[240,768]{1,0:T(8,128)(2,1)}, u32[]{:S(2)}, u32[]{:S(2)}) collective-permute-start(bf16[240,768]{1,0:T(8,128)(2,1)S(1)} %bitcast.275), channel_id=1, source_target_pairs={{0,16},{8,24},{16,0},{24,8},{1,17},{9,25},{17,1},{25,9},{2,18},{10... | collective-permute-start | bytes 1105928 | tf_op jit(solution)/shard_map/ppermute | solution.py:549
  350.0 8.5 %collective-permute-start.46 = (f32[104,384]{1,0:T(8,128)S(1)}, f32[104,384]{1,0:T(8,128)S(1)}, u32[]{:S(2)}, u32[]{:S(2)}) collective-permute-start(f32[104,384]{1,0:T(8,128)S(1)} %bitcast_add_fusion.2), channel_id=1, source_target_pairs={{0,2},{1,3},{2,0},{3,1},{4,6},{5,7},{6,4},{7,5},{8,10},{9,11},{10,... | collective-permute-start | bytes 479240 | tf_op jit(solution)/shard_map/ppermute | solution.py:549
  355.0 6.5 %collective-permute-start.39 = (f32[104,384]{1,0:T(8,128)S(1)}, f32[104,384]{1,0:T(8,128)S(1)}, u32[]{:S(2)}, u32[]{:S(2)}) collective-permute-start(f32[104,384]{1,0:T(8,128)S(1)} %bitcast_add_fusion.3), channel_id=1, source_target_pairs={{0,2},{1,3},{2,0},{3,1},{4,6},{5,7},{6,4},{7,5},{8,10},{9,11},{10,... | collective-permute-start | bytes 479240 | tf_op jit(solution)/shard_map/ppermute | solution.py:549
  358.5 12.3 %collective-permute-start.47 = (f32[104,384]{1,0:T(8,128)S(1)}, f32[104,384]{1,0:T(8,128)}, u32[]{:S(2)}, u32[]{:S(2)}) collective-permute-start(f32[104,384]{1,0:T(8,128)S(1)} %add.435), channel_id=1, source_target_pairs={{0,4},{1,5},{2,6},{3,7},{4,0},{5,1},{6,2},{7,3},{8,12},{9,13},{10,... | collective-permute-start | bytes 479240 | tf_op jit(solution)/shard_map/ppermute | solution.py:549
  359.4 15.7 %collective-permute-start.52 = (bf16[144,768]{1,0:T(8,128)(2,1)S(1)}, bf16[144,768]{1,0:T(8,128)(2,1)S(1)}, u32[]{:S(2)}, u32[]{:S(2)}) collective-permute-start(bf16[144,768]{1,0:T(8,128)(2,1)S(1)} %slice.122), channel_id=1, source_target_pairs={{0,16},{8,24},{16,0},{24,8},{1,17},{9,25},{17,1},{25,9},{2,18},{10... | collective-permute-start | bytes 663560 | tf_op jit(solution)/shard_map/ppermute | solution.py:549
  360.3 15.9 %collective-permute-start.51 = (bf16[192,768]{1,0:T(8,128)(2,1)S(1)}, bf16[192,768]{1,0:T(8,128)(2,1)S(1)}, u32[]{:S(2)}, u32[]{:S(2)}) collective-permute-start(bf16[192,768]{1,0:T(8,128)(2,1)S(1)} %slice.121), channel_id=1, source_target_pairs={{0,16},{8,24},{16,0},{24,8},{1,17},{9,25},{17,1},{25,9},{2,18},{10... | collective-permute-start | bytes 884744 | tf_op jit(solution)/shard_map/ppermute | solution.py:549
  361.5 14.9 %collective-permute-start.40 = (f32[104,384]{1,0:T(8,128)S(1)}, f32[104,384]{1,0:T(8,128)S(1)}, u32[]{:S(2)}, u32[]{:S(2)}) collective-permute-start(f32[104,384]{1,0:T(8,128)S(1)} %add.431), channel_id=1, source_target_pairs={{0,4},{1,5},{2,6},{3,7},{4,0},{5,1},{6,2},{7,3},{8,12},{9,13},{10,... | collective-permute-start | bytes 479240 | tf_op jit(solution)/shard_map/ppermute | solution.py:549
  377.9 7.7 %collective-permute-start.49 = (f32[208,384]{1,0:T(8,128)S(1)}, f32[208,384]{1,0:T(8,128)S(1)}, u32[]{:S(2)}, u32[]{:S(2)}) collective-permute-start(f32[208,384]{1,0:T(8,128)S(1)} %bitcast.285), channel_id=1, source_target_pairs={{0,1},{1,0},{2,3},{3,2},{4,5},{5,4},{6,7},{7,6},{8,9},{9,8},{10,11... | collective-permute-start | bytes 958472 | tf_op jit(solution)/shard_map/ppermute | solution.py:549
  381.9 7.1 %collective-permute-start.42 = (f32[208,384]{1,0:T(8,128)S(1)}, f32[208,384]{1,0:T(8,128)S(1)}, u32[]{:S(2)}, u32[]{:S(2)}) collective-permute-start(f32[208,384]{1,0:T(8,128)S(1)} %bitcast.286), channel_id=1, source_target_pairs={{0,1},{1,0},{2,3},{3,2},{4,5},{5,4},{6,7},{7,6},{8,9},{9,8},{10,11... | collective-permute-start | bytes 958472 | tf_op jit(solution)/shard_map/ppermute | solution.py:549
  385.7 6.5 %collective-permute-start.50 = (f32[416,384]{1,0:T(8,128)S(1)}, f32[416,384]{1,0:T(8,128)S(1)}, u32[]{:S(2)}, u32[]{:S(2)}) collective-permute-start(f32[416,384]{1,0:T(8,128)S(1)} %bitcast.278), channel_id=1, source_target_pairs={{0,8},{8,0},{16,24},{24,16},{1,9},{9,1},{17,25},{25,17},{2,10},{10... | collective-permute-start | bytes 1916936 | tf_op jit(solution)/shard_map/ppermute | solution.py:549
  432.5 14.4 %collective-permute-start.54 = (bf16[336,768]{1,0:T(8,128)(2,1)}, bf16[336,768]{1,0:T(8,128)(2,1)S(1)}, u32[]{:S(2)}, u32[]{:S(2)}) collective-permute-start(bf16[336,768]{1,0:T(8,128)(2,1)} %newton.1), channel_id=1, source_target_pairs={{0,16},{8,24},{16,0},{24,8},{1,17},{9,25},{17,1},{25,9},{2,18},{10... | collective-permute-start | bytes 1548296 | tf_op jit(solution)/shard_map/ppermute | solution.py:549
  (61 other events, 305.7 us)
Sparse Core Ops, SparseCore 0:
  11.5 88.3 all-gather.1
